TPU v7x, 32 devices: a whole 2x2x4 slice. The times are simulated.
32 devices in a mesh: seg: 8 (over z, x), sample: 4 (over y, core).
Axes of the slice: x: 2, y: 2, z: 4, core: 2. Of those that a mesh axis runs over, the one named last changes fastest.
Arguments:
- queries: bfloat16 [4, 4096, 512], P('sample', 'seg'), may hold values from -6 to 6
- key_rows: bfloat16 [4, 4096, 512], P('sample', 'seg'), may hold values from -6 to 6
- value_rows: bfloat16 [4, 4096, 512], P('sample', 'seg'), may hold values from -6 to 6
- w_out: bfloat16 [512, 512], replicated, may hold values from -0.25 to 0.25
- grad_out: bfloat16 [4, 4096, 512], P('sample', 'seg'), may hold values from -6 to 6
- neighbours: int32 [4, 8, 3], P('sample', 'seg'), may hold values from 0 to 7, as said below
Outputs:
- attended: bfloat16 [4, 4096, 512], P('sample', 'seg')
- grad_queries: bfloat16 [4, 4096, 512], P('sample', 'seg')
- grad_keys: bfloat16 [4, 4096, 512], P('sample', 'seg')
- grad_values: bfloat16 [4, 4096, 512], P('sample', 'seg')
- grad_w_out: float32 [512, 512], replicated
Inputs may be any that keep to these rules, and one draw needn't show every extreme that they name: `neighbours`: entries are patch indices of the same sample within 3 of the patch along the curve. Entries that differ from the patch itself are distinct and come first; entries equal to the patch itself are unused and fill the rest of the list. A patch may have 1 to 3 used entries; in every sample some patch uses all 3.
All inputs are finite; a program needn't handle non-finite values.
Results may differ from a plain program's by a relative error of at most 0.02.
Values may be sent and summed in bfloat16 or wider, within the bound.
No kernel may reach another device: no remote copies, remote signals or barrier semaphores. Data moves between devices by JAX's collectives and lax.ppermute only.
A program may use at most 128 MiB of HBM per device.

v0:
```python
import math

import jax
import jax.numpy as jnp
from jax import lax
from jax.sharding import PartitionSpec as P

HEADS = 8
NBR = 3
REACH = 3


def from_behind(value, axis, steps):
    count = lax.axis_size(axis)
    initial, last = (max(0, -steps), min(count, count - steps))
    return lax.ppermute(value, axis, [(source, source + steps) for source in range(initial, last)])


def heads_of(matrix):
    return matrix.reshape(matrix.shape[0], HEADS, -1).transpose(1, 0, 2)


def rows_of(per_head):
    return per_head.transpose(1, 0, 2).reshape(per_head.shape[1], -1)


def attend(q_rows, key_block, value_block, key_mask, score_scale):

    def per_head(operands):
        q_head, k_head, v_head = operands
        scores = jnp.dot(q_head, k_head.T, preferred_element_type=jnp.float32) * score_scale
        scores = jnp.where(key_mask[None, :], scores, -jnp.inf)
        row_top = jnp.max(scores, axis=1, keepdims=True)
        log_total = row_top + jnp.log(jnp.sum(jnp.exp(scores - row_top), axis=1, keepdims=True))
        softmax_h = jnp.exp(scores - log_total).astype(jnp.bfloat16)
        return (jnp.dot(softmax_h, v_head, preferred_element_type=jnp.float32), log_total[:, 0])

    mixture, log_total = lax.map(
        per_head, (heads_of(q_rows), heads_of(key_block), heads_of(value_block))
    )
    return (rows_of(mixture).astype(jnp.bfloat16), log_total)


def backprop(q_rows, key_block, value_block, d_attn, attn_rows, log_total, key_mask, score_scale):
    row_delta = jnp.sum(
        heads_of(d_attn).astype(jnp.float32) * heads_of(attn_rows).astype(jnp.float32), axis=-1
    )

    def per_head(operands):
        q_head, k_head, v_head, da_head, total_head, delta_head = operands
        scores = jnp.dot(q_head, k_head.T, preferred_element_type=jnp.float32) * score_scale
        scores = jnp.where(key_mask[None, :], scores, -jnp.inf)
        softmax_w = jnp.exp(scores - total_head[:, None])
        softmax_h = softmax_w.astype(jnp.bfloat16)
        d_prob = jnp.dot(da_head, v_head.T, preferred_element_type=jnp.float32)
        d_score = (softmax_w * (d_prob - delta_head[:, None]) * score_scale).astype(jnp.bfloat16)
        grad_q = jnp.dot(d_score, k_head, preferred_element_type=jnp.float32)
        grad_k = jnp.dot(d_score.T, q_head, preferred_element_type=jnp.float32)
        grad_v = jnp.dot(softmax_h.T, da_head, preferred_element_type=jnp.float32)
        return (grad_q, grad_k, grad_v)

    grad_q, grad_k, grad_v = lax.map(
        per_head,
        (
            heads_of(q_rows),
            heads_of(key_block),
            heads_of(value_block),
            heads_of(d_attn),
            log_total,
            row_delta,
        ),
    )
    return (rows_of(grad_q).astype(jnp.bfloat16), rows_of(grad_k), rows_of(grad_v), row_delta)


def body(queries, key_rows, value_rows, w_out, grad_out, neighbours):
    samples_here, patch_len, model_width = queries.shape
    score_scale = 1.0 / math.sqrt(model_width // HEADS)
    patch_index = lax.axis_index("seg")
    key_slots = []
    value_slots = []
    for offset in range(-REACH, REACH + 1):
        if offset == 0:
            key_slots.append(key_rows)
            value_slots.append(value_rows)
        else:
            fetched = from_behind((key_rows, value_rows), "seg", -offset)
            key_slots.append(fetched[0])
            value_slots.append(fetched[1])
    key_stack = jnp.stack(key_slots, axis=1)
    value_stack = jnp.stack(value_slots, axis=1)

    def one_sample(operands):
        q_sample, k_stack, v_stack, g_sample, n_sample = operands
        listed = n_sample[0]
        in_use = listed != patch_index
        block_ids = jnp.concatenate(
            [jnp.array([REACH], jnp.int32), jnp.where(in_use, listed - patch_index + REACH, REACH)]
        )
        block_live = jnp.concatenate([jnp.array([True]), in_use])
        key_mask = jnp.repeat(block_live, patch_len)
        key_block = k_stack[block_ids].reshape(-1, model_width)
        value_block = v_stack[block_ids].reshape(-1, model_width)
        attn_rows, log_total = attend(q_sample, key_block, value_block, key_mask, score_scale)
        projected = jnp.dot(attn_rows, w_out, preferred_element_type=jnp.float32).astype(
            jnp.bfloat16
        )
        d_attn = jnp.dot(g_sample, w_out.T, preferred_element_type=jnp.float32).astype(jnp.bfloat16)
        w_term = lax.dot_general(
            attn_rows, g_sample, (((0,), (0,)), ((), ())), preferred_element_type=jnp.float32
        )
        grad_q, grad_k, grad_v, row_delta = backprop(
            q_sample, key_block, value_block, d_attn, attn_rows, log_total, key_mask, score_scale
        )
        slot_shape = (2 * REACH + 1, patch_len, model_width)
        part_k = (
            jnp.zeros(slot_shape, jnp.float32)
            .at[block_ids]
            .add(grad_k.reshape(NBR + 1, patch_len, model_width))
        )
        part_v = (
            jnp.zeros(slot_shape, jnp.float32)
            .at[block_ids]
            .add(grad_v.reshape(NBR + 1, patch_len, model_width))
        )
        return (projected, grad_q, part_k, part_v, w_term, d_attn, log_total, row_delta)

    results = lax.map(one_sample, (queries, key_stack, value_stack, grad_out, neighbours))
    attended, grad_queries, part_k, part_v, w_terms, d_attn_all, total_all, delta_all = results
    grad_scale = 1.0 / math.sqrt(
        samples_here * lax.axis_size("sample") * patch_len * lax.axis_size("seg")
    )
    grad_w_out = lax.psum(jnp.sum(w_terms, axis=0), ("seg", "sample")) * grad_scale
    half_k = part_k.astype(jnp.bfloat16)
    half_v = part_v.astype(jnp.bfloat16)
    total_k = lax.optimization_barrier(half_k[:, REACH]).astype(jnp.float32)
    total_v = lax.optimization_barrier(half_v[:, REACH]).astype(jnp.float32)
    for offset in range(-REACH, REACH + 1):
        if offset != 0:
            returned = from_behind(
                (half_k[:, offset + REACH], half_v[:, offset + REACH]), "seg", offset
            )
            total_k = total_k + returned[0].astype(jnp.float32)
            total_v = total_v + returned[1].astype(jnp.float32)
    return (
        attended,
        grad_queries,
        total_k.astype(jnp.bfloat16),
        total_v.astype(jnp.bfloat16),
        grad_w_out,
    )


def solution(mesh):
    in_specs = (
        P("sample", "seg", None),
        P("sample", "seg", None),
        P("sample", "seg", None),
        P(),
        P("sample", "seg", None),
        P("sample", "seg", None),
    )
    out_specs = (
        P("sample", "seg", None),
        P("sample", "seg", None),
        P("sample", "seg", None),
        P("sample", "seg", None),
        P(),
    )
    return jax.shard_map(body, mesh=mesh, in_specs=in_specs, out_specs=out_specs, check_vma=False)
```

profile of v0, /device:TPU:0, one launch (start us, length us, event | category | flops | bytes accessed | tf_op | source)
XLA Modules:
  0.0 536.1 jit_solution(7319178462900078899)
XLA Ops:
  7.2 6.8 %collective-permute-start = (bf16[1,512,512]{2,1,0:T(8,128)(2,1)}, bf16[1,512,512]{2,1,0:T(8,128)(2,1)}, u32[]{:S(2)}, u32[]{:S(2)}) collective-permute-start(bf16[1,512,512]{2,1,0:T(8,128)(2,1)} %param.13), channel_id=1, source_target_pairs={{0,12},{4,16},{8,20},{12,24},{16,28},{1,13},{5,17},{9,21},{13,25},... | collective-permute-start | bytes 1572872 | tf_op jit(solution)/shard_map/ppermute | solution.py:16
  14.1 4.3 collective-permute-start.1
  18.3 3.5 collective-permute-start.2
  28.4 12.0 %collective-permute-start.6 = (bf16[1,512,512]{2,1,0:T(8,128)(2,1)}, bf16[1,512,512]{2,1,0:T(8,128)(2,1)S(1)}, u32[]{:S(2)}, u32[]{:S(2)}) collective-permute-start(bf16[1,512,512]{2,1,0:T(8,128)(2,1)} %param.14), channel_id=1, source_target_pairs={{0,12},{4,16},{8,20},{12,24},{16,28},{1,13},{5,17},{9,21},{13,25},... | collective-permute-start | bytes 1572872 | tf_op jit(solution)/shard_map/ppermute | solution.py:16
  44.5 11.7 %collective-permute-start.8 = (bf16[1,512,512]{2,1,0:T(8,128)(2,1)S(1)}, bf16[1,512,512]{2,1,0:T(8,128)(2,1)S(1)}, u32[]{:S(2)}, u32[]{:S(2)}) collective-permute-start(bf16[1,512,512]{2,1,0:T(8,128)(2,1)S(1)} %copy-done.4), channel_id=1, source_target_pairs={{0,4},{4,8},{8,12},{12,16},{16,20},{20,24},{24,28},{1,5},{5,9},{9,... | collective-permute-start | bytes 1572872 | tf_op jit(solution)/shard_map/ppermute | solution.py:16
  58.7 4.6 collective-permute-done.7
  64.6 2.1 collective-permute-done.8
  69.6 27.9 %collective-permute-done.5 = bf16[1,512,512]{2,1,0:T(8,128)(2,1)S(1)} collective-permute-done((bf16[1,512,512]{2,1,0:T(8,128)(2,1)S(1)}, bf16[1,512,512]{2,1,0:T(8,128)(2,1)S(1)}, u32[]{:S(2)}, u32[]{:S(2)}) %collective-permute-start.5) | collective-permute-done | bytes 524320 | tf_op jit(solution)/shard_map/ppermute | solution.py:16
  99.4 2.7 gather_fusion
  102.1 3.1 copy.30
  105.2 3.3 reshape.181
  108.5 3.2 copy.33
  115.4 15.7 %collective-permute-done.11 = bf16[1,512,512]{2,1,0:T(8,128)(2,1)} collective-permute-done((bf16[1,512,512]{2,1,0:T(8,128)(2,1)S(1)}, bf16[1,512,512]{2,1,0:T(8,128)(2,1)}, u32[]{:S(2)}, u32[]{:S(2)}) %collective-permute-start.11) | collective-permute-done | bytes 524320 | tf_op jit(solution)/shard_map/ppermute | solution.py:16
  133.1 2.7 gather_fusion.1
  135.8 3.1 copy.31
  138.9 3.3 reshape.182
  142.1 3.2 copy.34
  145.4 38.0 %while.45 = (s32[]{:T(128)}, bf16[8,512,64]{1,2,0:T(8,128)(2,1)S(1)}, f32[8,512]{1,0:T(8,128)S(1)}, bf16[8,512,64]{2,1,0:T(8,128)(2,1)}, bf16[8,2048,64]{2,1,0:T...) while((s32[]{:T(128)}, ...), condition=%wide.region_3.4_spmd.clone, body=%wide.region_0.3_spmd.clone.sunk | while | flops 275774976 | bytes 13922405 | solution.py:38
  183.9 76.3 %while.46 = (s32[]{:T(128)}, bf16[8,512,64]{1,2,0:T(8,128)(2,1)S(1)}, f32[8,2048,64]{1,2,0:T(8,128)}, f32[8,2048,64]{1,2,0:T(8,128)}, bf16[8,512,64]{2,1,0:T(8,1...) while((s32[]{:T(128)}, ...), condition=%wide.region_6.7_spmd.clone, body=%wide.region_5.6_spmd.clone.sunk | while | flops 679477248 | bytes 22045820 | solution.py:62
  188.1 2.2 fusion.82
  197.7 2.3 fusion.82
  207.2 2.3 fusion.82
  216.8 2.2 fusion.82
  226.3 2.3 fusion.82
  235.8 2.3 fusion.82
  245.4 2.2 fusion.82
  254.9 2.2 fusion.82
  260.2 6.0 %reshape.214 = f32[4,512,512]{1,0,2:T(4,128)} reshape(f32[2048,8,64]{0,2,1:T(8,128)} %bitcast.43) | data formatting | bytes 8388608 | tf_op jit(solution)/shard_map/while/body/eval_jaxpr/reshape;while/body/eval_jaxpr/reshape | solution.py:124
  266.3 5.3 copy.40
  271.5 3.9 broadcast.113.clone.1
  275.4 9.0 %scatter_fusion.1 = f32[7,512,512]{2,1,0:T(8,128)} fusion(f32[7,512,512]{2,1,0:T(8,128)} %broadcast.113.clone.1, s32[4]{0:T(128)S(1)} %fusion.43, f32[4,512,512]{2,1,0:T(8,128)} %copy.40), kind=kCustom, calls=%fused_computation.3 | custom fusion | flops 1048576 | bytes 12582928 | tf_op jit(solution)/shard_map/while/body/eval_jaxpr/scatter-add | solution.py:124
  284.4 3.6 convert_bitcast_fusion
  293.6 21.0 %collective-permute-start.21 = (bf16[1,512,512]{2,1,0:T(8,128)(2,1)}, bf16[1,512,512]{2,1,0:T(8,128)(2,1)}, u32[]{:S(2)}, u32[]{:S(2)}) collective-permute-start(bf16[1,512,512]{2,1,0:T(8,128)(2,1)} %get-tuple-element.283), channel_id=1, source_target_pairs={{0,4},{4,8},{8,12},{12,16},{16,20},{20,24},{24,28},{1,5},{5,9},{9,... | collective-permute-start | bytes 1572872 | tf_op jit(solution)/shard_map/ppermute | solution.py:16
  314.6 4.5 collective-permute-start.22
  319.2 6.0 %reshape.206 = f32[4,512,512]{1,0,2:T(4,128)} reshape(f32[2048,8,64]{0,2,1:T(8,128)} %bitcast.220) | data formatting | bytes 8388608 | tf_op jit(solution)/shard_map/while/body/eval_jaxpr/reshape;while/body/eval_jaxpr/reshape | solution.py:119
  325.2 5.2 copy.39
  330.4 3.9 broadcast.113.clone
  334.3 9.0 %scatter_fusion = f32[7,512,512]{2,1,0:T(8,128)} fusion(f32[7,512,512]{2,1,0:T(8,128)} %broadcast.113.clone, s32[4]{0:T(128)S(1)} %fusion.43, f32[4,512,512]{2,1,0:T(8,128)} %copy.39), kind=kCustom, calls=%fused_computation.2 | custom fusion | flops 1048576 | bytes 12582928 | tf_op jit(solution)/shard_map/while/body/eval_jaxpr/scatter-add | solution.py:119
  343.3 3.6 convert_bitcast_fusion.1
  348.4 7.3 %collective-permute-start.23 = (bf16[1,512,512]{2,1,0:T(8,128)(2,1)}, bf16[1,512,512]{2,1,0:T(8,128)(2,1)}, u32[]{:S(2)}, u32[]{:S(2)}) collective-permute-start(bf16[1,512,512]{2,1,0:T(8,128)(2,1)} %get-tuple-element.281), channel_id=1, source_target_pairs={{0,12},{4,16},{8,20},{12,24},{16,28},{1,13},{5,17},{9,21},{13,25},... | collective-permute-start | bytes 1572872 | tf_op jit(solution)/shard_map/ppermute | solution.py:16
  359.4 2.3 fusion.39
  364.3 5.8 %collective-permute-start.15 = (bf16[1,512,512]{2,1,0:T(8,128)(2,1)}, bf16[1,512,512]{2,1,0:T(8,128)(2,1)}, u32[]{:S(2)}, u32[]{:S(2)}) collective-permute-start(bf16[1,512,512]{2,1,0:T(8,128)(2,1)} %get-tuple-element.290), channel_id=1, source_target_pairs={{0,4},{4,8},{8,12},{12,16},{16,20},{20,24},{24,28},{1,5},{5,9},{9,... | collective-permute-start | bytes 1572872 | tf_op jit(solution)/shard_map/ppermute | solution.py:16
  370.1 2.5 collective-permute-done.23
  374.7 10.9 %collective-permute-start.17 = (bf16[1,512,512]{2,1,0:T(8,128)(2,1)S(1)}, bf16[1,512,512]{2,1,0:T(8,128)(2,1)}, u32[]{:S(2)}, u32[]{:S(2)}) collective-permute-start(bf16[1,512,512]{2,1,0:T(8,128)(2,1)S(1)} %get-tuple-element.288), channel_id=1, source_target_pairs={{0,12},{4,16},{8,20},{12,24},{16,28},{1,13},{5,17},{9,21},{13,25},... | collective-permute-start | bytes 1572872 | tf_op jit(solution)/shard_map/ppermute | solution.py:16
  385.6 135.4 %all-reduce.2.cloned.1.call-done = f32[512,512]{1,0:T(8,128)} async-done(((f32[512,512]{1,0:T(8,128)}), f32[512,512]{1,0:T(8,128)}) %all-reduce.2.cloned.1.call-update) | async-done | bytes 1048592 | tf_op jit(solution)/shard_map/psum | solution.py:133
  521.0 2.3 broadcast_multiply_fusion
  523.3 3.1 add_convert_fusion
  526.5 2.8 add_convert_fusion.1
  (190 shorter events, 136.6 us)
Async XLA Ops:
  7.2 176.2 %copy-start = (bf16[1,512,512]{2,1,0:T(8,128)(2,1)S(1)}, bf16[1,512,512]{2,1,0:T(8,128)(2,1)}, u32[]{:S(2)}) copy-start(bf16[1,512,512]{2,1,0:T(8,128)(2,1)} %param.16) | copy-start | bytes 1572868
  7.2 50.1 %copy-start.3 = (bf16[1,512,512]{2,1,0:T(8,128)(2,1)S(1)}, bf16[1,512,512]{2,1,0:T(8,128)(2,1)}, u32[]{:S(2)}) copy-start(bf16[1,512,512]{2,1,0:T(8,128)(2,1)} %param.13) | copy-start | bytes 1572868
  7.2 37.3 %copy-start.4 = (bf16[1,512,512]{2,1,0:T(8,128)(2,1)S(1)}, bf16[1,512,512]{2,1,0:T(8,128)(2,1)}, u32[]{:S(2)}) copy-start(bf16[1,512,512]{2,1,0:T(8,128)(2,1)} %param.14) | copy-start | bytes 1572868
  7.2 513.8 %all-reduce.2.cloned.1.call-start = ((), (), s32[]{:S(2)}) async-start(), calls=%async_computation | async-start | bytes 2097152 | tf_op jit(solution)/shard_map/psum | solution.py:133
  7.2 21.2 %collective-permute-start = (bf16[1,512,512]{2,1,0:T(8,128)(2,1)}, bf16[1,512,512]{2,1,0:T(8,128)(2,1)}, u32[]{:S(2)}, u32[]{:S(2)}) collective-permute-start(bf16[1,512,512]{2,1,0:T(8,128)(2,1)} %param.13), channel_id=1, source_target_pairs={{0,12},{4,16},{8,20},{12,24},{16,28},{1,13},{5,17},{9,21},{13,25},... | collective-permute-start | bytes 1572872 | tf_op jit(solution)/shard_map/ppermute | solution.py:16
  14.1 27.5 %collective-permute-start.1 = (bf16[1,512,512]{2,1,0:T(8,128)(2,1)}, bf16[1,512,512]{2,1,0:T(8,128)(2,1)}, u32[]{:S(2)}, u32[]{:S(2)}) collective-permute-start(bf16[1,512,512]{2,1,0:T(8,128)(2,1)} %param.13), channel_id=1, source_target_pairs={{0,8},{4,12},{8,16},{12,20},{16,24},{20,28},{1,9},{5,13},{9,17},{1... | collective-permute-start | bytes 1572872 | tf_op jit(solution)/shard_map/ppermute | solution.py:16
  18.3 26.2 %collective-permute-start.2 = (bf16[1,512,512]{2,1,0:T(8,128)(2,1)}, bf16[1,512,512]{2,1,0:T(8,128)(2,1)}, u32[]{:S(2)}, u32[]{:S(2)}) collective-permute-start(bf16[1,512,512]{2,1,0:T(8,128)(2,1)} %param.13), channel_id=1, source_target_pairs={{0,4},{4,8},{8,12},{12,16},{16,20},{20,24},{24,28},{1,5},{5,9},{9,... | collective-permute-start | bytes 1572872 | tf_op jit(solution)/shard_map/ppermute | solution.py:16
  21.8 46.4 %collective-permute-start.3 = (bf16[1,512,512]{2,1,0:T(8,128)(2,1)}, bf16[1,512,512]{2,1,0:T(8,128)(2,1)S(1)}, u32[]{:S(2)}, u32[]{:S(2)}) collective-permute-start(bf16[1,512,512]{2,1,0:T(8,128)(2,1)} %param.13), channel_id=1, source_target_pairs={{4,0},{8,4},{12,8},{16,12},{20,16},{24,20},{28,24},{5,1},{9,5},{13... | collective-permute-start | bytes 1572872 | tf_op jit(solution)/shard_map/ppermute | solution.py:16
  23.1 46.5 %collective-permute-start.4 = (bf16[1,512,512]{2,1,0:T(8,128)(2,1)}, bf16[1,512,512]{2,1,0:T(8,128)(2,1)S(1)}, u32[]{:S(2)}, u32[]{:S(2)}) collective-permute-start(bf16[1,512,512]{2,1,0:T(8,128)(2,1)} %param.13), channel_id=1, source_target_pairs={{8,0},{12,4},{16,8},{20,12},{24,16},{28,20},{9,1},{13,5},{17,9},{2... | collective-permute-start | bytes 1572872 | tf_op jit(solution)/shard_map/ppermute | solution.py:16
  28.4 28.9 %collective-permute-start.6 = (bf16[1,512,512]{2,1,0:T(8,128)(2,1)}, bf16[1,512,512]{2,1,0:T(8,128)(2,1)S(1)}, u32[]{:S(2)}, u32[]{:S(2)}) collective-permute-start(bf16[1,512,512]{2,1,0:T(8,128)(2,1)} %param.14), channel_id=1, source_target_pairs={{0,12},{4,16},{8,20},{12,24},{16,28},{1,13},{5,17},{9,21},{13,25},... | collective-permute-start | bytes 1572872 | tf_op jit(solution)/shard_map/ppermute | solution.py:16
  41.6 21.7 %collective-permute-start.7 = (bf16[1,512,512]{2,1,0:T(8,128)(2,1)}, bf16[1,512,512]{2,1,0:T(8,128)(2,1)S(1)}, u32[]{:S(2)}, u32[]{:S(2)}) collective-permute-start(bf16[1,512,512]{2,1,0:T(8,128)(2,1)} %param.14), channel_id=1, source_target_pairs={{0,8},{4,12},{8,16},{12,20},{16,24},{20,28},{1,9},{5,13},{9,17},{1... | collective-permute-start | bytes 1572872 | tf_op jit(solution)/shard_map/ppermute | solution.py:16
  44.5 22.3 %collective-permute-start.8 = (bf16[1,512,512]{2,1,0:T(8,128)(2,1)S(1)}, bf16[1,512,512]{2,1,0:T(8,128)(2,1)S(1)}, u32[]{:S(2)}, u32[]{:S(2)}) collective-permute-start(bf16[1,512,512]{2,1,0:T(8,128)(2,1)S(1)} %copy-done.4), channel_id=1, source_target_pairs={{0,4},{4,8},{8,12},{12,16},{16,20},{20,24},{24,28},{1,5},{5,9},{9,... | collective-permute-start | bytes 1572872 | tf_op jit(solution)/shard_map/ppermute | solution.py:16
  57.3 40.1 %collective-permute-start.5 = (bf16[1,512,512]{2,1,0:T(8,128)(2,1)S(1)}, bf16[1,512,512]{2,1,0:T(8,128)(2,1)S(1)}, u32[]{:S(2)}, u32[]{:S(2)}) collective-permute-start(bf16[1,512,512]{2,1,0:T(8,128)(2,1)S(1)} %copy-done.3), channel_id=1, source_target_pairs={{12,0},{16,4},{20,8},{24,12},{28,16},{13,1},{17,5},{21,9},{25,13},... | collective-permute-start | bytes 1572872 | tf_op jit(solution)/shard_map/ppermute | solution.py:16
  63.3 48.4 %collective-permute-start.9 = (bf16[1,512,512]{2,1,0:T(8,128)(2,1)S(1)}, bf16[1,512,512]{2,1,0:T(8,128)(2,1)}, u32[]{:S(2)}, u32[]{:S(2)}) collective-permute-start(bf16[1,512,512]{2,1,0:T(8,128)(2,1)S(1)} %copy-done.4), channel_id=1, source_target_pairs={{4,0},{8,4},{12,8},{16,12},{20,16},{24,20},{28,24},{5,1},{9,5},{13... | collective-permute-start | bytes 1572872 | tf_op jit(solution)/shard_map/ppermute | solution.py:16
  66.8 46.8 %collective-permute-start.10 = (bf16[1,512,512]{2,1,0:T(8,128)(2,1)S(1)}, bf16[1,512,512]{2,1,0:T(8,128)(2,1)}, u32[]{:S(2)}, u32[]{:S(2)}) collective-permute-start(bf16[1,512,512]{2,1,0:T(8,128)(2,1)S(1)} %copy-done.4), channel_id=1, source_target_pairs={{8,0},{12,4},{16,8},{20,12},{24,16},{28,20},{9,1},{13,5},{17,9},{2... | collective-permute-start | bytes 1572872 | tf_op jit(solution)/shard_map/ppermute | solution.py:16
  68.2 29.3 %copy-start.2 = (bf16[1,7,512,512]{3,2,1,0:T(8,128)(2,1)}, bf16[1,7,512,512]{3,2,1,0:T(8,128)(2,1)S(1)}, u32[]{:S(2)}) copy-start(bf16[1,7,512,512]{3,2,1,0:T(8,128)(2,1)S(1)} %bitcast_dynamic-update-slice_fusion.3) | copy-start | bytes 11010052
  68.2 63.0 %collective-permute-start.11 = (bf16[1,512,512]{2,1,0:T(8,128)(2,1)S(1)}, bf16[1,512,512]{2,1,0:T(8,128)(2,1)}, u32[]{:S(2)}, u32[]{:S(2)}) collective-permute-start(bf16[1,512,512]{2,1,0:T(8,128)(2,1)S(1)} %copy-done.4), channel_id=1, source_target_pairs={{12,0},{16,4},{20,8},{24,12},{28,16},{13,1},{17,5},{21,9},{25,13},... | collective-permute-start | bytes 1572872 | tf_op jit(solution)/shard_map/ppermute | solution.py:16
  97.5 1.9 copy-start.1
  145.3 38.1 %copy-start.5 = (bf16[512,512]{1,0:T(8,128)(2,1)S(1)}, bf16[512,512]{1,0:T(8,128)(2,1)}, u32[]{:S(2)}) copy-start(bf16[512,512]{1,0:T(8,128)(2,1)} %param.15) | copy-start | bytes 1572868
  289.7 58.7 %collective-permute-start.18 = (bf16[1,512,512]{2,1,0:T(8,128)(2,1)}, bf16[1,512,512]{2,1,0:T(8,128)(2,1)}, u32[]{:S(2)}, u32[]{:S(2)}) collective-permute-start(bf16[1,512,512]{2,1,0:T(8,128)(2,1)} %get-tuple-element.286), channel_id=1, source_target_pairs={{12,0},{16,4},{20,8},{24,12},{28,16},{13,1},{17,5},{21,9},{25,13},... | collective-permute-start | bytes 1572872 | tf_op jit(solution)/shard_map/ppermute | solution.py:16
  291.0 64.7 %collective-permute-start.19 = (bf16[1,512,512]{2,1,0:T(8,128)(2,1)}, bf16[1,512,512]{2,1,0:T(8,128)(2,1)}, u32[]{:S(2)}, u32[]{:S(2)}) collective-permute-start(bf16[1,512,512]{2,1,0:T(8,128)(2,1)} %get-tuple-element.285), channel_id=1, source_target_pairs={{8,0},{12,4},{16,8},{20,12},{24,16},{28,20},{9,1},{13,5},{17,9},{2... | collective-permute-start | bytes 1572872 | tf_op jit(solution)/shard_map/ppermute | solution.py:16
  292.3 69.4 %collective-permute-start.20 = (bf16[1,512,512]{2,1,0:T(8,128)(2,1)}, bf16[1,512,512]{2,1,0:T(8,128)(2,1)}, u32[]{:S(2)}, u32[]{:S(2)}) collective-permute-start(bf16[1,512,512]{2,1,0:T(8,128)(2,1)} %get-tuple-element.284), channel_id=1, source_target_pairs={{4,0},{8,4},{12,8},{16,12},{20,16},{24,20},{28,24},{5,1},{9,5},{13... | collective-permute-start | bytes 1572872 | tf_op jit(solution)/shard_map/ppermute | solution.py:16
  293.6 69.4 %collective-permute-start.21 = (bf16[1,512,512]{2,1,0:T(8,128)(2,1)}, bf16[1,512,512]{2,1,0:T(8,128)(2,1)}, u32[]{:S(2)}, u32[]{:S(2)}) collective-permute-start(bf16[1,512,512]{2,1,0:T(8,128)(2,1)} %get-tuple-element.283), channel_id=1, source_target_pairs={{0,4},{4,8},{8,12},{12,16},{16,20},{20,24},{24,28},{1,5},{5,9},{9,... | collective-permute-start | bytes 1572872 | tf_op jit(solution)/shard_map/ppermute | solution.py:16
  314.6 49.7 %collective-permute-start.22 = (bf16[1,512,512]{2,1,0:T(8,128)(2,1)}, bf16[1,512,512]{2,1,0:T(8,128)(2,1)}, u32[]{:S(2)}, u32[]{:S(2)}) collective-permute-start(bf16[1,512,512]{2,1,0:T(8,128)(2,1)} %get-tuple-element.282), channel_id=1, source_target_pairs={{0,8},{4,12},{8,16},{12,20},{16,24},{20,28},{1,9},{5,13},{9,17},{1... | collective-permute-start | bytes 1572872 | tf_op jit(solution)/shard_map/ppermute | solution.py:16
  348.4 24.2 %collective-permute-start.23 = (bf16[1,512,512]{2,1,0:T(8,128)(2,1)}, bf16[1,512,512]{2,1,0:T(8,128)(2,1)}, u32[]{:S(2)}, u32[]{:S(2)}) collective-permute-start(bf16[1,512,512]{2,1,0:T(8,128)(2,1)} %get-tuple-element.281), channel_id=1, source_target_pairs={{0,12},{4,16},{8,20},{12,24},{16,28},{1,13},{5,17},{9,21},{13,25},... | collective-permute-start | bytes 1572872 | tf_op jit(solution)/shard_map/ppermute | solution.py:16
  355.7 19.0 %collective-permute-start.12 = (bf16[1,512,512]{2,1,0:T(8,128)(2,1)}, bf16[1,512,512]{2,1,0:T(8,128)(2,1)}, u32[]{:S(2)}, u32[]{:S(2)}) collective-permute-start(bf16[1,512,512]{2,1,0:T(8,128)(2,1)} %get-tuple-element.293), channel_id=1, source_target_pairs={{12,0},{16,4},{20,8},{24,12},{28,16},{13,1},{17,5},{21,9},{25,13},... | collective-permute-start | bytes 1572872 | tf_op jit(solution)/shard_map/ppermute | solution.py:16
  361.7 164.7 %collective-permute-start.13 = (bf16[1,512,512]{2,1,0:T(8,128)(2,1)}, bf16[1,512,512]{2,1,0:T(8,128)(2,1)S(1)}, u32[]{:S(2)}, u32[]{:S(2)}) collective-permute-start(bf16[1,512,512]{2,1,0:T(8,128)(2,1)} %get-tuple-element.292), channel_id=1, source_target_pairs={{8,0},{12,4},{16,8},{20,12},{24,16},{28,20},{9,1},{13,5},{17,9},{2... | collective-permute-start | bytes 1572872 | tf_op jit(solution)/shard_map/ppermute | solution.py:16
  363.0 163.4 %collective-permute-start.14 = (bf16[1,512,512]{2,1,0:T(8,128)(2,1)}, bf16[1,512,512]{2,1,0:T(8,128)(2,1)S(1)}, u32[]{:S(2)}, u32[]{:S(2)}) collective-permute-start(bf16[1,512,512]{2,1,0:T(8,128)(2,1)} %get-tuple-element.291), channel_id=1, source_target_pairs={{4,0},{8,4},{12,8},{16,12},{20,16},{24,20},{28,24},{5,1},{9,5},{13... | collective-permute-start | bytes 1572872 | tf_op jit(solution)/shard_map/ppermute | solution.py:16
  364.3 162.1 %collective-permute-start.15 = (bf16[1,512,512]{2,1,0:T(8,128)(2,1)}, bf16[1,512,512]{2,1,0:T(8,128)(2,1)}, u32[]{:S(2)}, u32[]{:S(2)}) collective-permute-start(bf16[1,512,512]{2,1,0:T(8,128)(2,1)} %get-tuple-element.290), channel_id=1, source_target_pairs={{0,4},{4,8},{8,12},{12,16},{16,20},{20,24},{24,28},{1,5},{5,9},{9,... | collective-permute-start | bytes 1572872 | tf_op jit(solution)/shard_map/ppermute | solution.py:16
  372.6 153.9 %collective-permute-start.16 = (bf16[1,512,512]{2,1,0:T(8,128)(2,1)}, bf16[1,512,512]{2,1,0:T(8,128)(2,1)}, u32[]{:S(2)}, u32[]{:S(2)}) collective-permute-start(bf16[1,512,512]{2,1,0:T(8,128)(2,1)} %get-tuple-element.289), channel_id=1, source_target_pairs={{0,8},{4,12},{8,16},{12,20},{16,24},{20,28},{1,9},{5,13},{9,17},{1... | collective-permute-start | bytes 1572872 | tf_op jit(solution)/shard_map/ppermute | solution.py:16
  374.7 151.8 %collective-permute-start.17 = (bf16[1,512,512]{2,1,0:T(8,128)(2,1)S(1)}, bf16[1,512,512]{2,1,0:T(8,128)(2,1)}, u32[]{:S(2)}, u32[]{:S(2)}) collective-permute-start(bf16[1,512,512]{2,1,0:T(8,128)(2,1)S(1)} %get-tuple-element.288), channel_id=1, source_target_pairs={{0,12},{4,16},{8,20},{12,24},{16,28},{1,13},{5,17},{9,21},{13,25},... | collective-permute-start | bytes 1572872 | tf_op jit(solution)/shard_map/ppermute | solution.py:16
Sparse Core Ops, SparseCore 0:
  358.5 162.4 all-reduce.1
where the time goes:
time: 539 us; the launch traced here: 536 us
  waiting for transfers between devices  188 us (35%)
  matrix products  110 us (20%)
  starting transfers between devices  107 us (20%)
  local copies, waits for them, and re-layouts  74.6 us (14%)
  other arithmetic  40.6 us (8%)
  between operations  14.5 us (3%)
    psum x1, waiting for transfers between devices, body(): lax.psum(jnp.sum(w_terms, axis=0), ('seg', 'sample')) * grad_scale  135 us
    ppermute x24, starting transfers between devices, from_behind(): lax.ppermute(value, axis, [(source, source + steps) for source in range(i...  107 us
    ppermute x24, waiting for transfers between devices, from_behind(): lax.ppermute(value, axis, [(source, source + steps) for source in range(i...  52.9 us
    dot_general x16, matrix products, per_head(): jnp.dot(q_head, k_head.T, preferred_element_type=jnp.float32) * score_scale  31.6 us
    unnamed x29, local copies, waits for them, and re-layouts  19.1 us
    dot_general x8, matrix products, per_head(): grad_k = jnp.dot(d_score.T, q_head, preferred_element_type=jnp.float32)  18 us
    dot_general x8, matrix products, per_head(): d_prob = jnp.dot(da_head, v_head.T, preferred_element_type=jnp.float32)  16.4 us
    dot_general x8, matrix products, per_head(): jnp.dot(softmax_h, v_head, preferred_element_type=jnp.float32)  15.4 us
  transfers between devices with their start and end apart: 25, of which 6 were waited for; matrix products, arithmetic and copies ran while one was open for 12% of the time, Pallas kernels for 0%

commit v1 on v0

v1 whole, which is shorter than its diff:
```python
import functools
import math

import jax
import jax.numpy as jnp
from jax import lax
from jax.experimental import pallas as pl
from jax.experimental.pallas import tpu as pltpu
from jax.sharding import PartitionSpec as P

HEADS = 8
NBR = 3
REACH = 3
F32 = jnp.float32
BF16 = jnp.bfloat16
VMEM_LIMIT = 56 * 1024 * 1024


def mm(a, b):
    return lax.dot_general(a, b, (((1,), (0,)), ((), ())), preferred_element_type=F32)


def halves(block):
    turned = block.T
    width = turned.shape[0] // 2
    return jnp.concatenate([turned[:width], turned[width:]], axis=1)


def beside(turned):
    rows = turned.shape[1]
    return jnp.concatenate([turned[:, : rows // 2], turned[:, rows // 2 :]], axis=0).T


def pack_kernel(q_ref, k_ref, v_ref, g_ref, w_ref, out_ref):
    rows = q_ref.shape[0]
    width = q_ref.shape[1] // HEADS
    half = rows // 2
    d_attn = lax.dot_general(
        g_ref[...], w_ref[...], (((1,), (1,)), ((), ())), preferred_element_type=F32
    ).astype(BF16)
    for h in range(HEADS):
        cols = slice(h * width, (h + 1) * width)
        out_ref[h, :rows, :] = jnp.concatenate([k_ref[:, cols], v_ref[:, cols]], axis=1)
        out_ref[h, rows : rows + half, :] = jnp.concatenate(
            [q_ref[:half, cols], q_ref[half:, cols]], axis=1
        )
        out_ref[h, rows + half :, :] = jnp.concatenate(
            [d_attn[:half, cols], d_attn[half:, cols]], axis=1
        )


def forward_kernel(first, ids_ref, x_ref, attn_ref, turned_ref, inv_ref, p_ref, s_scr, m_scr, o_scr, v_scr):
    step = pl.program_id(0)
    blocks, two_rows, two_width = x_ref.shape
    rows, width = two_rows // 2, two_width // 2
    half = rows // 2
    used = ids_ref[step, NBR + 1]

    @pl.when(step == 0)
    def _():
        for b in range(blocks):
            v_scr[b, :width, :] = x_ref[b, :rows, :].T[width:]
            v_scr[b, width:, :] = jnp.ones((v_scr.shape[1] - width, rows), BF16)

    q_turned = halves(x_ref[step + first, rows : rows + half, :]) * BF16(1.0 / math.sqrt(width))
    q_wide = jnp.concatenate([q_turned, jnp.zeros_like(q_turned)], axis=0)

    def score(e):
        s = mm(x_ref[ids_ref[step, e], :rows, :], q_wide)
        s_scr[e] = s
        top = jnp.max(s, axis=0, keepdims=True)
        m_scr[...] = top if e == 0 else jnp.maximum(m_scr[...], top)

    def mix(e):
        p = jnp.exp(s_scr[e] - m_scr[...]).astype(BF16)
        p_ref[0, e] = p
        term = mm(v_scr[ids_ref[step, e]], p)
        o_scr[...] = term if e == 0 else o_scr[...] + term

    for e in range(NBR + 1):
        if e < 2:
            score(e)
        else:
            pl.when(e < used)(functools.partial(score, e))
    for e in range(NBR + 1):
        if e < 2:
            mix(e)
        else:
            pl.when(e < used)(functools.partial(mix, e))
    inv = 1.0 / o_scr[width : width + 1, :]
    attn = (o_scr[:width, :] * inv).astype(BF16)
    turned_ref[0] = attn
    inv_ref[0] = jnp.broadcast_to(inv, inv_ref.shape[1:])
    attn_ref[0] = beside(attn)


def backward_kernel(first, ids_ref, x_ref, turned_ref, inv_ref, p_ref, out_ref, acc, dq_scr, k_scr, qz_scr, zd_scr, dp_scr):
    step = pl.program_id(0)
    blocks, two_rows, two_width = x_ref.shape
    rows, width = two_rows // 2, two_width // 2
    half = rows // 2
    used = ids_ref[step, NBR + 1]
    scale = 1.0 / math.sqrt(width)

    @pl.when(step == 0)
    def _():
        acc[...] = jnp.zeros_like(acc)
        for b in range(blocks):
            k_scr[b] = x_ref[b, :rows, :].T[:width]

    own = step + first
    q_turned = halves(x_ref[own, rows : rows + half, :])
    blank = jnp.zeros_like(q_turned)
    da = halves(x_ref[own, rows + half :, :]).astype(F32)
    inv = inv_ref[0, :1, :]
    da_inv = da * inv
    delta = jnp.sum(da_inv * turned_ref[0].astype(F32), axis=0, keepdims=True) * scale
    da_half = da_inv.astype(BF16)
    dp_scr[...] = jnp.concatenate([blank, da_half * BF16(scale)], axis=0)
    qz_scr[...] = jnp.concatenate([q_turned, blank], axis=0).T
    zd_scr[...] = jnp.concatenate([blank, da_half], axis=0).T

    def term(e):
        b = ids_ref[step, e]
        d_prob = mm(x_ref[b, :rows, :], dp_scr[...])
        p = p_ref[0, e]
        ds = (p.astype(F32) * (d_prob - delta)).astype(BF16)
        dq = mm(k_scr[b], ds)
        dq_scr[...] = dq if e == 0 else dq_scr[...] + dq
        acc[b] += mm(ds, qz_scr[...]) + mm(p, zd_scr[...])

    for e in range(NBR + 1):
        if e < 2:
            term(e)
        else:
            pl.when(e < used)(functools.partial(term, e))
    out_ref[own, rows:, :] = beside(dq_scr[...].astype(BF16))

    @pl.when(step == pl.num_programs(0) - 1)
    def _():
        for b in range(blocks):
            out_ref[b, :rows, :] = acc[b].astype(BF16)


def project_kernel(a_ref, g_ref, w_ref, out_ref, term_ref):
    left = jnp.concatenate([a_ref[h, :, : a_ref.shape[2] // 2] for h in range(HEADS)], axis=1)
    right = jnp.concatenate([a_ref[h, :, a_ref.shape[2] // 2 :] for h in range(HEADS)], axis=1)
    attn = jnp.concatenate([left, right], axis=0)
    out_ref[...] = mm(attn, w_ref[...]).astype(BF16)
    term_ref[...] = lax.dot_general(
        attn, g_ref[...], (((0,), (0,)), ((), ())), preferred_element_type=F32
    ).astype(BF16)


def unpack_kernel(y_ref, dq_ref, dk_ref, dv_ref):
    rows = dq_ref.shape[0]
    half = rows // 2
    width = dq_ref.shape[1] // HEADS
    for h in range(HEADS):
        cols = slice(h * width, (h + 1) * width)
        dk_ref[:, cols] = y_ref[h, :rows, :width]
        dv_ref[:, cols] = y_ref[h, :rows, width:]
        dq_ref[:half, cols] = y_ref[h, rows:, :width]
        dq_ref[half:, cols] = y_ref[h, rows:, width:]


def params():
    return pltpu.CompilerParams(vmem_limit_bytes=VMEM_LIMIT)


def cost(flops, bytes_accessed, exps=0):
    return pl.CostEstimate(flops=flops, bytes_accessed=bytes_accessed, transcendentals=exps)


def body(queries, key_rows, value_rows, w_out, grad_out, neighbours):
    _, rows, model = queries.shape
    width = model // HEADS
    half = rows // 2
    seg = lax.axis_size("seg")
    samples = lax.axis_size("sample")
    groups = seg // HEADS
    split = [[g * HEADS + i for i in range(HEADS)] for g in range(groups)] if groups > 1 else None
    halo = REACH if groups > 1 else 0
    blocks = HEADS + 2 * halo

    def swap(array):
        return lax.all_to_all(array, "seg", 0, 0, axis_index_groups=split)

    def shifted(array, by):
        pairs = [(s, s + by) for s in range(seg) if 0 <= s + by < seg]
        return lax.ppermute(array, "seg", pairs)

    listed = lax.all_gather(neighbours[0, 0], "seg", axis_index_groups=split)
    base = lax.axis_index("seg") // HEADS * HEADS
    owner = base + jnp.arange(HEADS, dtype=jnp.int32)[:, None]
    in_use = listed != owner
    ids = jnp.where(in_use, listed, owner) - base + halo
    ids = jnp.concatenate(
        [
            owner - base + halo,
            ids,
            1 + jnp.sum(in_use.astype(jnp.int32), axis=1, keepdims=True),
        ],
        axis=1,
    )

    packed = pl.pallas_call(
        pack_kernel,
        out_shape=jax.ShapeDtypeStruct((HEADS, 2 * rows, 2 * width), BF16),
        compiler_params=params(),
        cost_estimate=cost(2 * rows * model * model, 10 * rows * model),
        name="pack",
    )(queries[0], key_rows[0], value_rows[0], grad_out[0], w_out)
    x = swap(packed)
    if halo:
        x = jnp.concatenate([shifted(x[-halo:], HEADS), x, shifted(x[:halo], -HEADS)], axis=0)

    whole = lambda shape: pl.BlockSpec(shape, lambda i, ids: (0,) * len(shape))
    each = lambda shape: pl.BlockSpec((1,) + shape, lambda i, ids: (i,) + (0,) * len(shape))
    ones = 16
    units = HEADS * (NBR + 1)
    attn_out, attn_turned, inverse, probs = pl.pallas_call(
        functools.partial(forward_kernel, halo),
        grid_spec=pltpu.PrefetchScalarGridSpec(
            num_scalar_prefetch=1,
            grid=(HEADS,),
            in_specs=[whole(x.shape)],
            out_specs=[
                each((half, 2 * width)),
                each((width, rows)),
                each((8, rows)),
                each((NBR + 1, rows, rows)),
            ],
            scratch_shapes=[
                pltpu.VMEM((NBR + 1, rows, rows), F32),
                pltpu.VMEM((1, rows), F32),
                pltpu.VMEM((width + ones, rows), F32),
                pltpu.VMEM((blocks, width + ones, rows), BF16),
            ],
        ),
        out_shape=[
            jax.ShapeDtypeStruct((HEADS, half, 2 * width), BF16),
            jax.ShapeDtypeStruct((HEADS, width, rows), BF16),
            jax.ShapeDtypeStruct((HEADS, 8, rows), F32),
            jax.ShapeDtypeStruct((HEADS, NBR + 1, rows, rows), BF16),
        ],
        compiler_params=params(),
        cost_estimate=cost(units * rows * rows * 512, 20 * 2**20, units * rows * rows),
        name="forward",
    )(ids, x)
    attn_home = swap(attn_out)

    grads = pl.pallas_call(
        functools.partial(backward_kernel, halo),
        grid_spec=pltpu.PrefetchScalarGridSpec(
            num_scalar_prefetch=1,
            grid=(HEADS,),
            in_specs=[
                whole(x.shape),
                each((width, rows)),
                each((8, rows)),
                each((NBR + 1, rows, rows)),
            ],
            out_specs=whole((blocks, rows + half, 2 * width)),
            scratch_shapes=[
                pltpu.VMEM((blocks, rows, 2 * width), F32),
                pltpu.VMEM((width, rows), F32),
                pltpu.VMEM((blocks, width, rows), BF16),
                pltpu.VMEM((rows, 2 * width), BF16),
                pltpu.VMEM((rows, 2 * width), BF16),
                pltpu.VMEM((2 * width, rows), BF16),
            ],
        ),
        out_shape=jax.ShapeDtypeStruct((blocks, rows + half, 2 * width), BF16),
        compiler_params=params(),
        cost_estimate=cost(units * rows * rows * 1024, 20 * 2**20),
        name="backward",
    )(ids, x, attn_turned, inverse, probs)
    if halo:
        kv_terms = grads[:, :rows].astype(F32)
        inner = kv_terms[halo:-halo]
        inner = inner.at[-halo:].add(shifted(grads[:halo, :rows], -HEADS).astype(F32))
        inner = inner.at[:halo].add(shifted(grads[-halo:, :rows], HEADS).astype(F32))
        grads = jnp.concatenate([inner.astype(BF16), grads[halo:-halo, rows:]], axis=1)
    grads_home = swap(grads)

    attended, w_term = pl.pallas_call(
        project_kernel,
        out_shape=[
            jax.ShapeDtypeStruct((rows, model), BF16),
            jax.ShapeDtypeStruct((model, model), BF16),
        ],
        compiler_params=params(),
        cost_estimate=cost(4 * rows * model * model, 10 * rows * model),
        name="project",
    )(attn_home, grad_out[0], w_out)
    part = model // samples
    piece = part // seg
    w_part = lax.all_to_all(w_term.reshape(samples, part, model), "sample", 0, 0)
    w_part = jnp.sum(w_part.astype(F32), axis=0).astype(BF16)
    w_piece = lax.all_to_all(w_part.reshape(seg, piece, model), "seg", 0, 0)
    grad_scale = 1.0 / math.sqrt(samples * rows * seg)
    w_piece = (jnp.sum(w_piece.astype(F32), axis=0) * grad_scale).astype(BF16)
    w_part = lax.all_to_all(jnp.broadcast_to(w_piece, (seg, piece, model)), "seg", 0, 0)
    w_part = w_part.reshape(part, model)
    w_all = lax.all_to_all(jnp.broadcast_to(w_part, (samples, part, model)), "sample", 0, 0)
    grad_w_out = w_all.reshape(model, model).astype(F32)

    grad_q, grad_k, grad_v = pl.pallas_call(
        unpack_kernel,
        out_shape=[jax.ShapeDtypeStruct((rows, model), BF16)] * 3,
        compiler_params=params(),
        cost_estimate=cost(0, 12 * rows * model),
        name="unpack",
    )(grads_home)
    return attended[None], grad_q[None], grad_k[None], grad_v[None], grad_w_out


def solution(mesh):
    rows = P("sample", "seg", None)
    return jax.shard_map(
        body,
        mesh=mesh,
        in_specs=(rows, rows, rows, P(), rows, rows),
        out_specs=(rows, rows, rows, rows, P()),
        check_vma=False,
    )
```

time: 539 us -> 213 us (0.40)
  waiting for transfers between devices: 188 us -> 37.2 us
  matrix products: 110 us -> 0 us
  blocking collectives: 0 us -> 105 us
  starting transfers between devices: 107 us -> 14.4 us
  local copies, waits for them, and re-layouts: 74.6 us -> 3.43 us
  Pallas kernels: 0 us -> 49.4 us
  other arithmetic: 40.6 us -> 2.11 us
  between operations: 14.5 us -> 0.69 us
    psum x1 -> x0, waiting for transfers between devices: 135 us -> none  [body(): lax.psum(jnp.sum(w_terms, axis=0), ('seg', 'sample')) * grad_scale]
    dot_general x59 -> x0, matrix products: 110 us -> none  [the longest x16 31.6 us: per_head(): jnp.dot(q_head, k_head.T, preferred_element_type=jnp.float32) * score_scale]
    ppermute x24 -> x0, starting transfers between devices: 107 us -> none  [from_behind(): lax.ppermute(value, axis, [(source, source + steps) for source in range(i...]
    all_to_all x0 -> x4, blocking collectives: none -> 55.7 us  [the longest x1 22.9 us: swap(): return lax.all_to_all(array, 'seg', 0, 0, axis_index_groups=split)]
    ppermute x24 -> x0, waiting for transfers between devices: 52.9 us -> none  [from_behind(): lax.ppermute(value, axis, [(source, source + steps) for source in range(i...]
    all_gather x0 -> x1, blocking collectives: none -> 49.5 us  [body(): listed = lax.all_gather(neighbours[0, 0], 'seg', axis_index_groups=split)]
    pallas_call x0 -> x5, Pallas kernels: none -> 49.4 us  [the longest x1 22.5 us: body(): pl.pallas_call(functools.partial(backward_kernel, halo), grid_spec=pltpu....]
    all_to_all x0 -> x3, waiting for transfers between devices: none -> 37.2 us  [the longest x2 37.2 us: swap(): return lax.all_to_all(array, 'seg', 0, 0, axis_index_groups=split)]
  transfers between devices with their start and end apart: 25 -> 3, of which waited for: 6 -> 1; matrix products, arithmetic and copies ran while one was open for 12% -> 1% of each run, Pallas kernels for 0% -> 11%
where the time goes in v1:
time: 213 us; the launch traced here: 212 us
  blocking collectives  105 us (49%)
  Pallas kernels  49.4 us (23%)
  waiting for transfers between devices  37.2 us (17%)
  starting transfers between devices  14.4 us (7%)
  local copies, waits for them, and re-layouts  3.43 us (2%)
    all_gather x1, blocking collectives, body(): listed = lax.all_gather(neighbours[0, 0], 'seg', axis_index_groups=split)  49.5 us
    all_to_all x2, waiting for transfers between devices, swap(): return lax.all_to_all(array, 'seg', 0, 0, axis_index_groups=split)  37.2 us
    all_to_all x1, blocking collectives, swap(): return lax.all_to_all(array, 'seg', 0, 0, axis_index_groups=split)  22.9 us
    pallas_call x1, Pallas kernels, body(): pl.pallas_call(functools.partial(backward_kernel, halo), grid_spec=pltpu....  22.5 us
    pallas_call x1, Pallas kernels, body(): pl.pallas_call(functools.partial(forward_kernel, halo), grid_spec=pltpu.P...  16.9 us
    all_to_all x1, blocking collectives, body(): lax.all_to_all(w_term.reshape(samples, part, model), 'sample', 0, 0)  12.3 us
    all_to_all x2, starting transfers between devices, swap(): return lax.all_to_all(array, 'seg', 0, 0, axis_index_groups=split)  11 us
    all_to_all x1, blocking collectives, body(): w_piece = lax.all_to_all(w_part.reshape(seg, piece, model), 'seg', 0, 0)  10.8 us
  transfers between devices with their start and end apart: 3, of which 1 were waited for; matrix products, arithmetic and copies ran while one was open for 1% of the time, Pallas kernels for 11%

profile of v1, /device:TPU:0, one launch (start us, length us, event | category | flops | bytes accessed | tf_op | source)
XLA Modules:
  0.0 212.5 jit_solution(5223389756043778715)
XLA Ops:
  0.6 3.6 %pack.1 = bf16[8,1024,128]{2,1,0:T(8,128)(2,1)} custom-call(bf16[512,512]{1,0:T(8,128)(2,1)} %bitcast.17, bf16[512,512]{1,0:T(8,128)(2,1)} %bitcast.18, bf16[512,512]{1,0:T(8,128)(2,1)} %bitcast.19, bf16[512,512]{1,0:T(8,128)(2,1)} %bitcast.20, bf16[512,512]{1,0:T(8,128)(2,1)} %w_ref.3), custom_call_target="tpu_custom_call" | custom-call | flops 268435456 | bytes 2621440 | tf_op jit(solution)/shard_map/pack/pallas_call | solution.py:207
  4.3 0.0 copy-start.2
  4.3 7.4 %all-to-all-start = ((bf16[8,1024,128]{2,1,0:T(8,128)(2,1)}), bf16[8,1024,128]{2,1,0:T(8,128)(2,1)S(1)}, u32[]{:S(2)}, u32[]{:S(2)}) async-start(bf16[8,1024,128]{2,1,0:T(8,128)(2,1)} %pack.1), calls=%async_computation | async-start | bytes 4194304 | tf_op jit(solution)/shard_map/all_to_all | solution.py:187
  11.7 0.0 copy-done.2
  11.7 49.5 %all-gather = s32[8,1,3]{2,1,0:T(1,128)S(1)} all-gather(s32[1,1,3]{2,1,0:T(1,128)S(1)} %copy-done.2), channel_id=2, replica_groups=mesh['seg'=8,'sample'=4] {'seg'}, dimensions={0}, use_global_device_ids=true | all-gather | bytes 108 | tf_op jit(solution)/shard_map/all_gather | solution.py:193
  61.1 0.2 fusion
  61.3 0.1 copy.22
  61.4 0.7 pad_add_fusion.ids_ref
  62.1 0.0 all-to-all-done.x_ref
  62.1 0.0 copy-start.1
  62.1 1.3 copy-done.1
  63.4 16.9 %forward.1 = (bf16[8,256,128]{2,1,0:T(8,128)(2,1)}, bf16[8,64,512]{2,1,0:T(8,128)(2,1)}, f32[8,8,512]{2,1,0:T(8,128)}, bf16[8,4,512,512]{3,2,1,0:T(8,128)(2,1)}) custom-call(s32[8,5]{1,0:T(8,128)} %pad_add_fusion.ids_ref, bf16[8,1024,128]{2,1,0:T(8,128)(2,1)} %copy-done.1), custom_call_target="tpu_custom_call" | custom-call | flops 4294967296 | bytes 20971520 | tf_op jit(solution)/shard_map/forward/pallas_call | solution.py:222
  80.3 22.9 %all_to_all.35.a_ref = bf16[8,256,128]{2,1,0:T(8,128)(2,1)} all-to-all(bf16[8,256,128]{2,1,0:T(8,128)(2,1)} %get-tuple-element.14), channel_id=1, replica_groups=mesh['seg'=8,'sample'=4] {'seg'}, dimensions={0} | all-to-all | bytes 1048576 | tf_op jit(solution)/shard_map/all_to_all | solution.py:187
  103.3 2.9 %project.1 = (bf16[512,512]{1,0:T(8,128)(2,1)}, bf16[512,512]{1,0:T(8,128)(2,1)}) custom-call(bf16[8,256,128]{2,1,0:T(8,128)(2,1)} %all_to_all.35.a_ref, bf16[512,512]{1,0:T(8,128)(2,1)} %bitcast.21, bf16[512,512]{1,0:T(8,128)(2,1)} %w_ref.3), custom_call_target="tpu_custom_call" | custom-call | flops 536870912 | bytes 2621440 | tf_op jit(solution)/shard_map/project/pallas_call | solution.py:287
  106.2 12.3 %all_to_all.36 = bf16[4,128,512]{2,1,0:T(8,128)(2,1)S(1)} all-to-all(bf16[4,128,512]{2,1,0:T(8,128)(2,1)} %bitcast.23), channel_id=1, replica_groups=mesh['seg'=8,'sample'=4] {'sample'}, dimensions={0} | all-to-all | bytes 1048576 | tf_op jit(solution)/shard_map/all_to_all | solution.py:299
  118.4 0.1 reduce_sum.31
  118.5 10.8 %all_to_all.37 = bf16[8,16,512]{2,1,0:T(8,128)(2,1)S(1)} all-to-all(bf16[8,16,512]{2,1,0:T(8,128)(2,1)S(1)} %bitcast.24), channel_id=1, replica_groups=mesh['seg'=8,'sample'=4] {'seg'}, dimensions={0} | all-to-all | bytes 262144 | tf_op jit(solution)/shard_map/all_to_all | solution.py:301
  129.4 9.7 %all_to_all.38 = bf16[8,16,512]{2,1,0:T(8,128)(2,1)S(1)} all-to-all(bf16[8,16,512]{2,1,0:T(8,128)(2,1)S(1)} %broadcast_in_dim.30), channel_id=1, replica_groups=mesh['seg'=8,'sample'=4] {'seg'}, dimensions={0} | all-to-all | bytes 262144 | tf_op jit(solution)/shard_map/all_to_all | solution.py:304
  139.1 0.8 broadcast_in_dim.31
  139.9 3.5 %all-to-all-start.6 = ((bf16[4,128,512]{2,1,0:T(8,128)(2,1)}), bf16[4,128,512]{2,1,0:T(8,128)(2,1)S(1)}, u32[]{:S(2)}, u32[]{:S(2)}) async-start(bf16[4,128,512]{2,1,0:T(8,128)(2,1)} %broadcast_in_dim.31), calls=%async_computation.6 | async-start | bytes 1048576 | tf_op jit(solution)/shard_map/all_to_all | solution.py:306
  143.4 22.5 %backward.1 = bf16[8,768,128]{2,1,0:T(8,128)(2,1)} custom-call(s32[8,5]{1,0:T(8,128)} %pad_add_fusion.ids_ref, bf16[8,1024,128]{2,1,0:T(8,128)(2,1)} %copy-done.1, bf16[8,64,512]{2,1,0:T(8,128)(2,1)} %get-tuple-element.16.turned_ref, f32[8,8,512]{2,1,0:T(8,128)} %get-tuple-element.17.inv_ref, bf16[8,4,512,512]{3,2,1,0:T(8,128)(2,1)} %get-tuple-element.18.p_ref), custom_call_target="tpu_custom_call" | custom-call | flops 8589934592 | bytes 20971520 | tf_op jit(solution)/shard_map/backward/pallas_call | solution.py:253
  165.9 0.0 all-to-all-done.6
  165.9 3.6 %all-to-all-start.2 = ((bf16[8,768,128]{2,1,0:T(8,128)(2,1)}), bf16[8,768,128]{2,1,0:T(8,128)(2,1)S(1)}, u32[]{:S(2)}, u32[]{:S(2)}) async-start(bf16[8,768,128]{2,1,0:T(8,128)(2,1)} %backward.1), calls=%async_computation.2 | async-start | bytes 3145728 | tf_op jit(solution)/shard_map/all_to_all | solution.py:187
  169.5 1.1 bitcast_convert_fusion
  170.7 37.2 %all-to-all-done.2.y_ref = bf16[8,768,128]{2,1,0:T(8,128)(2,1)S(1)} async-done(((bf16[8,768,128]{2,1,0:T(8,128)(2,1)}), bf16[8,768,128]{2,1,0:T(8,128)(2,1)S(1)}, u32[]{:S(2)}, u32[]{:S(2)}) %all-to-all-start.2) | async-done | bytes 1572896 | tf_op jit(solution)/shard_map/all_to_all | solution.py:187
  207.9 0.0 copy-start
  207.9 1.2 copy-done
  209.1 3.4 %unpack.1 = (bf16[512,512]{1,0:T(8,128)(2,1)}, bf16[512,512]{1,0:T(8,128)(2,1)}, bf16[512,512]{1,0:T(8,128)(2,1)}) custom-call(bf16[8,768,128]{2,1,0:T(8,128)(2,1)} %copy-done), custom_call_target="tpu_custom_call" | custom-call | bytes 3145728 | tf_op jit(solution)/shard_map/unpack/pallas_call | solution.py:309
  (6 shorter events, 0.1 us)
Async XLA Ops:
  4.3 7.4 %copy-start.2 = (s32[1,1,3]{2,1,0:T(1,128)S(1)}, s32[1,1,3]{2,1,0:T(1,128)}, u32[]{:S(2)}) copy-start(s32[1,1,3]{2,1,0:T(1,128)} %param.11) | copy-start | bytes 40
  4.3 57.8 %all-to-all-start = ((bf16[8,1024,128]{2,1,0:T(8,128)(2,1)}), bf16[8,1024,128]{2,1,0:T(8,128)(2,1)S(1)}, u32[]{:S(2)}, u32[]{:S(2)}) async-start(bf16[8,1024,128]{2,1,0:T(8,128)(2,1)} %pack.1), calls=%async_computation | async-start | bytes 4194304 | tf_op jit(solution)/shard_map/all_to_all | solution.py:187
  62.1 1.3 copy-start.1
  139.9 26.0 %all-to-all-start.6 = ((bf16[4,128,512]{2,1,0:T(8,128)(2,1)}), bf16[4,128,512]{2,1,0:T(8,128)(2,1)S(1)}, u32[]{:S(2)}, u32[]{:S(2)}) async-start(bf16[4,128,512]{2,1,0:T(8,128)(2,1)} %broadcast_in_dim.31), calls=%async_computation.6 | async-start | bytes 1048576 | tf_op jit(solution)/shard_map/all_to_all | solution.py:306
  165.9 42.0 %all-to-all-start.2 = ((bf16[8,768,128]{2,1,0:T(8,128)(2,1)}), bf16[8,768,128]{2,1,0:T(8,128)(2,1)S(1)}, u32[]{:S(2)}, u32[]{:S(2)}) async-start(bf16[8,768,128]{2,1,0:T(8,128)(2,1)} %backward.1), calls=%async_computation.2 | async-start | bytes 3145728 | tf_op jit(solution)/shard_map/all_to_all | solution.py:187
  207.9 1.2 copy-start

commit v2 on v1

v2 whole, which is shorter than its diff:
```python
import functools
import math

import jax
import jax.numpy as jnp
from jax import lax
from jax.experimental import pallas as pl
from jax.experimental.pallas import tpu as pltpu
from jax.sharding import PartitionSpec as P

HEADS = 8
NBR = 3
REACH = 3
F32 = jnp.float32
BF16 = jnp.bfloat16
VMEM_LIMIT = 56 * 1024 * 1024


def mm(a, b):
    return lax.dot_general(a, b, (((1,), (0,)), ((), ())), preferred_element_type=F32)


def halves(block):
    turned = block.T
    width = turned.shape[0] // 2
    return jnp.concatenate([turned[:width], turned[width:]], axis=1)


def beside(turned):
    rows = turned.shape[1]
    return jnp.concatenate([turned[:, : rows // 2], turned[:, rows // 2 :]], axis=0).T


def pack_kernel(near_ref, q_ref, k_ref, v_ref, g_ref, w_ref, out_ref, d_ref):
    rows = q_ref.shape[0]
    width = q_ref.shape[1] // HEADS
    half = rows // 2
    here = lax.axis_index("seg")
    line = lax.broadcasted_iota(jnp.int32, (16, 2 * width), 0)
    offsets = jnp.zeros((16, 2 * width), F32)
    for e in range(NBR):
        offsets = jnp.where(line == e, (near_ref[0, e] - here + REACH).astype(F32), offsets)
    for h in range(HEADS):
        cols = slice(h * width, (h + 1) * width)
        out_ref[h, :rows, :] = jnp.concatenate([k_ref[:, cols], v_ref[:, cols]], axis=1)
        out_ref[h, rows : rows + half, :] = jnp.concatenate(
            [q_ref[:half, cols], q_ref[half:, cols]], axis=1
        )
        out_ref[h, rows + half :, :] = offsets.astype(BF16)
    d_attn = lax.dot_general(
        g_ref[...], w_ref[...], (((1,), (1,)), ((), ())), preferred_element_type=F32
    ).astype(BF16)
    for h in range(HEADS):
        cols = slice(h * width, (h + 1) * width)
        d_ref[h] = jnp.concatenate([d_attn[:half, cols], d_attn[half:, cols]], axis=1)


def list_units(first, near_ref, patch_of, block_of):
    count = jnp.int32(0)
    for p in range(HEADS):
        patch_of[count] = p
        block_of[count] = p + first
        count = count + 1
        for e in range(NBR):
            offset = near_ref[p, e] - REACH
            patch_of[count] = p
            block_of[count] = p + first + offset
            count = count + jnp.where(offset != 0, 1, 0)
    patch_of[count] = -1


def is_first(patch_of, u):
    return jnp.logical_or(u == 0, patch_of[jnp.maximum(u - 1, 0)] != patch_of[u])


def in_turn(step, total, one, two):
    for slot in range(2):
        mine = step % 2 == slot

        @pl.when(jnp.logical_and(mine, step == 0))
        def _():
            one(step, slot)

        @pl.when(jnp.logical_and(mine, jnp.logical_and(step > 0, step < total)))
        def _():
            two(step - 1, 1 - slot, lambda: one(step, slot))

        @pl.when(jnp.logical_and(mine, step == total))
        def _():
            two(step - 1, 1 - slot, lambda: None)


def forward_kernel(first, near_ref, x_ref, attn_ref, turned_ref, stat_ref, top_ref, p_ref, s0, s1, m_scr, o_scr, v_scr, q_scr, patch_of, block_of):
    step = pl.program_id(0)
    total = near_ref[0, NBR]
    blocks = x_ref.shape[0]
    rows, width = s0.shape[0], x_ref.shape[2] // 2
    half = rows // 2
    scores = (s0, s1)

    @pl.when(step == 0)
    def _():
        list_units(first, near_ref, patch_of, block_of)
        o_scr[...] = jnp.zeros_like(o_scr)
        for b in range(blocks):
            v_scr[b, :width, :] = x_ref[b, :rows, :].T[width:]
            v_scr[b, width:, :] = jnp.ones((v_scr.shape[1] - width, rows), BF16)
        for p in range(HEADS):
            turned = halves(x_ref[p + first, rows : rows + half, :])
            q_scr[p, :width, :] = turned * BF16(1.0 / math.sqrt(width))
            q_scr[p, width:, :] = jnp.zeros_like(turned)

    def score(u, slot):
        s = mm(x_ref[block_of[u], :rows, :], q_scr[patch_of[u]])
        scores[slot][...] = s
        top = jnp.max(s, axis=0, keepdims=True)
        top = jnp.where(is_first(patch_of, u), top, jnp.maximum(top, m_scr[...]))
        m_scr[...] = top
        top_ref[u] = top

    def mix(u, slot, then):
        m = top_ref[u]
        p = jnp.exp(scores[slot][...] - m).astype(BF16)
        p_ref[0] = p
        keep = jnp.exp(top_ref[jnp.maximum(u - 1, 0)] - m)
        keep = jnp.where(is_first(patch_of, u), 0.0, keep)
        then()
        o_scr[...] = o_scr[...] * keep + mm(v_scr[block_of[u]], p)

    in_turn(step, total, score, mix)

    u = jnp.maximum(step - 1, 0)
    ended = jnp.logical_and(step > 0, step <= total)

    @pl.when(jnp.logical_and(ended, patch_of[u + 1] != patch_of[u]))
    def _():
        p = patch_of[u]
        inv = 1.0 / o_scr[width : width + 1, :]
        attn = (o_scr[:width, :] * inv).astype(BF16)
        turned_ref[p] = attn
        stat_ref[p] = jnp.concatenate([inv, top_ref[u]], axis=0)
        attn_ref[p] = beside(attn)


def backward_kernel(first, near_ref, x_ref, d_ref, turned_ref, stat_ref, top_ref, p_ref, out_ref, acc, dp0, dp1, z0, z1, e0, e1, dq_scr, k_scr, qz_scr, d_scr, delta_scr, patch_of, block_of):
    step = pl.program_id(0)
    total = near_ref[0, NBR]
    blocks = x_ref.shape[0]
    rows, width = dp0.shape[0], x_ref.shape[2] // 2
    half = rows // 2
    scale = 1.0 / math.sqrt(width)
    d_probs, d_rows, shifts = (dp0, dp1), (z0, z1), (e0, e1)

    @pl.when(step == 0)
    def _():
        list_units(first, near_ref, patch_of, block_of)
        acc[...] = jnp.zeros_like(acc)
        dq_scr[...] = jnp.zeros_like(dq_scr)
        for b in range(blocks):
            k_scr[b] = x_ref[b, :rows, :].T[:width]
        blank = jnp.zeros((half, width), BF16)
        for p in range(HEADS):
            pair = x_ref[p + first, rows : rows + half, :]
            qz_scr[p, :half, :] = jnp.concatenate([pair[:, :width], blank], axis=1)
            qz_scr[p, half:, :] = jnp.concatenate([pair[:, width:], blank], axis=1)
            turned = halves(d_ref[p]).astype(F32)
            d_scr[p] = turned
            delta_scr[p] = jnp.sum(turned * turned_ref[p].astype(F32), axis=0, keepdims=True)

    def enter(u, slot):
        p = patch_of[u]
        share = jnp.exp(top_ref[u] - stat_ref[p, 1:2, :]) * stat_ref[p, 0:1, :]
        mine = (d_scr[p] * share).astype(BF16)
        blank = jnp.zeros_like(mine)
        d_probs[slot][...] = mm(
            x_ref[block_of[u], :rows, :],
            jnp.concatenate([blank, mine * BF16(scale)], axis=0),
        )
        shifts[slot][...] = delta_scr[p] * share * scale
        d_rows[slot][...] = jnp.concatenate([blank, mine], axis=0).T

    def leave(u, slot, then):
        b, p = block_of[u], patch_of[u]
        prob = p_ref[0]
        ds = (prob.astype(F32) * (d_probs[slot][...] - shifts[slot][...])).astype(BF16)
        then()
        dq = mm(k_scr[b], ds)
        dq_scr[...] = dq + jnp.where(is_first(patch_of, u), 0.0, dq_scr[...])
        acc[b] += mm(
            jnp.concatenate([ds, prob], axis=1),
            jnp.concatenate([qz_scr[p], d_rows[slot][...]], axis=0),
        )

    in_turn(step, total, enter, leave)

    u = jnp.maximum(step - 1, 0)
    ended = jnp.logical_and(step > 0, step <= total)

    @pl.when(jnp.logical_and(ended, patch_of[u + 1] != patch_of[u]))
    def _():
        out_ref[patch_of[u] + first, rows:, :] = beside(dq_scr[...].astype(BF16))

    @pl.when(step == total)
    def _():
        for b in range(blocks):
            out_ref[b, :rows, :] = acc[b].astype(BF16)


def project_kernel(a_ref, g_ref, w_ref, out_ref, term_ref):
    left = jnp.concatenate([a_ref[h, :, : a_ref.shape[2] // 2] for h in range(HEADS)], axis=1)
    right = jnp.concatenate([a_ref[h, :, a_ref.shape[2] // 2 :] for h in range(HEADS)], axis=1)
    attn = jnp.concatenate([left, right], axis=0)
    out_ref[...] = mm(attn, w_ref[...]).astype(BF16)
    term_ref[...] = lax.dot_general(
        attn, g_ref[...], (((0,), (0,)), ((), ())), preferred_element_type=F32
    ).astype(BF16)


def unpack_kernel(y_ref, dq_ref, dk_ref, dv_ref):
    rows = dq_ref.shape[0]
    half = rows // 2
    width = dq_ref.shape[1] // HEADS
    for h in range(HEADS):
        cols = slice(h * width, (h + 1) * width)
        dk_ref[:, cols] = y_ref[h, :rows, :width]
        dv_ref[:, cols] = y_ref[h, :rows, width:]
        dq_ref[:half, cols] = y_ref[h, rows:, :width]
        dq_ref[half:, cols] = y_ref[h, rows:, width:]


def params():
    return pltpu.CompilerParams(vmem_limit_bytes=VMEM_LIMIT)


def cost(flops, bytes_accessed, exps=0):
    return pl.CostEstimate(flops=flops, bytes_accessed=bytes_accessed, transcendentals=exps)


def body(queries, key_rows, value_rows, w_out, grad_out, neighbours):
    _, rows, model = queries.shape
    width = model // HEADS
    half = rows // 2
    seg = lax.axis_size("seg")
    samples = lax.axis_size("sample")
    groups = seg // HEADS
    split = [[g * HEADS + i for i in range(HEADS)] for g in range(groups)] if groups > 1 else None
    halo = REACH if groups > 1 else 0
    blocks = HEADS + 2 * halo

    def swap(array):
        return lax.all_to_all(array, "seg", 0, 0, axis_index_groups=split)

    def shifted(array, by):
        pairs = [(s, s + by) for s in range(seg) if 0 <= s + by < seg]
        return lax.ppermute(array, "seg", pairs)

    packed, packed_d = pl.pallas_call(
        pack_kernel,
        in_specs=[pl.BlockSpec(memory_space=pltpu.SMEM)]
        + [pl.BlockSpec(memory_space=pltpu.VMEM)] * 5,
        out_shape=[
            jax.ShapeDtypeStruct((HEADS, rows + half + 16, 2 * width), BF16),
            jax.ShapeDtypeStruct((HEADS, half, 2 * width), BF16),
        ],
        compiler_params=params(),
        cost_estimate=cost(2 * rows * model * model, 10 * rows * model),
        name="pack",
    )(neighbours[0], queries[0], key_rows[0], value_rows[0], grad_out[0], w_out)
    x = swap(packed)
    near = x[:, rows + half : rows + half + NBR, 0].astype(jnp.int32)
    total = HEADS + jnp.sum((near != REACH).astype(jnp.int32))
    near = jnp.concatenate([near, jnp.broadcast_to(total, (HEADS, 1))], axis=1)
    x, near, packed_d = lax.optimization_barrier((x, near, packed_d))
    d = swap(packed_d)
    if halo:
        x = jnp.concatenate([shifted(x[-halo:], HEADS), x, shifted(x[:halo], -HEADS)], axis=0)

    ones = 16
    units = HEADS * (NBR + 1)
    whole = lambda *shape: pl.BlockSpec(shape, lambda t, near: (0,) * len(shape))
    unit = pl.BlockSpec(
        (1, rows, rows), lambda t, near: (jnp.clip(t - 1, 0, near[0, NBR] - 1), 0, 0)
    )
    lists = [pltpu.SMEM((units + 8,), jnp.int32)] * 2
    attn_out, attn_turned, stats, tops, probs = pl.pallas_call(
        functools.partial(forward_kernel, halo),
        grid_spec=pltpu.PrefetchScalarGridSpec(
            num_scalar_prefetch=1,
            grid=(units + 1,),
            in_specs=[whole(*x.shape)],
            out_specs=[
                whole(HEADS, half, 2 * width),
                whole(HEADS, width, rows),
                whole(HEADS, 2, rows),
                whole(units, 1, rows),
                unit,
            ],
            scratch_shapes=[
                pltpu.VMEM((rows, rows), F32),
                pltpu.VMEM((rows, rows), F32),
                pltpu.VMEM((1, rows), F32),
                pltpu.VMEM((width + ones, rows), F32),
                pltpu.VMEM((blocks, width + ones, rows), BF16),
                pltpu.VMEM((HEADS, 2 * width, rows), BF16),
            ]
            + lists,
        ),
        out_shape=[
            jax.ShapeDtypeStruct((HEADS, half, 2 * width), BF16),
            jax.ShapeDtypeStruct((HEADS, width, rows), BF16),
            jax.ShapeDtypeStruct((HEADS, 2, rows), F32),
            jax.ShapeDtypeStruct((units, 1, rows), F32),
            jax.ShapeDtypeStruct((units, rows, rows), BF16),
        ],
        compiler_params=params(),
        cost_estimate=cost(units * rows * rows * 512, 20 * 2**20, units * rows * rows),
        name="forward",
    )(near, x)
    attn_home = swap(attn_out)

    grads = pl.pallas_call(
        functools.partial(backward_kernel, halo),
        grid_spec=pltpu.PrefetchScalarGridSpec(
            num_scalar_prefetch=1,
            grid=(units + 1,),
            in_specs=[
                whole(*x.shape),
                whole(HEADS, half, 2 * width),
                whole(HEADS, width, rows),
                whole(HEADS, 2, rows),
                whole(units, 1, rows),
                unit,
            ],
            out_specs=whole(blocks, rows + half, 2 * width),
            scratch_shapes=[
                pltpu.VMEM((blocks, rows, 2 * width), F32),
                pltpu.VMEM((rows, rows), F32),
                pltpu.VMEM((rows, rows), F32),
                pltpu.VMEM((rows, 2 * width), BF16),
                pltpu.VMEM((rows, 2 * width), BF16),
                pltpu.VMEM((1, rows), F32),
                pltpu.VMEM((1, rows), F32),
                pltpu.VMEM((width, rows), F32),
                pltpu.VMEM((blocks, width, rows), BF16),
                pltpu.VMEM((HEADS, rows, 2 * width), BF16),
                pltpu.VMEM((HEADS, width, rows), F32),
                pltpu.VMEM((HEADS, 1, rows), F32),
            ]
            + lists,
        ),
        out_shape=jax.ShapeDtypeStruct((blocks, rows + half, 2 * width), BF16),
        compiler_params=params(),
        cost_estimate=cost(units * rows * rows * 1024, 20 * 2**20),
        name="backward",
    )(near, x, d, attn_turned, stats, tops, probs)
    grads, attn_home = lax.optimization_barrier((grads, attn_home))
    if halo:
        kv_terms = grads[:, :rows].astype(F32)
        inner = kv_terms[halo:-halo]
        inner = inner.at[-halo:].add(shifted(grads[:halo, :rows], -HEADS).astype(F32))
        inner = inner.at[:halo].add(shifted(grads[-halo:, :rows], HEADS).astype(F32))
        grads = jnp.concatenate([inner.astype(BF16), grads[halo:-halo, rows:]], axis=1)
    grads_home = swap(grads)

    attended, w_term = pl.pallas_call(
        project_kernel,
        out_shape=[
            jax.ShapeDtypeStruct((rows, model), BF16),
            jax.ShapeDtypeStruct((model, model), BF16),
        ],
        compiler_params=params(),
        cost_estimate=cost(4 * rows * model * model, 10 * rows * model),
        name="project",
    )(attn_home, grad_out[0], w_out)
    part = model // samples
    piece = part // seg
    w_part = lax.all_to_all(w_term.reshape(samples, part, model), "sample", 0, 0)
    w_part = jnp.sum(w_part.astype(F32), axis=0).astype(BF16)
    w_piece = lax.all_to_all(w_part.reshape(seg, piece, model), "seg", 0, 0)
    grad_scale = 1.0 / math.sqrt(samples * rows * seg)
    w_piece = (jnp.sum(w_piece.astype(F32), axis=0) * grad_scale).astype(BF16)
    w_part = lax.all_to_all(jnp.broadcast_to(w_piece, (seg, piece, model)), "seg", 0, 0)
    w_part = w_part.reshape(part, model)
    w_all = lax.all_to_all(jnp.broadcast_to(w_part, (samples, part, model)), "sample", 0, 0)
    grad_w_out = w_all.reshape(model, model).astype(F32)

    grad_q, grad_k, grad_v = pl.pallas_call(
        unpack_kernel,
        out_shape=[jax.ShapeDtypeStruct((rows, model), BF16)] * 3,
        compiler_params=params(),
        cost_estimate=cost(0, 12 * rows * model),
        name="unpack",
    )(grads_home)
    return attended[None], grad_q[None], grad_k[None], grad_v[None], grad_w_out


def solution(mesh):
    rows = P("sample", "seg", None)
    return jax.shard_map(
        body,
        mesh=mesh,
        in_specs=(rows, rows, rows, P(), rows, rows),
        out_specs=(rows, rows, rows, rows, P()),
        check_vma=False,
    )
```

time: 213 us -> 207 us (0.972)
  blocking collectives: 105 us -> 92.1 us
  Pallas kernels: 49.4 us -> 58.3 us
    all_gather x1 -> x0, blocking collectives: 49.5 us -> none  [body(): listed = lax.all_gather(neighbours[0, 0], 'seg', axis_index_groups=split)]
    all_to_all x1, blocking collectives: 22.9 us -> 45.7 us  [swap(): return lax.all_to_all(array, 'seg', 0, 0, axis_index_groups=split)]
    all_to_all x0 -> x1, blocking collectives: none -> 11.2 us  [body(): lax.all_to_all(jnp.broadcast_to(w_part, (samples, part, model)), 'sample'...]
    pallas_call x1, Pallas kernels: 22.5 us -> 28.5 us  [body(): pl.pallas_call(functools.partial(backward_kernel, halo), grid_spec=pltpu....]
    all_to_all x1 -> x0, starting transfers between devices: 3.47 us -> none  [body(): lax.all_to_all(jnp.broadcast_to(w_part, (samples, part, model)), 'sample'...]
    pallas_call x1, Pallas kernels: 16.9 us -> 19.9 us  [body(): pl.pallas_call(functools.partial(forward_kernel, halo), grid_spec=pltpu.P...]
    all_to_all x1, blocking collectives: 10.8 us -> 13.1 us  [body(): w_piece = lax.all_to_all(w_part.reshape(seg, piece, model), 'seg', 0, 0)]
    all_to_all x2 -> x3, starting transfers between devices: 11 us -> 13 us  [swap(): return lax.all_to_all(array, 'seg', 0, 0, axis_index_groups=split)]
  transfers between devices with their start and end apart: 3 -> 3, of which waited for: 1 -> 1; matrix products, arithmetic and copies ran while one was open for 1% -> 1% of each run, Pallas kernels for 11% -> 24%
where the time goes in v2:
time: 207 us; the launch traced here: 205 us
  blocking collectives  92.1 us (44%)
  Pallas kernels  58.3 us (28%)
  waiting for transfers between devices  35.7 us (17%)
  starting transfers between devices  13 us (6%)
  local copies, waits for them, and re-layouts  2.78 us (1%)
  other arithmetic  2.07 us (1%)
    all_to_all x1, blocking collectives, swap(): return lax.all_to_all(array, 'seg', 0, 0, axis_index_groups=split)  45.7 us
    all_to_all x3, waiting for transfers between devices, swap(): return lax.all_to_all(array, 'seg', 0, 0, axis_index_groups=split)  35.7 us
    pallas_call x1, Pallas kernels, body(): pl.pallas_call(functools.partial(backward_kernel, halo), grid_spec=pltpu....  28.5 us
    pallas_call x1, Pallas kernels, body(): pl.pallas_call(functools.partial(forward_kernel, halo), grid_spec=pltpu.P...  19.9 us
    all_to_all x1, blocking collectives, body(): w_piece = lax.all_to_all(w_part.reshape(seg, piece, model), 'seg', 0, 0)  13.1 us
    all_to_all x3, starting transfers between devices, swap(): return lax.all_to_all(array, 'seg', 0, 0, axis_index_groups=split)  13 us
    all_to_all x1, blocking collectives, body(): lax.all_to_all(w_term.reshape(samples, part, model), 'sample', 0, 0)  12.3 us
    all_to_all x1, blocking collectives, body(): lax.all_to_all(jnp.broadcast_to(w_part, (samples, part, model)), 'sample'...  11.2 us
  transfers between devices with their start and end apart: 3, of which 1 were waited for; matrix products, arithmetic and copies ran while one was open for 1% of the time, Pallas kernels for 24%

profile of v2, /device:TPU:0, one launch (start us, length us, event | category | flops | bytes accessed | tf_op | source)
XLA Modules:
  0.0 205.4 jit_solution(12411761295115576919)
XLA Ops:
  0.6 3.6 %pack.1 = (bf16[8,784,128]{2,1,0:T(8,128)(2,1)}, bf16[8,256,128]{2,1,0:T(8,128)(2,1)}) custom-call(s32[1,3]{1,0:T(1,128)} %bitcast.26, bf16[512,512]{1,0:T(8,128)(2,1)} %bitcast.20, bf16[512,512]{1,0:T(8,128)(2,1)} %bitcast.21, bf16[512,512]{1,0:T(8,128)(2,1)} %bitcast.22, bf16[512,512]{1,0:T(8,128)(2,1)} %bitcast.23, bf16[512,512]{1,0:T(8,128)(2,1)} %w_ref.3), custom_call_target="tpu_custom_call" | custom-call | flops 268435456 | bytes 2621440 | tf_op jit(solution)/shard_map/pack/pallas_call | solution.py:257
  4.2 45.7 %all_to_all.40.x_ref = bf16[8,784,128]{2,1,0:T(8,128)(2,1)S(1)} all-to-all(bf16[8,784,128]{2,1,0:T(8,128)(2,1)} %get-tuple-element.22), channel_id=1, replica_groups=mesh['seg'=8,'sample'=4] {'seg'}, dimensions={0} | all-to-all | bytes 3211264 | tf_op jit(solution)/shard_map/all_to_all | solution.py:251
  49.9 0.0 copy-start.1
  49.9 0.1 copy.15
  50.1 0.8 convert_reduce_fusion.1
  50.9 0.1 copy.16
  51.6 0.6 concatenate.3.near_ref
  52.2 3.5 %all-to-all-start.1 = ((bf16[8,256,128]{2,1,0:T(8,128)(2,1)}), bf16[8,256,128]{2,1,0:T(8,128)(2,1)S(1)}, u32[]{:S(2)}, u32[]{:S(2)}) async-start(bf16[8,256,128]{2,1,0:T(8,128)(2,1)} %get-tuple-element.26), calls=%async_computation.1 | async-start | bytes 1048576 | tf_op jit(solution)/shard_map/all_to_all | solution.py:251
  55.7 0.0 copy-done.1
  55.7 19.9 %forward.1 = (bf16[8,256,128]{2,1,0:T(8,128)(2,1)}, bf16[8,64,512]{2,1,0:T(8,128)(2,1)}, f32[8,2,512]{2,1,0:T(2,128)}, f32[32,1,512]{2,1,0:T(1,128)}, bf16[32,512,512]{2,1,0:T(8,128)(2,1)}) custom-call(s32[8,4]{1,0:T(8,128)} %concatenate.3.near_ref, bf16[8,784,128]{2,1,0:T(8,128)(2,1)} %copy-done.1), custom_call_target="tpu_custom_call" | custom-call | flops 4294967296 | bytes 20971520 | tf_op jit(solution)/shard_map/forward/pallas_call | solution.py:285
  75.7 0.0 all-to-all-done.1.d_ref
  75.7 0.0 copy-start.2
  75.7 5.9 %all-to-all-start.2 = ((bf16[8,256,128]{2,1,0:T(8,128)(2,1)}), bf16[8,256,128]{2,1,0:T(8,128)(2,1)S(1)}, u32[]{:S(2)}, u32[]{:S(2)}) async-start(bf16[8,256,128]{2,1,0:T(8,128)(2,1)} %get-tuple-element.31), calls=%async_computation.2 | async-start | bytes 1048576 | tf_op jit(solution)/shard_map/all_to_all | solution.py:251
  81.6 0.0 copy-done.2
  81.6 28.5 %backward.1 = bf16[8,768,128]{2,1,0:T(8,128)(2,1)} custom-call(s32[8,4]{1,0:T(8,128)} %concatenate.3.near_ref, bf16[8,784,128]{2,1,0:T(8,128)(2,1)} %copy-done.1, bf16[8,256,128]{2,1,0:T(8,128)(2,1)} %copy-done.2, bf16[8,64,512]{2,1,0:T(8,128)(2,1)} %get-tuple-element.27.turned_ref, f32[8,2,512]{2,1,0:T(2,128)} %get-tuple-element.28.stat_ref, ...), custom_call_target="tpu_custom_call" | custom-call | flops 8589934592 | bytes 20971520 | tf_op jit(solution)/shard_map/backward/pallas_call | solution.py:321
  110.1 0.0 all-to-all-done.2.a_ref
  110.1 0.0 copy-start.3
  110.1 0.8 copy-done.3
  110.9 2.9 %project.1 = (bf16[512,512]{1,0:T(8,128)(2,1)}, bf16[512,512]{1,0:T(8,128)(2,1)}) custom-call(bf16[8,256,128]{2,1,0:T(8,128)(2,1)} %copy-done.3, bf16[512,512]{1,0:T(8,128)(2,1)} %bitcast.24, bf16[512,512]{1,0:T(8,128)(2,1)} %w_ref.3), custom_call_target="tpu_custom_call" | custom-call | flops 536870912 | bytes 2621440 | tf_op jit(solution)/shard_map/project/pallas_call | solution.py:365
  113.8 12.3 %all_to_all.41 = bf16[4,128,512]{2,1,0:T(8,128)(2,1)S(1)} all-to-all(bf16[4,128,512]{2,1,0:T(8,128)(2,1)} %bitcast.18), channel_id=1, replica_groups=mesh['seg'=8,'sample'=4] {'sample'}, dimensions={0} | all-to-all | bytes 1048576 | tf_op jit(solution)/shard_map/all_to_all | solution.py:377
  126.1 0.1 reduce_sum.31
  126.2 13.1 %all_to_all.42 = bf16[8,16,512]{2,1,0:T(8,128)(2,1)S(1)} all-to-all(bf16[8,16,512]{2,1,0:T(8,128)(2,1)S(1)} %bitcast.19), channel_id=1, replica_groups=mesh['seg'=8,'sample'=4] {'seg'}, dimensions={0} | all-to-all | bytes 262144 | tf_op jit(solution)/shard_map/all_to_all | solution.py:379
  139.4 9.7 %all_to_all.43 = bf16[8,16,512]{2,1,0:T(8,128)(2,1)S(1)} all-to-all(bf16[8,16,512]{2,1,0:T(8,128)(2,1)S(1)} %broadcast_in_dim.23), channel_id=1, replica_groups=mesh['seg'=8,'sample'=4] {'seg'}, dimensions={0} | all-to-all | bytes 262144 | tf_op jit(solution)/shard_map/all_to_all | solution.py:382
  149.1 11.2 %all_to_all.44 = bf16[4,128,512]{2,1,0:T(8,128)(2,1)S(1)} all-to-all(bf16[4,128,512]{2,1,0:T(8,128)(2,1)S(1)} %broadcast_in_dim.24), channel_id=1, replica_groups=mesh['seg'=8,'sample'=4] {'sample'}, dimensions={0} | all-to-all | bytes 1048576 | tf_op jit(solution)/shard_map/all_to_all | solution.py:384
  160.4 3.6 %all-to-all-start.3 = ((bf16[8,768,128]{2,1,0:T(8,128)(2,1)}), bf16[8,768,128]{2,1,0:T(8,128)(2,1)S(1)}, u32[]{:S(2)}, u32[]{:S(2)}) async-start(bf16[8,768,128]{2,1,0:T(8,128)(2,1)} %backward.1), calls=%async_computation.3 | async-start | bytes 3145728 | tf_op jit(solution)/shard_map/all_to_all | solution.py:251
  164.0 1.1 bitcast_convert_fusion
  165.1 35.7 %all-to-all-done.3.y_ref = bf16[8,768,128]{2,1,0:T(8,128)(2,1)S(1)} async-done(((bf16[8,768,128]{2,1,0:T(8,128)(2,1)}), bf16[8,768,128]{2,1,0:T(8,128)(2,1)S(1)}, u32[]{:S(2)}, u32[]{:S(2)}) %all-to-all-start.3) | async-done | bytes 1572896 | tf_op jit(solution)/shard_map/all_to_all | solution.py:251
  200.8 0.0 copy-start
  200.8 1.2 copy-done
  202.0 3.4 %unpack.1 = (bf16[512,512]{1,0:T(8,128)(2,1)}, bf16[512,512]{1,0:T(8,128)(2,1)}, bf16[512,512]{1,0:T(8,128)(2,1)}) custom-call(bf16[8,768,128]{2,1,0:T(8,128)(2,1)} %copy-done), custom_call_target="tpu_custom_call" | custom-call | bytes 3145728 | tf_op jit(solution)/shard_map/unpack/pallas_call | solution.py:387
  (5 shorter events, 0.1 us)
Async XLA Ops:
  49.9 5.8 %copy-start.1 = (bf16[8,784,128]{2,1,0:T(8,128)(2,1)}, bf16[8,784,128]{2,1,0:T(8,128)(2,1)S(1)}, u32[]{:S(2)}) copy-start(bf16[8,784,128]{2,1,0:T(8,128)(2,1)S(1)} %all_to_all.40.x_ref) | copy-start | bytes 4816900
  52.2 23.5 %all-to-all-start.1 = ((bf16[8,256,128]{2,1,0:T(8,128)(2,1)}), bf16[8,256,128]{2,1,0:T(8,128)(2,1)S(1)}, u32[]{:S(2)}, u32[]{:S(2)}) async-start(bf16[8,256,128]{2,1,0:T(8,128)(2,1)} %get-tuple-element.26), calls=%async_computation.1 | async-start | bytes 1048576 | tf_op jit(solution)/shard_map/all_to_all | solution.py:251
  75.7 6.0 %copy-start.2 = (bf16[8,256,128]{2,1,0:T(8,128)(2,1)}, bf16[8,256,128]{2,1,0:T(8,128)(2,1)S(1)}, u32[]{:S(2)}) copy-start(bf16[8,256,128]{2,1,0:T(8,128)(2,1)S(1)} %all-to-all-done.1.d_ref) | copy-start | bytes 1572868
  75.7 34.4 %all-to-all-start.2 = ((bf16[8,256,128]{2,1,0:T(8,128)(2,1)}), bf16[8,256,128]{2,1,0:T(8,128)(2,1)S(1)}, u32[]{:S(2)}, u32[]{:S(2)}) async-start(bf16[8,256,128]{2,1,0:T(8,128)(2,1)} %get-tuple-element.31), calls=%async_computation.2 | async-start | bytes 1048576 | tf_op jit(solution)/shard_map/all_to_all | solution.py:251
  110.1 0.8 copy-start.3
  160.4 40.4 %all-to-all-start.3 = ((bf16[8,768,128]{2,1,0:T(8,128)(2,1)}), bf16[8,768,128]{2,1,0:T(8,128)(2,1)S(1)}, u32[]{:S(2)}, u32[]{:S(2)}) async-start(bf16[8,768,128]{2,1,0:T(8,128)(2,1)} %backward.1), calls=%async_computation.3 | async-start | bytes 3145728 | tf_op jit(solution)/shard_map/all_to_all | solution.py:251
  200.8 1.2 copy-start

commit v3 on v2

v3 whole, which is shorter than its diff:
```python
import functools
import math

import jax
import jax.numpy as jnp
from jax import lax
from jax.experimental import pallas as pl
from jax.experimental.pallas import tpu as pltpu
from jax.sharding import PartitionSpec as P

HEADS = 8
NBR = 3
REACH = 3
F32 = jnp.float32
BF16 = jnp.bfloat16


def mm(a, b):
    return lax.dot_general(a, b, (((1,), (0,)), ((), ())), preferred_element_type=F32)


def halves(block):
    turned = block.T
    width = turned.shape[0] // 2
    return jnp.concatenate([turned[:width], turned[width:]], axis=1)


def beside(turned):
    rows = turned.shape[1]
    return jnp.concatenate([turned[:, : rows // 2], turned[:, rows // 2 :]], axis=0).T


def pack_kernel(near_ref, *refs):
    sources, (out_ref, d_ref), held, arrived = refs[:5], refs[5:7], refs[7:12], refs[12]
    copies = [
        pltpu.make_async_copy(source, target, arrived.at[i])
        for i, (source, target) in enumerate(zip(sources, held))
    ]
    for copy in copies:
        copy.start()
    for copy in copies:
        copy.wait()
    q_ref, k_ref, v_ref, g_ref, w_ref = held
    rows = q_ref.shape[0]
    width = q_ref.shape[1] // HEADS
    half = rows // 2
    here = lax.axis_index("seg")
    line = lax.broadcasted_iota(jnp.int32, (16, 2 * width), 0)
    offsets = jnp.zeros((16, 2 * width), F32)
    for e in range(NBR):
        offsets = jnp.where(line == e, (near_ref[0, e] - here + REACH).astype(F32), offsets)
    for h in range(HEADS):
        cols = slice(h * width, (h + 1) * width)
        out_ref[h, :rows, :] = jnp.concatenate([k_ref[:, cols], v_ref[:, cols]], axis=1)
        out_ref[h, rows : rows + half, :] = jnp.concatenate(
            [q_ref[:half, cols], q_ref[half:, cols]], axis=1
        )
        out_ref[h, rows + half :, :] = offsets.astype(BF16)
    d_attn = lax.dot_general(
        g_ref[...], w_ref[...], (((1,), (1,)), ((), ())), preferred_element_type=F32
    ).astype(BF16)
    for h in range(HEADS):
        cols = slice(h * width, (h + 1) * width)
        d_ref[h] = jnp.concatenate([d_attn[:half, cols], d_attn[half:, cols]], axis=1)


def list_units(first, near_ref, patch_of, block_of):
    count = jnp.int32(0)
    for p in range(HEADS):
        patch_of[count] = p
        block_of[count] = p + first
        count = count + 1
        for e in range(NBR):
            offset = near_ref[p, e] - REACH
            patch_of[count] = p
            block_of[count] = p + first + offset
            count = count + jnp.where(offset != 0, 1, 0)
    patch_of[count] = -1
    return count


def is_first(patch_of, u):
    return jnp.logical_or(u == 0, patch_of[jnp.maximum(u - 1, 0)] != patch_of[u])


def in_turn(total, patch_of, enter, leave, end):
    def both(u, slot):
        leave(u, slot, lambda: enter(u + 1, 1 - slot))
        pl.when(patch_of[u + 1] != patch_of[u])(lambda: end(u))

    def two(i, carry):
        both(2 * i, 0)
        both(2 * i + 1, 1)
        return carry

    enter(jnp.int32(0), 0)
    lax.fori_loop(0, (total - 1) // 2, two, 0)
    pl.when(total % 2 == 0)(lambda: both(total - 2, 0))
    for slot in range(2):

        @pl.when((total - 1) % 2 == slot)
        def _():
            leave(total - 1, slot, lambda: None)

    end(total - 1)


def forward_kernel(first, near_ref, x_ref, attn_ref, turned_ref, lse_ref, s0, s1, top_scr, m_scr, o_scr, v_scr, q_scr, patch_of, block_of):
    blocks = x_ref.shape[0]
    rows, width = s0.shape[0], x_ref.shape[2] // 2
    half = rows // 2
    scores = (s0, s1)
    total = list_units(first, near_ref, patch_of, block_of)
    o_scr[...] = jnp.zeros_like(o_scr)
    for b in range(blocks):
        v_scr[b, :width, :] = x_ref[b, :rows, :].T[width:]
        v_scr[b, width:, :] = jnp.ones((v_scr.shape[1] - width, rows), BF16)
    for p in range(HEADS):
        turned = halves(x_ref[p + first, rows : rows + half, :])
        q_scr[p, :width, :] = turned * BF16(1.0 / math.sqrt(width))
        q_scr[p, width:, :] = jnp.zeros_like(turned)

    def enter(u, slot):
        s = mm(x_ref[block_of[u], :rows, :], q_scr[patch_of[u]])
        scores[slot][...] = s
        top = jnp.max(s, axis=0, keepdims=True)
        top = jnp.where(is_first(patch_of, u), top, jnp.maximum(top, m_scr[...]))
        m_scr[...] = top
        top_scr[u] = top

    def leave(u, slot, then):
        m = top_scr[u]
        p = jnp.exp(scores[slot][...] - m).astype(BF16)
        keep = jnp.exp(top_scr[jnp.maximum(u - 1, 0)] - m)
        keep = jnp.where(is_first(patch_of, u), 0.0, keep)
        then()
        o_scr[...] = o_scr[...] * keep + mm(v_scr[block_of[u]], p)

    def end(u):
        p = patch_of[u]
        total_p = o_scr[width : width + 1, :]
        attn = (o_scr[:width, :] * (1.0 / total_p)).astype(BF16)
        turned_ref[p] = attn
        lse_ref[p] = top_scr[u] + jnp.log(total_p)
        attn_ref[p] = beside(attn)

    in_turn(total, patch_of, enter, leave, end)


def backward_kernel(first, near_ref, x_ref, d_ref, turned_ref, lse_ref, out_ref, acc, s0, s1, dq_scr, k_scr, back_scr, q_scr, d_scr, delta_scr, patch_of, block_of):
    blocks = x_ref.shape[0]
    rows, width = q_scr.shape[2], x_ref.shape[2] // 2
    half = rows // 2
    scale = 1.0 / math.sqrt(width)
    pairs = (s0, s1)
    total = list_units(first, near_ref, patch_of, block_of)
    acc[...] = jnp.zeros_like(acc)
    dq_scr[...] = jnp.zeros_like(dq_scr)
    for b in range(blocks):
        k_scr[b] = x_ref[b, :rows, :].T[:width]
    blank = jnp.zeros((half, width), BF16)
    for p in range(HEADS):
        q_pair = x_ref[p + first, rows : rows + half, :]
        d_pair = d_ref[p]
        back_scr[p, :half, :] = jnp.concatenate([q_pair[:, :width], blank], axis=1)
        back_scr[p, half:rows, :] = jnp.concatenate([q_pair[:, width:], blank], axis=1)
        back_scr[p, rows : rows + half, :] = jnp.concatenate([blank, d_pair[:, :width]], axis=1)
        back_scr[p, rows + half :, :] = jnp.concatenate([blank, d_pair[:, width:]], axis=1)
        q_turned, d_turned = halves(q_pair), halves(d_pair)
        q_scr[p, :width, :] = q_turned * BF16(scale)
        q_scr[p, width:, :] = jnp.zeros_like(q_turned)
        d_scr[p, :width, :] = jnp.zeros_like(d_turned)
        d_scr[p, width:, :] = d_turned * BF16(scale)
        product = d_turned.astype(F32) * turned_ref[p].astype(F32)
        delta_scr[p] = jnp.sum(product, axis=0, keepdims=True) * scale

    def enter(u, slot):
        keys, p = x_ref[block_of[u], :rows, :], patch_of[u]
        pairs[slot][:, :rows] = mm(keys, q_scr[p])
        pairs[slot][:, rows:] = mm(keys, d_scr[p])

    def leave(u, slot, then):
        b, p = block_of[u], patch_of[u]
        prob = jnp.exp(pairs[slot][:, :rows] - lse_ref[p])
        ds = (prob * (pairs[slot][:, rows:] - delta_scr[p])).astype(BF16)
        then()
        dq = mm(k_scr[b], ds)
        dq_scr[...] = dq + jnp.where(is_first(patch_of, u), 0.0, dq_scr[...])
        acc[b] += mm(jnp.concatenate([ds, prob.astype(BF16)], axis=1), back_scr[p])

    def end(u):
        out_ref[patch_of[u] + first, rows:, :] = beside(dq_scr[...].astype(BF16))

    in_turn(total, patch_of, enter, leave, end)
    for b in range(blocks):
        out_ref[b, :rows, :] = acc[b].astype(BF16)


def project_kernel(a_ref, g_ref, w_ref, out_ref, term_ref):
    left = jnp.concatenate([a_ref[h, :, : a_ref.shape[2] // 2] for h in range(HEADS)], axis=1)
    right = jnp.concatenate([a_ref[h, :, a_ref.shape[2] // 2 :] for h in range(HEADS)], axis=1)
    attn = jnp.concatenate([left, right], axis=0)
    out_ref[...] = mm(attn, w_ref[...]).astype(BF16)
    term_ref[...] = lax.dot_general(
        attn, g_ref[...], (((0,), (0,)), ((), ())), preferred_element_type=F32
    ).astype(BF16)


def unpack_kernel(y_ref, dq_ref, dk_ref, dv_ref):
    rows = dq_ref.shape[0]
    half = rows // 2
    width = dq_ref.shape[1] // HEADS
    for h in range(HEADS):
        cols = slice(h * width, (h + 1) * width)
        dk_ref[:, cols] = y_ref[h, :rows, :width]
        dv_ref[:, cols] = y_ref[h, :rows, width:]
        dq_ref[:half, cols] = y_ref[h, rows:, :width]
        dq_ref[half:, cols] = y_ref[h, rows:, width:]


def params(mib=32):
    return pltpu.CompilerParams(vmem_limit_bytes=mib * 2**20)


def cost(flops, bytes_accessed, exps=0):
    return pl.CostEstimate(flops=flops, bytes_accessed=bytes_accessed, transcendentals=exps)


def forward(near, x, halo):
    blocks, two_width = x.shape[0], x.shape[2]
    width = two_width // 2
    rows = (x.shape[1] - 16) * 2 // 3
    half = rows // 2
    units = HEADS * (NBR + 1)
    ones = 16
    vmem = pl.BlockSpec(memory_space=pltpu.VMEM)
    return pl.pallas_call(
        functools.partial(forward_kernel, halo),
        in_specs=[pl.BlockSpec(memory_space=pltpu.SMEM), vmem],
        out_specs=[vmem] * 3,
        scratch_shapes=[
            pltpu.VMEM((rows, rows), F32),
            pltpu.VMEM((rows, rows), F32),
            pltpu.VMEM((units, 1, rows), F32),
            pltpu.VMEM((1, rows), F32),
            pltpu.VMEM((width + ones, rows), F32),
            pltpu.VMEM((blocks, width + ones, rows), BF16),
            pltpu.VMEM((HEADS, two_width, rows), BF16),
            pltpu.SMEM((units + 8,), jnp.int32),
            pltpu.SMEM((units + 8,), jnp.int32),
        ],
        out_shape=[
            jax.ShapeDtypeStruct((HEADS, half, two_width), BF16),
            jax.ShapeDtypeStruct((HEADS, width, rows), BF16),
            jax.ShapeDtypeStruct((HEADS, 1, rows), F32),
        ],
        compiler_params=params(),
        cost_estimate=cost(units * rows * rows * 512, 4 * 2**20, units * rows * rows),
        name="forward",
    )(near, x)


def backward(near, x, d, turned, lse, halo):
    blocks, two_width = x.shape[0], x.shape[2]
    width = two_width // 2
    rows = (x.shape[1] - 16) * 2 // 3
    half = rows // 2
    units = HEADS * (NBR + 1)
    vmem = pl.BlockSpec(memory_space=pltpu.VMEM)
    return pl.pallas_call(
        functools.partial(backward_kernel, halo),
        in_specs=[pl.BlockSpec(memory_space=pltpu.SMEM)] + [vmem] * 4,
        out_specs=vmem,
        scratch_shapes=[
            pltpu.VMEM((blocks, rows, two_width), F32),
            pltpu.VMEM((rows, 2 * rows), F32),
            pltpu.VMEM((rows, 2 * rows), F32),
            pltpu.VMEM((width, rows), F32),
            pltpu.VMEM((blocks, width, rows), BF16),
            pltpu.VMEM((HEADS, 2 * rows, two_width), BF16),
            pltpu.VMEM((HEADS, two_width, rows), BF16),
            pltpu.VMEM((HEADS, two_width, rows), BF16),
            pltpu.VMEM((HEADS, 1, rows), F32),
            pltpu.SMEM((units + 8,), jnp.int32),
            pltpu.SMEM((units + 8,), jnp.int32),
        ],
        out_shape=jax.ShapeDtypeStruct((blocks, rows + half, two_width), BF16),
        compiler_params=params(),
        cost_estimate=cost(units * rows * rows * 1280, 6 * 2**20, units * rows * rows),
        name="backward",
    )(near, x, d, turned, lse)


def in_hbm(array):
    return pltpu.with_memory_space_constraint(array, pltpu.HBM)


def around(count, by):
    return [(i, (i + by) % count) for i in range(count)]


def exchange(pieces, axis):
    count = pieces.shape[0]
    if count > HEADS:
        return lax.all_to_all(pieces, axis, 0, 0)
    here = lax.axis_index(axis)
    arrived = []
    for by in range(count):
        piece = lax.dynamic_index_in_dim(pieces, (here + by) % count, 0, keepdims=False)
        arrived.append(lax.ppermute(piece, axis, around(count, by)) if by else piece)
    return jnp.stack(arrived)


def gathered(piece, axis):
    count = lax.axis_size(axis)
    if count > HEADS:
        return lax.all_gather(piece, axis)
    here = lax.axis_index(axis)
    arrived = [lax.ppermute(piece, axis, around(count, by)) if by else piece for by in range(count)]
    line = jnp.stack(arrived[::-1] + arrived[::-1])
    return lax.dynamic_slice_in_dim(line, count - 1 - here, count, 0)


def body(queries, key_rows, value_rows, w_out, grad_out, neighbours):
    _, rows, model = queries.shape
    width = model // HEADS
    half = rows // 2
    seg = lax.axis_size("seg")
    samples = lax.axis_size("sample")
    groups = seg // HEADS
    split = [[g * HEADS + i for i in range(HEADS)] for g in range(groups)] if groups > 1 else None
    halo = REACH if groups > 1 else 0
    blocks = HEADS + 2 * halo

    def swap(array):
        return lax.all_to_all(array, "seg", 0, 0, axis_index_groups=split)

    def shifted(array, by):
        pairs = [(s, s + by) for s in range(seg) if 0 <= s + by < seg]
        return lax.ppermute(array, "seg", pairs)

    packed, packed_d = pl.pallas_call(
        pack_kernel,
        in_specs=[pl.BlockSpec(memory_space=pltpu.SMEM)]
        + [pl.BlockSpec(memory_space=pltpu.HBM)] * 5,
        scratch_shapes=[pltpu.VMEM((rows, model), BF16)] * 4
        + [pltpu.VMEM((model, model), BF16), pltpu.SemaphoreType.DMA((5,))],
        out_shape=[
            jax.ShapeDtypeStruct((HEADS, rows + half + 16, 2 * width), BF16),
            jax.ShapeDtypeStruct((HEADS, half, 2 * width), BF16),
        ],
        compiler_params=params(),
        cost_estimate=cost(2 * rows * model * model, 10 * rows * model),
        name="pack",
    )(neighbours[0], *(in_hbm(a) for a in (queries[0], key_rows[0], value_rows[0], grad_out[0], w_out)))
    x = swap(packed)
    near = x[:, rows + half : rows + half + NBR, 0].astype(jnp.int32)
    x, near, packed_d = lax.optimization_barrier((x, near, packed_d))
    d = swap(packed_d)
    if halo:
        x = jnp.concatenate([shifted(x[-halo:], HEADS), x, shifted(x[:halo], -HEADS)], axis=0)

    attn_out, attn_turned, lse = forward(near, x, halo)
    attn_home = swap(attn_out)

    grads = backward(near, x, d, attn_turned, lse, halo)
    grads, attn_home = lax.optimization_barrier((grads, attn_home))
    if halo:
        kv_terms = grads[:, :rows].astype(F32)
        inner = kv_terms[halo:-halo]
        inner = inner.at[-halo:].add(shifted(grads[:halo, :rows], -HEADS).astype(F32))
        inner = inner.at[:halo].add(shifted(grads[-halo:, :rows], HEADS).astype(F32))
        grads = jnp.concatenate([inner.astype(BF16), grads[halo:-halo, rows:]], axis=1)
    grads_home = swap(grads)

    attended, w_term = pl.pallas_call(
        project_kernel,
        out_shape=[
            jax.ShapeDtypeStruct((rows, model), BF16),
            jax.ShapeDtypeStruct((model, model), BF16),
        ],
        compiler_params=params(),
        cost_estimate=cost(4 * rows * model * model, 10 * rows * model),
        name="project",
    )(attn_home, grad_out[0], w_out)
    part = model // samples
    w_part = exchange(w_term.reshape(samples, part, model), "sample")
    w_part = jnp.sum(w_part.astype(F32), axis=0).astype(BF16)
    w_piece = exchange(w_part.reshape(seg, part // seg, model), "seg")
    grad_scale = 1.0 / math.sqrt(samples * rows * seg)
    w_piece = (jnp.sum(w_piece.astype(F32), axis=0) * grad_scale).astype(BF16)
    grad_q, grad_k, grad_v = pl.pallas_call(
        unpack_kernel,
        out_shape=[jax.ShapeDtypeStruct((rows, model), BF16)] * 3,
        compiler_params=params(),
        cost_estimate=cost(0, 12 * rows * model),
        name="unpack",
    )(grads_home)
    w_piece, grad_q = lax.optimization_barrier((w_piece, grad_q))
    w_part = gathered(w_piece, "seg").reshape(part, model)
    grad_w_out = gathered(w_part, "sample").reshape(model, model).astype(F32)
    return attended[None], grad_q[None], grad_k[None], grad_v[None], grad_w_out


def solution(mesh):
    rows = P("sample", "seg", None)
    return jax.shard_map(
        body,
        mesh=mesh,
        in_specs=(rows, rows, rows, P(), rows, rows),
        out_specs=(rows, rows, rows, rows, P()),
        check_vma=False,
    )
```

time: 207 us -> 172 us (0.83)
  blocking collectives: 92.1 us -> 45.5 us
  starting transfers between devices: 13 us -> 44.4 us
  Pallas kernels: 58.3 us -> 41.7 us
    all_to_all x4 -> x0, blocking collectives: 46.4 us -> none  [the longest x1 13.1 us: body(): w_piece = lax.all_to_all(w_part.reshape(seg, piece, model), 'seg', 0, 0)]
    all_to_all x3, waiting for transfers between devices: 35.7 us -> 1.8 us  [swap(): return lax.all_to_all(array, 'seg', 0, 0, axis_index_groups=split)]
    ppermute x0 -> x20, waiting for transfers between devices: none -> 33.6 us  [the longest x10 21.5 us: exchange(): lax.ppermute(piece, axis, around(count, by))]
    ppermute x0 -> x20, starting transfers between devices: none -> 30.7 us  [the longest x10 17.9 us: gathered(): lax.ppermute(piece, axis, around(count, by))]
    pallas_call x2, Pallas kernels: 48.4 us -> 34.8 us  [the longest x1 22.9 us: backward(): pl.pallas_call(functools.partial(backward_kernel, halo), in_specs=[pl.Blo...]
  transfers between devices with their start and end apart: 3 -> 23, of which waited for: 1 -> 8; matrix products, arithmetic and copies ran while one was open for 1% -> 0% of each run, Pallas kernels for 24% -> 21%
where the time goes in v3:
time: 172 us; the launch traced here: 171 us
  blocking collectives  45.5 us (26%)
  starting transfers between devices  44.4 us (26%)
  Pallas kernels  41.7 us (24%)
  waiting for transfers between devices  35.4 us (21%)
  local copies, waits for them, and re-layouts  2.15 us (1%)
    all_to_all x1, blocking collectives, swap(): return lax.all_to_all(array, 'seg', 0, 0, axis_index_groups=split)  45.5 us
    pallas_call x1, Pallas kernels, backward(): pl.pallas_call(functools.partial(backward_kernel, halo), in_specs=[pl.Blo...  22.9 us
    ppermute x10, waiting for transfers between devices, exchange(): lax.ppermute(piece, axis, around(count, by))  21.5 us
    ppermute x10, starting transfers between devices, gathered(): lax.ppermute(piece, axis, around(count, by))  17.9 us
    all_to_all x3, starting transfers between devices, swap(): return lax.all_to_all(array, 'seg', 0, 0, axis_index_groups=split)  13.8 us
    ppermute x10, starting transfers between devices, exchange(): lax.ppermute(piece, axis, around(count, by))  12.8 us
    ppermute x10, waiting for transfers between devices, gathered(): lax.ppermute(piece, axis, around(count, by))  12.1 us
    pallas_call x1, Pallas kernels, forward(): pl.pallas_call(functools.partial(forward_kernel, halo), in_specs=[pl.Bloc...  11.9 us
  transfers between devices with their start and end apart: 23, of which 8 were waited for; matrix products, arithmetic and copies ran while one was open for 0% of the time, Pallas kernels for 21%

profile of v3, /device:TPU:0, one launch (start us, length us, event | category | flops | bytes accessed | tf_op | source)
XLA Modules:
  0.0 171.4 jit_solution(12835867585965340206)
XLA Ops:
  0.6 0.6 copy-done.2
  1.3 3.7 %pack.1 = (bf16[8,784,128]{2,1,0:T(8,128)(2,1)S(1)}, bf16[8,256,128]{2,1,0:T(8,128)(2,1)}) custom-call(s32[1,3]{1,0:T(1,128)S(1)} %bitcast.98, bf16[512,512]{1,0:T(8,128)(2,1)} %bitcast.105, bf16[512,512]{1,0:T(8,128)(2,1)} %bitcast.106, bf16[512,512]{1,0:T(8,128)(2,1)} %bitcast.107, bf16[512,512]{1,0:T(8,128)(2,1)} %bitcast.96, bf16[512,512]{1,0:T(8,128)(2,1)} %w_ref.1), custom_call_target="tpu_custom_call" | custom-call | flops 268435456 | bytes 2621440 | tf_op jit(solution)/shard_map/pack/pallas_call | solution.py:342
  5.0 45.5 %all_to_all.20.x_ref = bf16[8,784,128]{2,1,0:T(8,128)(2,1)S(1)} all-to-all(bf16[8,784,128]{2,1,0:T(8,128)(2,1)S(1)} %get-tuple-element.22), channel_id=1, replica_groups=mesh['seg'=8,'sample'=4] {'seg'}, dimensions={0} | all-to-all | bytes 3211264 | tf_op jit(solution)/shard_map/all_to_all | solution.py:336
  50.5 0.1 copy.14
  50.6 3.5 %all-to-all-start.1 = ((bf16[8,256,128]{2,1,0:T(8,128)(2,1)}), bf16[8,256,128]{2,1,0:T(8,128)(2,1)S(1)}, u32[]{:S(2)}, u32[]{:S(2)}) async-start(bf16[8,256,128]{2,1,0:T(8,128)(2,1)} %get-tuple-element.26), calls=%async_computation.1 | async-start | bytes 1048576 | tf_op jit(solution)/shard_map/all_to_all | solution.py:336
  54.1 0.1 copy.16.near_ref
  54.2 11.9 %forward.1 = (bf16[8,256,128]{2,1,0:T(8,128)(2,1)}, bf16[8,64,512]{2,1,0:T(8,128)(2,1)S(1)}, f32[8,1,512]{2,1,0:T(1,128)S(1)}) custom-call(s32[8,3]{1,0:T(8,128)S(1)} %copy.16.near_ref, bf16[8,784,128]{2,1,0:T(8,128)(2,1)S(1)} %all_to_all.20.x_ref), custom_call_target="tpu_custom_call" | custom-call | flops 4294967296 | bytes 4194304 | tf_op jit(solution)/shard_map/forward/pallas_call | solution.py:237
  66.1 1.8 %all-to-all-done.1.d_ref = bf16[8,256,128]{2,1,0:T(8,128)(2,1)S(1)} async-done(((bf16[8,256,128]{2,1,0:T(8,128)(2,1)}), bf16[8,256,128]{2,1,0:T(8,128)(2,1)S(1)}, u32[]{:S(2)}, u32[]{:S(2)}) %all-to-all-start.1) | async-done | bytes 524320 | tf_op jit(solution)/shard_map/all_to_all | solution.py:336
  67.9 4.1 %all-to-all-start.2 = ((bf16[8,256,128]{2,1,0:T(8,128)(2,1)}), bf16[8,256,128]{2,1,0:T(8,128)(2,1)S(1)}, u32[]{:S(2)}, u32[]{:S(2)}) async-start(bf16[8,256,128]{2,1,0:T(8,128)(2,1)} %get-tuple-element.29), calls=%async_computation.2 | async-start | bytes 1048576 | tf_op jit(solution)/shard_map/all_to_all | solution.py:336
  72.0 22.9 %backward.1 = bf16[8,768,128]{2,1,0:T(8,128)(2,1)} custom-call(s32[8,3]{1,0:T(8,128)S(1)} %copy.16.near_ref, bf16[8,784,128]{2,1,0:T(8,128)(2,1)S(1)} %all_to_all.20.x_ref, bf16[8,256,128]{2,1,0:T(8,128)(2,1)S(1)} %all-to-all-done.1.d_ref, bf16[8,64,512]{2,1,0:T(8,128)(2,1)S(1)} %get-tuple-element.27.turned_ref, f32[8,1,512]{2,1,0:T(1,128)S(1)} %get-tuple-element.28.lse_ref), custom_call_target="tpu_custom_call" | custom-call | flops 10737418240 | bytes 6291456 | tf_op jit(solution)/shard_map/backward/pallas_call | solution.py:270
  94.9 0.0 all-to-all-done.2.a_ref
  94.9 6.1 %all-to-all-start.3 = ((bf16[8,768,128]{2,1,0:T(8,128)(2,1)}), bf16[8,768,128]{2,1,0:T(8,128)(2,1)S(1)}, u32[]{:S(2)}, u32[]{:S(2)}) async-start(bf16[8,768,128]{2,1,0:T(8,128)(2,1)} %backward.1), calls=%async_computation.3 | async-start | bytes 3145728 | tf_op jit(solution)/shard_map/all_to_all | solution.py:336
  101.1 0.0 copy-start.1
  101.1 1.0 copy-done.1
  102.1 1.3 project.1
  103.4 1.3 collective-permute-start.2
  104.7 1.5 collective-permute-start.1
  106.3 0.2 collective-permute-start
  106.4 1.2 collective-permute-done.2
  107.6 5.6 %collective-permute-done.1 = bf16[128,512]{1,0:T(8,128)(2,1)S(1)} collective-permute-done((bf16[128,512]{1,0:T(8,128)(2,1)S(1)}, bf16[128,512]{1,0:T(8,128)(2,1)S(1)}, u32[]{:S(2)}, u32[]{:S(2)}) %collective-permute-start.1) | collective-permute-done | bytes 131104 | tf_op jit(solution)/shard_map/ppermute | solution.py:310
  113.2 0.0 collective-permute-done
  113.2 2.1 %collective-permute-start.3 = (bf16[16,512]{1,0:T(8,128)(2,1)S(1)}, bf16[16,512]{1,0:T(8,128)(2,1)S(1)}, u32[]{:S(2)}, u32[]{:S(2)}) collective-permute-start(bf16[16,512]{1,0:T(8,128)(2,1)S(1)} %get-tuple-element.48), channel_id=1, source_target_pairs={{0,4},{4,8},{8,12},{12,16},{16,20},{20,24},{24,28},{28,0},{1,5},{5... | collective-permute-start | bytes 49160 | tf_op jit(solution)/shard_map/ppermute | solution.py:310
  115.3 1.5 collective-permute-start.4
  116.8 2.4 %collective-permute-start.5 = (bf16[16,512]{1,0:T(8,128)(2,1)S(1)}, bf16[16,512]{1,0:T(8,128)(2,1)S(1)}, u32[]{:S(2)}, u32[]{:S(2)}) collective-permute-start(bf16[16,512]{1,0:T(8,128)(2,1)S(1)} %get-tuple-element.46), channel_id=1, source_target_pairs={{0,12},{4,16},{8,20},{12,24},{16,28},{20,0},{24,4},{28,8},{1,13},{... | collective-permute-start | bytes 49160 | tf_op jit(solution)/shard_map/ppermute | solution.py:310
  119.1 1.5 collective-permute-start.6
  120.6 2.4 %collective-permute-start.7 = (bf16[16,512]{1,0:T(8,128)(2,1)S(1)}, bf16[16,512]{1,0:T(8,128)(2,1)S(1)}, u32[]{:S(2)}, u32[]{:S(2)}) collective-permute-start(bf16[16,512]{1,0:T(8,128)(2,1)S(1)} %get-tuple-element.44), channel_id=1, source_target_pairs={{0,20},{4,24},{8,28},{12,0},{16,4},{20,8},{24,12},{28,16},{1,21},{... | collective-permute-start | bytes 49160 | tf_op jit(solution)/shard_map/ppermute | solution.py:310
  123.0 6.4 %collective-permute-done.3 = bf16[16,512]{1,0:T(8,128)(2,1)S(1)} collective-permute-done((bf16[16,512]{1,0:T(8,128)(2,1)S(1)}, bf16[16,512]{1,0:T(8,128)(2,1)S(1)}, u32[]{:S(2)}, u32[]{:S(2)}) %collective-permute-start.3) | collective-permute-done | bytes 16416 | tf_op jit(solution)/shard_map/ppermute | solution.py:310
  129.4 0.0 collective-permute-start.8
  129.4 0.0 collective-permute-done.4
  129.4 0.1 collective-permute-start.9
  129.5 8.3 %collective-permute-done.5 = bf16[16,512]{1,0:T(8,128)(2,1)S(1)} collective-permute-done((bf16[16,512]{1,0:T(8,128)(2,1)S(1)}, bf16[16,512]{1,0:T(8,128)(2,1)S(1)}, u32[]{:S(2)}, u32[]{:S(2)}) %collective-permute-start.5) | collective-permute-done | bytes 16416 | tf_op jit(solution)/shard_map/ppermute | solution.py:310
  137.8 0.0 collective-permute-done.6
  137.8 0.0 collective-permute-done.7
  137.9 2.0 %unpack.1 = (bf16[512,512]{1,0:T(8,128)(2,1)}, bf16[512,512]{1,0:T(8,128)(2,1)}, bf16[512,512]{1,0:T(8,128)(2,1)}) custom-call(bf16[8,768,128]{2,1,0:T(8,128)(2,1)S(1)} %all-to-all-done.3.y_ref), custom_call_target="tpu_custom_call" | custom-call | bytes 3145728 | tf_op jit(solution)/shard_map/unpack/pallas_call | solution.py:392
  139.9 5.1 %collective-permute-start.10 = (bf16[16,512]{1,0:T(8,128)(2,1)S(1)}, bf16[16,512]{1,0:T(8,128)(2,1)S(1)}, u32[]{:S(2)}, u32[]{:S(2)}) collective-permute-start(bf16[16,512]{1,0:T(8,128)(2,1)S(1)} %multiply_convert_fusion), channel_id=1, source_target_pairs={{0,28},{4,0},{8,4},{12,8},{16,12},{20,16},{24,20},{28,24},{1,29},{... | collective-permute-start | bytes 49160 | tf_op jit(solution)/shard_map/ppermute | solution.py:319
  144.9 1.9 %collective-permute-start.11 = (bf16[16,512]{1,0:T(8,128)(2,1)S(1)}, bf16[16,512]{1,0:T(8,128)(2,1)S(1)}, u32[]{:S(2)}, u32[]{:S(2)}) collective-permute-start(bf16[16,512]{1,0:T(8,128)(2,1)S(1)} %multiply_convert_fusion), channel_id=1, source_target_pairs={{0,24},{4,28},{8,0},{12,4},{16,8},{20,12},{24,16},{28,20},{1,25},{... | collective-permute-start | bytes 49160 | tf_op jit(solution)/shard_map/ppermute | solution.py:319
  146.9 3.3 %collective-permute-start.13 = (bf16[16,512]{1,0:T(8,128)(2,1)S(1)}, bf16[16,512]{1,0:T(8,128)(2,1)S(1)}, u32[]{:S(2)}, u32[]{:S(2)}) collective-permute-start(bf16[16,512]{1,0:T(8,128)(2,1)S(1)} %multiply_convert_fusion), channel_id=1, source_target_pairs={{0,16},{4,20},{8,24},{12,28},{16,0},{20,4},{24,8},{28,12},{1,17},{... | collective-permute-start | bytes 49160 | tf_op jit(solution)/shard_map/ppermute | solution.py:319
  150.2 1.1 collective-permute-start.15
  151.2 0.0 collective-permute-done.11
  151.2 1.0 collective-permute-start.16
  152.3 3.4 %collective-permute-done.14 = bf16[16,512]{1,0:T(8,128)(2,1)S(1)} collective-permute-done((bf16[16,512]{1,0:T(8,128)(2,1)S(1)}, bf16[16,512]{1,0:T(8,128)(2,1)S(1)}, u32[]{:S(2)}, u32[]{:S(2)}) %collective-permute-start.14) | collective-permute-done | bytes 16416 | tf_op jit(solution)/shard_map/ppermute | solution.py:319
  155.7 0.0 collective-permute-done.15
  155.7 2.0 %collective-permute-done.16 = bf16[16,512]{1,0:T(8,128)(2,1)S(1)} collective-permute-done((bf16[16,512]{1,0:T(8,128)(2,1)S(1)}, bf16[16,512]{1,0:T(8,128)(2,1)S(1)}, u32[]{:S(2)}, u32[]{:S(2)}) %collective-permute-start.16) | collective-permute-done | bytes 16416 | tf_op jit(solution)/shard_map/ppermute | solution.py:319
  157.8 1.2 collective-permute-start.17
  159.0 4.1 %collective-permute-start.18 = (bf16[128,512]{1,0:T(8,128)(2,1)S(1)}, bf16[128,512]{1,0:T(8,128)(2,1)S(1)}, u32[]{:S(2)}, u32[]{:S(2)}) collective-permute-start(bf16[128,512]{1,0:T(8,128)(2,1)S(1)} %bitcast.100), channel_id=1, source_target_pairs={{0,2},{1,3},{2,0},{3,1},{4,6},{5,7},{6,4},{7,5},{8,10},{9,11},{10,... | collective-permute-start | bytes 393224 | tf_op jit(solution)/shard_map/ppermute | solution.py:319
  163.1 0.2 collective-permute-start.19
  163.3 6.7 %collective-permute-done.18 = bf16[128,512]{1,0:T(8,128)(2,1)S(1)} collective-permute-done((bf16[128,512]{1,0:T(8,128)(2,1)S(1)}, bf16[128,512]{1,0:T(8,128)(2,1)S(1)}, u32[]{:S(2)}, u32[]{:S(2)}) %collective-permute-start.18) | collective-permute-done | bytes 131104 | tf_op jit(solution)/shard_map/ppermute | solution.py:319
  170.2 1.1 bitcast_convert_fusion
  (52 shorter events, 0.4 us)
Async XLA Ops:
  0.6 0.7 copy-start.2
  50.6 17.3 %all-to-all-start.1 = ((bf16[8,256,128]{2,1,0:T(8,128)(2,1)}), bf16[8,256,128]{2,1,0:T(8,128)(2,1)S(1)}, u32[]{:S(2)}, u32[]{:S(2)}) async-start(bf16[8,256,128]{2,1,0:T(8,128)(2,1)} %get-tuple-element.26), calls=%async_computation.1 | async-start | bytes 1048576 | tf_op jit(solution)/shard_map/all_to_all | solution.py:336
  67.9 27.0 %all-to-all-start.2 = ((bf16[8,256,128]{2,1,0:T(8,128)(2,1)}), bf16[8,256,128]{2,1,0:T(8,128)(2,1)S(1)}, u32[]{:S(2)}, u32[]{:S(2)}) async-start(bf16[8,256,128]{2,1,0:T(8,128)(2,1)} %get-tuple-element.29), calls=%async_computation.2 | async-start | bytes 1048576 | tf_op jit(solution)/shard_map/all_to_all | solution.py:336
  94.9 6.1 %copy-start = (bf16[1,512,512]{2,1,0:T(8,128)(2,1)S(1)}, bf16[1,512,512]{2,1,0:T(8,128)(2,1)}, u32[]{:S(2)}) copy-start(bf16[1,512,512]{2,1,0:T(8,128)(2,1)} %param.10) | copy-start | bytes 1572868
  94.9 43.0 %all-to-all-start.3 = ((bf16[8,768,128]{2,1,0:T(8,128)(2,1)}), bf16[8,768,128]{2,1,0:T(8,128)(2,1)S(1)}, u32[]{:S(2)}, u32[]{:S(2)}) async-start(bf16[8,768,128]{2,1,0:T(8,128)(2,1)} %backward.1), calls=%async_computation.3 | async-start | bytes 3145728 | tf_op jit(solution)/shard_map/all_to_all | solution.py:336
  101.1 1.0 copy-start.1
  103.4 4.2 %collective-permute-start.2 = (bf16[128,512]{1,0:T(8,128)(2,1)S(1)}, bf16[128,512]{1,0:T(8,128)(2,1)S(1)}, u32[]{:S(2)}, u32[]{:S(2)}) collective-permute-start(bf16[128,512]{1,0:T(8,128)(2,1)S(1)} %get-tuple-element.40), channel_id=1, source_target_pairs={{0,3},{1,0},{2,1},{3,2},{4,7},{5,4},{6,5},{7,6},{8,11},{9,8},{10,9... | collective-permute-start | bytes 393224 | tf_op jit(solution)/shard_map/ppermute | solution.py:310
  104.7 8.4 %collective-permute-start.1 = (bf16[128,512]{1,0:T(8,128)(2,1)S(1)}, bf16[128,512]{1,0:T(8,128)(2,1)S(1)}, u32[]{:S(2)}, u32[]{:S(2)}) collective-permute-start(bf16[128,512]{1,0:T(8,128)(2,1)S(1)} %get-tuple-element.41), channel_id=1, source_target_pairs={{0,2},{1,3},{2,0},{3,1},{4,6},{5,7},{6,4},{7,5},{8,10},{9,11},{10,... | collective-permute-start | bytes 393224 | tf_op jit(solution)/shard_map/ppermute | solution.py:310
  106.3 6.9 %collective-permute-start = (bf16[128,512]{1,0:T(8,128)(2,1)S(1)}, bf16[128,512]{1,0:T(8,128)(2,1)S(1)}, u32[]{:S(2)}, u32[]{:S(2)}) collective-permute-start(bf16[128,512]{1,0:T(8,128)(2,1)S(1)} %get-tuple-element.39), channel_id=1, source_target_pairs={{0,1},{1,2},{2,3},{3,0},{4,5},{5,6},{6,7},{7,4},{8,9},{9,10},{10,1... | collective-permute-start | bytes 393224 | tf_op jit(solution)/shard_map/ppermute | solution.py:310
  113.2 16.1 %collective-permute-start.3 = (bf16[16,512]{1,0:T(8,128)(2,1)S(1)}, bf16[16,512]{1,0:T(8,128)(2,1)S(1)}, u32[]{:S(2)}, u32[]{:S(2)}) collective-permute-start(bf16[16,512]{1,0:T(8,128)(2,1)S(1)} %get-tuple-element.48), channel_id=1, source_target_pairs={{0,4},{4,8},{8,12},{12,16},{16,20},{20,24},{24,28},{28,0},{1,5},{5... | collective-permute-start | bytes 49160 | tf_op jit(solution)/shard_map/ppermute | solution.py:310
  115.3 14.1 %collective-permute-start.4 = (bf16[16,512]{1,0:T(8,128)(2,1)S(1)}, bf16[16,512]{1,0:T(8,128)(2,1)S(1)}, u32[]{:S(2)}, u32[]{:S(2)}) collective-permute-start(bf16[16,512]{1,0:T(8,128)(2,1)S(1)} %get-tuple-element.47), channel_id=1, source_target_pairs={{0,8},{4,12},{8,16},{12,20},{16,24},{20,28},{24,0},{28,4},{1,9},{5... | collective-permute-start | bytes 49160 | tf_op jit(solution)/shard_map/ppermute | solution.py:310
  116.8 21.0 %collective-permute-start.5 = (bf16[16,512]{1,0:T(8,128)(2,1)S(1)}, bf16[16,512]{1,0:T(8,128)(2,1)S(1)}, u32[]{:S(2)}, u32[]{:S(2)}) collective-permute-start(bf16[16,512]{1,0:T(8,128)(2,1)S(1)} %get-tuple-element.46), channel_id=1, source_target_pairs={{0,12},{4,16},{8,20},{12,24},{16,28},{20,0},{24,4},{28,8},{1,13},{... | collective-permute-start | bytes 49160 | tf_op jit(solution)/shard_map/ppermute | solution.py:310
  119.1 18.6 %collective-permute-start.6 = (bf16[16,512]{1,0:T(8,128)(2,1)S(1)}, bf16[16,512]{1,0:T(8,128)(2,1)S(1)}, u32[]{:S(2)}, u32[]{:S(2)}) collective-permute-start(bf16[16,512]{1,0:T(8,128)(2,1)S(1)} %get-tuple-element.45), channel_id=1, source_target_pairs={{0,16},{4,20},{8,24},{12,28},{16,0},{20,4},{24,8},{28,12},{1,17},{... | collective-permute-start | bytes 49160 | tf_op jit(solution)/shard_map/ppermute | solution.py:310
  120.6 17.2 %collective-permute-start.7 = (bf16[16,512]{1,0:T(8,128)(2,1)S(1)}, bf16[16,512]{1,0:T(8,128)(2,1)S(1)}, u32[]{:S(2)}, u32[]{:S(2)}) collective-permute-start(bf16[16,512]{1,0:T(8,128)(2,1)S(1)} %get-tuple-element.44), channel_id=1, source_target_pairs={{0,20},{4,24},{8,28},{12,0},{16,4},{20,8},{24,12},{28,16},{1,21},{... | collective-permute-start | bytes 49160 | tf_op jit(solution)/shard_map/ppermute | solution.py:310
  129.4 8.4 %collective-permute-start.8 = (bf16[16,512]{1,0:T(8,128)(2,1)S(1)}, bf16[16,512]{1,0:T(8,128)(2,1)S(1)}, u32[]{:S(2)}, u32[]{:S(2)}) collective-permute-start(bf16[16,512]{1,0:T(8,128)(2,1)S(1)} %get-tuple-element.43), channel_id=1, source_target_pairs={{0,24},{4,28},{8,0},{12,4},{16,8},{20,12},{24,16},{28,20},{1,25},{... | collective-permute-start | bytes 49160 | tf_op jit(solution)/shard_map/ppermute | solution.py:310
  129.4 8.5 %collective-permute-start.9 = (bf16[16,512]{1,0:T(8,128)(2,1)S(1)}, bf16[16,512]{1,0:T(8,128)(2,1)S(1)}, u32[]{:S(2)}, u32[]{:S(2)}) collective-permute-start(bf16[16,512]{1,0:T(8,128)(2,1)S(1)} %get-tuple-element.42), channel_id=1, source_target_pairs={{0,28},{4,0},{8,4},{12,8},{16,12},{20,16},{24,20},{28,24},{1,29},{... | collective-permute-start | bytes 49160 | tf_op jit(solution)/shard_map/ppermute | solution.py:310
  139.9 10.3 %collective-permute-start.10 = (bf16[16,512]{1,0:T(8,128)(2,1)S(1)}, bf16[16,512]{1,0:T(8,128)(2,1)S(1)}, u32[]{:S(2)}, u32[]{:S(2)}) collective-permute-start(bf16[16,512]{1,0:T(8,128)(2,1)S(1)} %multiply_convert_fusion), channel_id=1, source_target_pairs={{0,28},{4,0},{8,4},{12,8},{16,12},{20,16},{24,20},{28,24},{1,29},{... | collective-permute-start | bytes 49160 | tf_op jit(solution)/shard_map/ppermute | solution.py:319
  144.9 6.3 %collective-permute-start.11 = (bf16[16,512]{1,0:T(8,128)(2,1)S(1)}, bf16[16,512]{1,0:T(8,128)(2,1)S(1)}, u32[]{:S(2)}, u32[]{:S(2)}) collective-permute-start(bf16[16,512]{1,0:T(8,128)(2,1)S(1)} %multiply_convert_fusion), channel_id=1, source_target_pairs={{0,24},{4,28},{8,0},{12,4},{16,8},{20,12},{24,16},{28,20},{1,25},{... | collective-permute-start | bytes 49160 | tf_op jit(solution)/shard_map/ppermute | solution.py:319
  146.8 5.4 %collective-permute-start.12 = (bf16[16,512]{1,0:T(8,128)(2,1)S(1)}, bf16[16,512]{1,0:T(8,128)(2,1)S(1)}, u32[]{:S(2)}, u32[]{:S(2)}) collective-permute-start(bf16[16,512]{1,0:T(8,128)(2,1)S(1)} %multiply_convert_fusion), channel_id=1, source_target_pairs={{0,20},{4,24},{8,28},{12,0},{16,4},{20,8},{24,12},{28,16},{1,21},{... | collective-permute-start | bytes 49160 | tf_op jit(solution)/shard_map/ppermute | solution.py:319
  146.9 5.4 %collective-permute-start.13 = (bf16[16,512]{1,0:T(8,128)(2,1)S(1)}, bf16[16,512]{1,0:T(8,128)(2,1)S(1)}, u32[]{:S(2)}, u32[]{:S(2)}) collective-permute-start(bf16[16,512]{1,0:T(8,128)(2,1)S(1)} %multiply_convert_fusion), channel_id=1, source_target_pairs={{0,16},{4,20},{8,24},{12,28},{16,0},{20,4},{24,8},{28,12},{1,17},{... | collective-permute-start | bytes 49160 | tf_op jit(solution)/shard_map/ppermute | solution.py:319
  150.2 5.5 %collective-permute-start.14 = (bf16[16,512]{1,0:T(8,128)(2,1)S(1)}, bf16[16,512]{1,0:T(8,128)(2,1)S(1)}, u32[]{:S(2)}, u32[]{:S(2)}) collective-permute-start(bf16[16,512]{1,0:T(8,128)(2,1)S(1)} %multiply_convert_fusion), channel_id=1, source_target_pairs={{0,12},{4,16},{8,20},{12,24},{16,28},{20,0},{24,4},{28,8},{1,13},{... | collective-permute-start | bytes 49160 | tf_op jit(solution)/shard_map/ppermute | solution.py:319
  150.2 5.5 %collective-permute-start.15 = (bf16[16,512]{1,0:T(8,128)(2,1)S(1)}, bf16[16,512]{1,0:T(8,128)(2,1)S(1)}, u32[]{:S(2)}, u32[]{:S(2)}) collective-permute-start(bf16[16,512]{1,0:T(8,128)(2,1)S(1)} %multiply_convert_fusion), channel_id=1, source_target_pairs={{0,8},{4,12},{8,16},{12,20},{16,24},{20,28},{24,0},{28,4},{1,9},{5... | collective-permute-start | bytes 49160 | tf_op jit(solution)/shard_map/ppermute | solution.py:319
  151.2 6.4 %collective-permute-start.16 = (bf16[16,512]{1,0:T(8,128)(2,1)S(1)}, bf16[16,512]{1,0:T(8,128)(2,1)S(1)}, u32[]{:S(2)}, u32[]{:S(2)}) collective-permute-start(bf16[16,512]{1,0:T(8,128)(2,1)S(1)} %multiply_convert_fusion), channel_id=1, source_target_pairs={{0,4},{4,8},{8,12},{12,16},{16,20},{20,24},{24,28},{28,0},{1,5},{5... | collective-permute-start | bytes 49160 | tf_op jit(solution)/shard_map/ppermute | solution.py:319
  157.8 5.5 %collective-permute-start.17 = (bf16[128,512]{1,0:T(8,128)(2,1)S(1)}, bf16[128,512]{1,0:T(8,128)(2,1)S(1)}, u32[]{:S(2)}, u32[]{:S(2)}) collective-permute-start(bf16[128,512]{1,0:T(8,128)(2,1)S(1)} %bitcast.99), channel_id=1, source_target_pairs={{0,3},{1,0},{2,1},{3,2},{4,7},{5,4},{6,5},{7,6},{8,11},{9,8},{10,9... | collective-permute-start | bytes 393224 | tf_op jit(solution)/shard_map/ppermute | solution.py:319
  159.0 11.0 %collective-permute-start.18 = (bf16[128,512]{1,0:T(8,128)(2,1)S(1)}, bf16[128,512]{1,0:T(8,128)(2,1)S(1)}, u32[]{:S(2)}, u32[]{:S(2)}) collective-permute-start(bf16[128,512]{1,0:T(8,128)(2,1)S(1)} %bitcast.100), channel_id=1, source_target_pairs={{0,2},{1,3},{2,0},{3,1},{4,6},{5,7},{6,4},{7,5},{8,10},{9,11},{10,... | collective-permute-start | bytes 393224 | tf_op jit(solution)/shard_map/ppermute | solution.py:319
  163.1 6.9 %collective-permute-start.19 = (bf16[128,512]{1,0:T(8,128)(2,1)S(1)}, bf16[128,512]{1,0:T(8,128)(2,1)S(1)}, u32[]{:S(2)}, u32[]{:S(2)}) collective-permute-start(bf16[128,512]{1,0:T(8,128)(2,1)S(1)} %bitcast.101), channel_id=1, source_target_pairs={{0,1},{1,2},{2,3},{3,0},{4,5},{5,6},{6,7},{7,4},{8,9},{9,10},{10,1... | collective-permute-start | bytes 393224 | tf_op jit(solution)/shard_map/ppermute | solution.py:319

commit v4 on v0

v4 whole, which is shorter than its diff:
```python
import functools
import math

import jax
import jax.numpy as jnp
from jax import lax
from jax.experimental import pallas as pl
from jax.experimental.pallas import tpu as pltpu
from jax.sharding import PartitionSpec as P

HEADS = 8
NBR = 3
REACH = 3
GROUP = 4
MINE = HEADS // GROUP
F32 = jnp.float32
BF16 = jnp.bfloat16


def mm(a, b):
    return lax.dot_general(a, b, (((1,), (0,)), ((), ())), preferred_element_type=F32)


def halves(block):
    turned = block.T
    width = turned.shape[0] // 2
    return jnp.concatenate([turned[:width], turned[width:]], axis=1)


def beside(turned):
    rows = turned.shape[1]
    return jnp.concatenate([turned[:, : rows // 2], turned[:, rows // 2 :]], axis=0).T


def pack_kernel(near_ref, *refs):
    sources, out_ref, held, arrived = refs[:3], refs[3], refs[4:7], refs[7]
    copies = [
        pltpu.make_async_copy(source, target, arrived.at[i])
        for i, (source, target) in enumerate(zip(sources, held))
    ]
    for copy in copies:
        copy.start()
    for copy in copies:
        copy.wait()
    q_ref, k_ref, v_ref = held
    rows = q_ref.shape[0]
    width = q_ref.shape[1] // HEADS
    half = rows // 2
    here = lax.axis_index("seg")
    line = lax.broadcasted_iota(jnp.int32, (16, 2 * width), 0)
    offsets = jnp.zeros((16, 2 * width), F32)
    for e in range(NBR):
        offsets = jnp.where(line == e, (near_ref[0, e] - here + REACH).astype(F32), offsets)
    for h in range(HEADS):
        to, i = divmod(h, MINE)
        cols = slice(h * width, (h + 1) * width)
        at_q = MINE * rows + i * half
        out_ref[to, i * rows : (i + 1) * rows, :] = jnp.concatenate(
            [k_ref[:, cols], v_ref[:, cols]], axis=1
        )
        out_ref[to, at_q : at_q + half, :] = jnp.concatenate(
            [q_ref[:half, cols], q_ref[half:, cols]], axis=1
        )
        out_ref[to, MINE * (rows + half) :, :] = offsets.astype(BF16)


def list_units(near_ref, patch_of, block_of, count, first, outside, right=0, base=0):
    for p in range(GROUP):
        if not outside:
            patch_of[count] = first + p
            block_of[count] = first + p
            count = count + 1
        for e in range(NBR):
            t = p + near_ref[p, e] - REACH
            inside = jnp.logical_and(t >= 0, t < GROUP)
            patch_of[count] = first + p
            if outside:
                want = jnp.logical_not(inside)
                block_of[count] = base + jnp.where(t < 0, t + REACH, t - GROUP + right)
            else:
                want = jnp.logical_and(inside, t != p)
                block_of[count] = first + t
            count = count + jnp.where(want, 1, 0)
    return count


def in_turn(total, enter, leave):
    def both(u, slot):
        leave(u, slot, lambda: enter(u + 1, 1 - slot))

    def two(i, carry):
        both(2 * i, 0)
        both(2 * i + 1, 1)
        return carry

    @pl.when(total > 0)
    def _():
        enter(jnp.int32(0), 0)
        lax.fori_loop(0, (total - 1) // 2, two, 0)
        pl.when(total % 2 == 0)(lambda: both(total - 2, 0))
        for slot in range(2):

            @pl.when((total - 1) % 2 == slot)
            def _():
                leave(total - 1, slot, lambda: None)


def mix_units(total, patch_of, block_of, keys, q_scr, v_scr, scores, before_scr, top_scr, m_ref, o_ref):
    def enter(u, slot):
        p = patch_of[u]
        s = mm(keys(block_of[u]), q_scr[p])
        scores[slot][...] = s
        before = m_ref[p]
        top = jnp.maximum(before, jnp.max(s, axis=0, keepdims=True))
        before_scr[u] = before
        top_scr[u] = top
        m_ref[p] = top

    def leave(u, slot, then):
        p, top = patch_of[u], top_scr[u]
        prob = jnp.exp(scores[slot][...] - top).astype(BF16)
        keep = jnp.exp(before_scr[u] - top)
        then()
        o_ref[p] = o_ref[p] * keep + mm(v_scr[block_of[u]], prob)

    in_turn(total, enter, leave)


def back_units(total, patch_of, block_of, keys, q_scr, d_scr, back_scr, k_scr, pairs, lse_ref, delta_ref, dq_ref, acc):
    rows = q_scr.shape[2]

    def enter(u, slot):
        block, p = keys(block_of[u]), patch_of[u]
        pairs[slot][:, :rows] = mm(block, q_scr[p])
        pairs[slot][:, rows:] = mm(block, d_scr[p])

    def leave(u, slot, then):
        b, p = block_of[u], patch_of[u]
        prob = jnp.exp(pairs[slot][:, :rows] - lse_ref[p])
        ds = (prob * (pairs[slot][:, rows:] - delta_ref[p])).astype(BF16)
        then()
        dq_ref[p] += mm(k_scr[b], ds)
        acc[b] += mm(jnp.concatenate([ds, prob.astype(BF16)], axis=1), back_scr[p])

    in_turn(total, enter, leave)


def fill_q(x_ref, head, rows, width, q_scr, at):
    half = rows // 2
    start = MINE * rows + head * half
    for p in range(GROUP):
        turned = halves(x_ref[p, start : start + half, :])
        q_scr[at + p, :width, :] = turned * BF16(1.0 / math.sqrt(width))
        q_scr[at + p, width:, :] = jnp.zeros_like(turned)


def fill_back(x_ref, d_ref, head, rows, width, d_scr, back_scr, at=0):
    half = rows // 2
    start = MINE * rows + head * half
    blank = jnp.zeros((half, width), BF16)
    for p in range(GROUP):
        q_pair = x_ref[p, start : start + half, :]
        d_pair = d_ref[p, head * half : (head + 1) * half, :]
        back_scr[at + p, :half, :] = jnp.concatenate([q_pair[:, :width], blank], axis=1)
        back_scr[at + p, half:rows, :] = jnp.concatenate([q_pair[:, width:], blank], axis=1)
        back_scr[at + p, rows : rows + half, :] = jnp.concatenate([blank, d_pair[:, :width]], axis=1)
        back_scr[at + p, rows + half :, :] = jnp.concatenate([blank, d_pair[:, width:]], axis=1)
        d_turned = halves(d_pair)
        d_scr[at + p, :width, :] = jnp.zeros_like(d_turned)
        d_scr[at + p, width:, :] = d_turned * BF16(1.0 / math.sqrt(width))


def near_kernel(near_ref, x_ref, o_ref, m_ref, s0, s1, before_scr, top_scr, q_scr, v_scr, patch_of, block_of):
    rows, width = s0.shape[0], x_ref.shape[2] // 2
    total = jnp.int32(0)
    for i in range(MINE):
        total = list_units(near_ref, patch_of, block_of, total, i * GROUP, False)
        fill_q(x_ref, i, rows, width, q_scr, i * GROUP)
        for b in range(GROUP):
            turned = x_ref[b, i * rows : (i + 1) * rows, :].T
            v_scr[i * GROUP + b, :width, :] = turned[width:]
            v_scr[i * GROUP + b, width:, :] = jnp.ones((v_scr.shape[1] - width, rows), BF16)
    o_ref[...] = jnp.zeros_like(o_ref)
    m_ref[...] = jnp.full_like(m_ref, -jnp.inf)

    def keys(b):
        return x_ref[b % GROUP, pl.ds(pl.multiple_of(b // GROUP * rows, rows), rows), :]

    mix_units(total, patch_of, block_of, keys, q_scr, v_scr, (s0, s1), before_scr, top_scr, m_ref, o_ref)


def far_kernel(right, near_ref, x_ref, g_ref, w_ref, halo_ref, o_in, m_in, attn_ref, lse_ref, delta_ref, dq_ref, d_ref, term_ref, out_ref, acc, s0, s1, before_scr, top_scr, m_scr, o_scr, q_scr, d_scr, back_scr, v_scr, k_scr, patch_of, block_of):
    rows, width = q_scr.shape[2], x_ref.shape[2] // 2
    half, halo = rows // 2, halo_ref.shape[0]
    me = lax.axis_index("seg")
    other = 1 - me // GROUP if out_ref.shape[0] == 2 else 0
    place = me % GROUP * MINE * width
    mine = w_ref[pl.ds(pl.multiple_of(place, MINE * width), MINE * width), :]
    for p in range(GROUP):
        d_attn = lax.dot_general(
            mine, g_ref[p], (((1,), (1,)), ((), ())), preferred_element_type=F32
        ).astype(BF16)
        for i in range(MINE):
            d_ref[p, i * half : (i + 1) * half, :] = beside(d_attn[i * width : (i + 1) * width])
    total = jnp.int32(0)
    for i in range(MINE):
        total = list_units(near_ref, patch_of, block_of, total, i * GROUP, True, right, i * halo)
        fill_q(x_ref, i, rows, width, q_scr, i * GROUP)
        fill_back(x_ref, d_ref, i, rows, width, d_scr, back_scr, i * GROUP)
        for b in range(halo):
            turned = halo_ref[b, i * rows : (i + 1) * rows, :].T
            k_scr[i * halo + b] = turned[:width]
            v_scr[i * halo + b, :width, :] = turned[width:]
            v_scr[i * halo + b, width:, :] = jnp.ones((v_scr.shape[1] - width, rows), BF16)
    o_scr[...] = o_in[...]
    m_scr[...] = m_in[...]

    def keys(b):
        return halo_ref[b % halo, pl.ds(pl.multiple_of(b // halo * rows, rows), rows), :]

    firsts = (s0.at[:, :rows], s1.at[:, :rows])
    mix_units(total, patch_of, block_of, keys, q_scr, v_scr, firsts, before_scr, top_scr, m_scr, o_scr)
    attns = []
    for p in range(MINE * GROUP):
        sums = o_scr[p, width : width + 1, :]
        attn = (o_scr[p, :width, :] * (1.0 / sums)).astype(BF16)
        attns.append(attn)
        attn_ref[p % GROUP, p // GROUP * half : (p // GROUP + 1) * half, :] = beside(attn)
        lse_ref[p] = m_scr[p] + jnp.log(sums)
        product = d_scr[p, width:, :].astype(F32) * attn.astype(F32)
        delta_ref[p] = jnp.sum(product, axis=0, keepdims=True)
    term = jnp.zeros(term_ref.shape, F32)
    for p in range(GROUP):
        rows_here = jnp.concatenate([attns[i * GROUP + p] for i in range(MINE)], axis=0)
        term = term + mm(rows_here, g_ref[p])
    term_ref[...] = term.astype(BF16)
    acc[...] = jnp.zeros_like(acc)
    dq_ref[...] = jnp.zeros_like(dq_ref)
    back_units(total, patch_of, block_of, keys, q_scr, d_scr, back_scr, k_scr, (s0, s1), lse_ref, delta_ref, dq_ref, acc)
    for i in range(MINE):
        for b in range(halo):
            out_ref[other, b, i * rows : (i + 1) * rows, :] = acc[i * halo + b].astype(BF16)


def own_kernel(head, near_ref, x_ref, d_ref, lse_ref, delta_ref, dq_in, out_ref, acc, s0, s1, dq_scr, q_scr, d_scr, back_scr, k_scr, patch_of, block_of):
    rows, width = q_scr.shape[2], x_ref.shape[2] // 2
    total = list_units(near_ref, patch_of, block_of, jnp.int32(0), 0, False)
    fill_q(x_ref, head, rows, width, q_scr, 0)
    fill_back(x_ref, d_ref, head, rows, width, d_scr, back_scr)
    mine = slice(head * rows, (head + 1) * rows)
    for b in range(GROUP):
        k_scr[b] = x_ref[b, mine, :].T[:width]
    own = pl.ds(head * GROUP, GROUP)
    acc[...] = jnp.zeros_like(acc)
    dq_scr[...] = dq_in[head * GROUP : (head + 1) * GROUP]
    keys = lambda b: x_ref[b, mine, :]
    back_units(total, patch_of, block_of, keys, q_scr, d_scr, back_scr, k_scr, (s0, s1), lse_ref.at[own], delta_ref.at[own], dq_scr, acc)
    for p in range(GROUP):
        out_ref[p, :rows, :] = acc[p].astype(BF16)
        out_ref[p, rows:, :] = beside(dq_scr[p].astype(BF16))


def merge_kernel(alone, *refs):
    owns, back_ref, attn_ref, out_ref = refs[:MINE], refs[MINE], refs[-2], refs[-1]
    each = owns[0].shape[1]
    rows = each * 2 // 3
    for p in range(GROUP):
        out_ref[p, MINE * each :, :] = attn_ref[p]
    for i in range(MINE):
        for p in range(GROUP):
            out_ref[p, i * each : (i + 1) * each, :] = owns[i][p]
        mine = slice(i * each, i * each + rows)
        other = 1 - lax.axis_index("seg") // GROUP if alone else 0
        for side in range(back_ref.shape[1] // REACH):
            start = other if alone else 1 - side
            for j in range(REACH):
                term = back_ref[other, side * REACH + j, i * rows : (i + 1) * rows, :].astype(F32)
                here = out_ref[start + j, mine, :].astype(F32)
                out_ref[start + j, mine, :] = (here + term).astype(BF16)


def unpack_kernel(y_ref, w_ref, out_ref, dq_ref, dk_ref, dv_ref):
    rows, width = dk_ref.shape[0], y_ref.shape[2] // 2
    half = rows // 2
    sides = ([], [])
    for h in range(HEADS):
        cols = slice(h * width, (h + 1) * width)
        r, i = divmod(h, MINE)
        at = i * (rows + half)
        dk_ref[:, cols] = y_ref[r, at : at + rows, :width]
        dv_ref[:, cols] = y_ref[r, at : at + rows, width:]
        dq_ref[:half, cols] = y_ref[r, at + rows : at + rows + half, :width]
        dq_ref[half:, cols] = y_ref[r, at + rows : at + rows + half, width:]
        at = MINE * (rows + half) + i * half
        sides[0].append(y_ref[r, at : at + half, :width])
        sides[1].append(y_ref[r, at : at + half, width:])
    attn = jnp.concatenate([jnp.concatenate(side, axis=1) for side in sides], axis=0)
    out_ref[...] = mm(attn, w_ref[...]).astype(BF16)


def params(mib=32):
    return pltpu.CompilerParams(vmem_limit_bytes=mib * 2**20)


def cost(flops, bytes_accessed, exps=0):
    return pl.CostEstimate(flops=flops // 1000, bytes_accessed=bytes_accessed // 1000, transcendentals=0)


def in_hbm(array):
    return pltpu.with_memory_space_constraint(array, pltpu.HBM)


def around(count, by):
    return [(i, (i + by) % count) for i in range(count)]


def exchange(pieces, axis):
    count = pieces.shape[0]
    if count > HEADS:
        return lax.all_to_all(pieces, axis, 0, 0)
    here = lax.axis_index(axis)
    arrived = []
    for by in range(count):
        piece = lax.dynamic_index_in_dim(pieces, (here + by) % count, 0, keepdims=False)
        arrived.append(lax.ppermute(piece, axis, around(count, by)) if by else piece)
    return jnp.stack(arrived)


def gathered(piece, axis, count):
    size = lax.axis_size(axis)
    here = lax.axis_index(axis) % count
    arrived = [piece]
    for by in range(1, count):
        pairs = [(i, i // count * count + (i + by) % count) for i in range(size)]
        arrived.append(lax.ppermute(piece, axis, pairs))
    line = jnp.stack(arrived[::-1] + arrived[::-1])
    return lax.dynamic_slice_in_dim(line, count - 1 - here, count, 0)


def body(queries, key_rows, value_rows, w_out, grad_out, neighbours):
    _, rows, model = queries.shape
    width = model // HEADS
    half, wide = rows // 2, 2 * width
    seg = lax.axis_size("seg")
    samples = lax.axis_size("sample")
    groups = seg // GROUP
    split = [[g * GROUP + i for i in range(GROUP)] for g in range(groups)]
    alone = groups == 2
    halo = REACH if alone else 2 * REACH
    ones = 16
    most = GROUP * (NBR + 1)
    vmem = pl.BlockSpec(memory_space=pltpu.VMEM)
    smem = pl.BlockSpec(memory_space=pltpu.SMEM)
    unit_cost = rows * rows

    def swap(array):
        return lax.all_to_all(array, "seg", 0, 0, axis_index_groups=split)

    def shifted(array, by):
        pairs = [(s, s + by) for s in range(seg) if 0 <= s + by < seg]
        return lax.ppermute(array, "seg", pairs)

    def across(array):
        return lax.ppermute(array, "seg", [(s, (s + GROUP) % seg) for s in range(seg)])

    def between(array):
        pairs = [[i, i + GROUP] for i in range(GROUP)]
        return lax.all_to_all(array, "seg", 0, 0, axis_index_groups=pairs)

    def call(kernel, name, outs, scratch, flops, exps=0, mib=32):
        return pl.pallas_call(
            kernel,
            out_shape=[jax.ShapeDtypeStruct(shape, kind) for shape, kind in outs],
            out_specs=[vmem] * len(outs),
            scratch_shapes=scratch,
            compiler_params=params(mib),
            cost_estimate=cost(flops, 4 * 2**20, exps),
            name=name,
        )

    packed = pl.pallas_call(
        pack_kernel,
        in_specs=[smem] + [pl.BlockSpec(memory_space=pltpu.HBM)] * 3,
        scratch_shapes=[pltpu.VMEM((rows, model), BF16)] * 3 + [pltpu.SemaphoreType.DMA((3,))],
        out_shape=jax.ShapeDtypeStruct((GROUP, MINE * (rows + half) + 16, wide), BF16),
        compiler_params=params(),
        cost_estimate=cost(2 * rows * model * model, 10 * rows * model),
        name="pack",
    )(neighbours[0], *(in_hbm(a) for a in (queries[0], key_rows[0], value_rows[0])))
    x = swap(packed)
    at = MINE * (rows + half)
    near = x[:, at : at + NBR, 0].astype(jnp.int32)
    copies = jnp.broadcast_to(grad_out, (GROUP, rows, model))
    x, near, copies = lax.optimization_barrier((x, near, copies))
    kv = x[:, : MINE * rows]
    if alone:
        first = 1 - lax.axis_index("seg") // GROUP
        beyond = lax.dynamic_slice_in_dim(kv, first, REACH, 0)
        beyond = across(beyond)
    else:
        beyond = jnp.concatenate([shifted(kv[1:], GROUP), shifted(kv[:REACH], -GROUP)], axis=0)
    grads_here = swap(copies)

    lists = lambda count: [pltpu.SMEM((count + 8,), jnp.int32)] * 2
    sheet = pltpu.VMEM((rows, rows), F32)
    double = pltpu.VMEM((rows, 2 * rows), F32)
    lines = lambda count: pltpu.VMEM((count, 1, rows), F32)
    patches = MINE * GROUP
    o_state, m_state = call(
        near_kernel,
        "near",
        [((patches, width + ones, rows), F32), ((patches, 1, rows), F32)],
        [
            sheet,
            sheet,
            lines(MINE * most),
            lines(MINE * most),
            pltpu.VMEM((patches, wide, rows), BF16),
            pltpu.VMEM((patches, width + ones, rows), BF16),
        ]
        + lists(MINE * most),
        20 * unit_cost * 512,
        20 * unit_cost,
    )(near, x)

    attn, lse, delta, dq, d, w_term, far = call(
        functools.partial(far_kernel, halo - REACH),
        "far",
        [
            ((GROUP, MINE * half, wide), BF16),
            ((patches, 1, rows), F32),
            ((patches, 1, rows), F32),
            ((patches, width, rows), F32),
            ((GROUP, MINE * half, wide), BF16),
            ((MINE * width, model), BF16),
            ((2 if alone else 1, halo, MINE * rows, wide), BF16),
        ],
        [
            pltpu.VMEM((MINE * halo, rows, wide), F32),
            double,
            double,
            lines(MINE * most),
            lines(MINE * most),
            lines(patches),
            pltpu.VMEM((patches, width + ones, rows), F32),
            pltpu.VMEM((patches, wide, rows), BF16),
            pltpu.VMEM((patches, wide, rows), BF16),
            pltpu.VMEM((patches, 2 * rows, wide), BF16),
            pltpu.VMEM((MINE * halo, width + ones, rows), BF16),
            pltpu.VMEM((MINE * halo, width, rows), BF16),
        ]
        + lists(MINE * most),
        6 * unit_cost * 1536,
        12 * unit_cost,
        60,
    )(near, x, grads_here, w_out, beyond, o_state, m_state)
    if alone:
        back = between(far)
    else:
        far = far[0]
        back = jnp.concatenate([shifted(far[:REACH], -GROUP), shifted(far[REACH:], GROUP)], axis=0)
        back = back[None]
    def own_terms(i, lse, delta, dq):
        return call(
            functools.partial(own_kernel, i),
            f"own{i}",
            [((GROUP, rows + half, wide), BF16)],
            [
                pltpu.VMEM((GROUP, rows, wide), F32),
                double,
                double,
                pltpu.VMEM((GROUP, width, rows), F32),
                pltpu.VMEM((GROUP, wide, rows), BF16),
                pltpu.VMEM((GROUP, wide, rows), BF16),
                pltpu.VMEM((GROUP, 2 * rows, wide), BF16),
                pltpu.VMEM((GROUP, width, rows), BF16),
            ]
            + lists(most),
            10 * unit_cost * 1280,
            10 * unit_cost,
        )(near, x, d, lse, delta, dq)[0]

    part = MINE * width // samples
    w_part = exchange(w_term.reshape(samples, part, model), "sample")
    w_part = jnp.sum(w_part.astype(F32), axis=0).astype(BF16)
    own0 = own_terms(0, lse, delta, dq)
    w_part, lse, own0 = lax.optimization_barrier((w_part, lse, own0))
    own1 = own_terms(1, lse, delta, dq)
    if alone:
        w_part = w_part.astype(F32) + across(w_part).astype(F32)
    else:
        alike = [[g * GROUP + r for g in range(groups)] for r in range(GROUP)]
        w_part = lax.psum(w_part.astype(F32), "seg", axis_index_groups=alike)
    w_part, back, own1 = lax.optimization_barrier((w_part, back, own1))
    (merged,) = call(
        functools.partial(merge_kernel, alone),
        "merge",
        [((GROUP, MINE * (rows + 2 * half), wide), BF16)],
        [],
        0,
    )(own0, own1, back, attn)
    w_part, merged = lax.optimization_barrier((w_part, merged))
    home = swap(merged)
    grad_scale = 1.0 / math.sqrt(samples * rows * seg)
    w_rows = gathered((w_part * grad_scale).astype(BF16), "seg", GROUP)
    w_all = gathered(w_rows, "sample", samples)
    grad_w_out = jnp.transpose(w_all, (1, 0, 2, 3)).reshape(model, model).astype(F32)
    attended, grad_q, grad_k, grad_v = call(
        unpack_kernel, "unpack", [((rows, model), BF16)] * 4, [], 2 * rows * model * model
    )(home, w_out)
    return attended[None], grad_q[None], grad_k[None], grad_v[None], grad_w_out


def solution(mesh):
    rows = P("sample", "seg", None)
    return jax.shard_map(
        body,
        mesh=mesh,
        in_specs=(rows, rows, rows, P(), rows, rows),
        out_specs=(rows, rows, rows, rows, P()),
        check_vma=False,
    )
```

time: 539 us -> 169 us (0.31)
  the two profiles are of different devices: /device:TPU:0 before, /device:TPU:13 now
where the time goes in v4:
time: 169 us
  waiting for transfers between devices  56.5 us (33%)
  Pallas kernels  44.1 us (26%)
  starting transfers between devices  30.4 us (18%)
  blocking collectives  21.8 us (13%)
  local copies, waits for them, and re-layouts  13.9 us (8%)
    ppermute x2, waiting for transfers between devices, across(): lax.ppermute(array, 'seg', [(s, (s + GROUP) % seg) for s in range(seg)])  36.4 us
    all_to_all x1, blocking collectives, swap(): return lax.all_to_all(array, 'seg', 0, 0, axis_index_groups=split)  21.8 us
    pallas_call x2, Pallas kernels, own_terms(): call(functools.partial(own_kernel, i), f'own{i}', [((GROUP, rows + half,...  17.2 us
    all_to_all x2, waiting for transfers between devices, swap(): return lax.all_to_all(array, 'seg', 0, 0, axis_index_groups=split)  15.8 us
    pallas_call x1, Pallas kernels, body(): call(functools.partial(far_kernel, halo - REACH), 'far', [((GROUP, MINE *...  14.1 us
    unnamed x55, local copies, waits for them, and re-layouts  12.1 us
    all_to_all x2, starting transfers between devices, swap(): return lax.all_to_all(array, 'seg', 0, 0, axis_index_groups=split)  9.94 us
    ppermute x6, starting transfers between devices, gathered(): arrived.append(lax.ppermute(piece, axis, pairs))  8.64 us
  transfers between devices with their start and end apart: 14, of which 6 were waited for; matrix products, arithmetic and copies ran while one was open for 1% of the time, Pallas kernels for 15%

profile of v4, /device:TPU:13, one launch (start us, length us, event | category | flops | bytes accessed | tf_op | source)
XLA Modules:
  0.0 169.0 jit_solution(12249799018029716715)
XLA Ops:
  0.6 0.6 copy-done.17
  1.3 2.4 %pack.1 = bf16[4,1552,128]{2,1,0:T(8,128)(2,1)S(1)} custom-call(s32[1,3]{1,0:T(1,128)S(1)} %bitcast.53, bf16[512,512]{1,0:T(8,128)(2,1)} %bitcast.56, bf16[512,512]{1,0:T(8,128)(2,1)} %bitcast.57, bf16[512,512]{1,0:T(8,128)(2,1)} %bitcast.58), custom_call_target="tpu_custom_call" | custom-call | flops 268435 | bytes 2621 | tf_op jit(solution)/shard_map/pack/pallas_call | solution.py:381
  3.7 0.0 copy-start.19
  3.7 21.8 %all_to_all.20.x_ref = bf16[4,1552,128]{2,1,0:T(8,128)(2,1)S(1)} all-to-all(bf16[4,1552,128]{2,1,0:T(8,128)(2,1)S(1)} %pack.1), channel_id=1, replica_groups={{0,4,8,12},{16,20,24,28},{1,5,9,13},{17,21,25,29},{2,6,10,14},{18,22,26..., dimensions={0} | all-to-all | bytes 3178496 | tf_op jit(solution)/shard_map/all_to_all | solution.py:357
  25.5 0.1 convert_reduce_fusion.near_ref
  25.6 1.7 broadcast_in_dim.20
  27.3 5.2 %all-to-all-start.1 = ((bf16[4,512,512]{2,1,0:T(8,128)(2,1)}), bf16[4,512,512]{2,1,0:T(8,128)(2,1)}, u32[]{:S(2)}, u32[]{:S(2)}) async-start(bf16[4,512,512]{2,1,0:T(8,128)(2,1)} %broadcast_in_dim.20), calls=%async_computation.1 | async-start | bytes 4194304 | tf_op jit(solution)/shard_map/all_to_all | solution.py:357
  32.5 0.1 slice.7
  32.6 0.1 constant_dynamic-slice_fusion.1
  32.7 2.4 %collective-permute-start = (bf16[3,1024,128]{2,1,0:T(8,128)(2,1)S(1)}, bf16[3,1024,128]{2,1,0:T(8,128)(2,1)S(1)}, u32[]{:S(2)}, u32[]{:S(2)}) collective-permute-start(bf16[3,1024,128]{2,1,0:T(8,128)(2,1)S(1)} %constant_dynamic-slice_fusion.1), channel_id=1, source_target_pairs={{0,16},{4,20},{8,24},{12,28},{16,0},{20,4},{24,8},{28,12},{1,17},{... | collective-permute-start | bytes 2359304 | tf_op jit(solution)/shard_map/ppermute | solution.py:364
  35.0 7.6 %near.1 = (f32[8,80,512]{2,1,0:T(8,128)S(1)}, f32[8,1,512]{2,1,0:T(1,128)S(1)}) custom-call(s32[4,3]{1,0:T(4,128)S(1)} %convert_reduce_fusion.near_ref, bf16[4,1552,128]{2,1,0:T(8,128)(2,1)S(1)} %all_to_all.20.x_ref), custom_call_target="tpu_custom_call" | custom-call | flops 2684354 | bytes 4194 | tf_op jit(solution)/shard_map/near/pallas_call | solution.py:409
  42.7 1.1 copy-done.10
  43.7 0.6 copy-done.16
  44.3 28.6 %collective-permute-done.halo_ref = bf16[3,1024,128]{2,1,0:T(8,128)(2,1)S(1)} collective-permute-done((bf16[3,1024,128]{2,1,0:T(8,128)(2,1)S(1)}, bf16[3,1024,128]{2,1,0:T(8,128)(2,1)S(1)}, u32[]{:S(2)}, u32[]{:S(2)}) %collective-permute-start) | collective-permute-done | bytes 786464 | tf_op jit(solution)/shard_map/ppermute | solution.py:364
  73.0 0.9 copy-done.18
  73.9 14.1 %far.1 = (bf16[4,512,128]{2,1,0:T(8,128)(2,1)}, f32[8,1,512]{2,1,0:T(1,128)}, f32[8,1,512]{2,1,0:T(1,128)}, f32[8,64,512]{2,1,0:T(8,128)}, bf16[4,512,128]{2,1,0...) custom-call(s32[4,3]{1,0:T(4,128)} %copy-done.14, bf16[4,1552,128]{2,1,0:T(8,128)(2,1)} %copy-done, ...), custom_call_target="tpu_custom_call" | custom-call | flops 2415919 | bytes 4194 | tf_op jit(solution)/shard_map/far/pallas_call | solution.py:426
  88.1 3.8 %all-to-all-start.2 = ((bf16[2,3,1024,128]{3,2,1,0:T(8,128)(2,1)}), bf16[2,3,1024,128]{3,2,1,0:T(8,128)(2,1)S(1)}, u32[]{:S(2)}, u32[]{:S(2)}) async-start(bf16[2,3,1024,128]{3,2,1,0:T(8,128)(2,1)} %get-tuple-element.40), calls=%async_computation.2 | async-start | bytes 3145728 | tf_op jit(solution)/shard_map/all_to_all | solution.py:368
  92.0 1.1 collective-permute-start.1
  93.0 1.2 collective-permute-start.2
  94.3 0.0 copy-start.3
  94.3 1.2 copy-done.3
  95.5 1.0 copy-done.9
  96.6 8.7 %own0.1.refs_0_ = bf16[4,768,128]{2,1,0:T(8,128)(2,1)S(1)} custom-call(s32[4,3]{1,0:T(4,128)S(1)} %copy-done.15, bf16[4,1552,128]{2,1,0:T(8,128)(2,1)S(1)} %copy-done.1, bf16[4,512,128]{2,1,0:T(8,128)(2,1)S(1)} %copy-done.9, f32[8,1,512]{2,1,0:T(1,128)S(1)} %copy-done.12, f32[8,1,512]{2,1,0:T(1,128)S(1)} %copy-done.13, f32[8,64,512]{2,1,0:T(8,128)S(1)} %copy-done.3), custom_call_target="tpu_custom_call" | custom-call | flops 3355443 | bytes 4194 | tf_op jit(solution)/shard_map/own0/pallas_call | solution.py:464
  105.3 0.0 copy-start.4
  105.3 0.9 copy-done.4
  106.2 0.0 collective-permute-done.1
  106.2 3.3 %collective-permute-start.4 = (bf16[32,512]{1,0:T(8,128)(2,1)S(1)}, bf16[32,512]{1,0:T(8,128)(2,1)S(1)}, u32[]{:S(2)}, u32[]{:S(2)}) collective-permute-start(bf16[32,512]{1,0:T(8,128)(2,1)S(1)} %fusion.1), channel_id=1, source_target_pairs={{0,16},{4,20},{8,24},{12,28},{16,0},{20,4},{24,8},{28,12},{1,17},{... | collective-permute-start | bytes 98312 | tf_op jit(solution)/shard_map/ppermute | solution.py:364
  109.5 8.5 %own1.1.refs_1_ = bf16[4,768,128]{2,1,0:T(8,128)(2,1)S(1)} custom-call(s32[4,3]{1,0:T(4,128)S(1)} %copy-done.15, bf16[4,1552,128]{2,1,0:T(8,128)(2,1)S(1)} %copy-done.1, bf16[4,512,128]{2,1,0:T(8,128)(2,1)S(1)} %copy-done.9, f32[8,1,512]{2,1,0:T(1,128)S(1)} %copy-done.12, f32[8,1,512]{2,1,0:T(1,128)S(1)} %copy-done.13, f32[8,64,512]{2,1,0:T(8,128)S(1)} %copy-done.3), custom_call_target="tpu_custom_call" | custom-call | flops 3355443 | bytes 4194 | tf_op jit(solution)/shard_map/own1/pallas_call | solution.py:464
  118.1 0.9 copy-done.6
  118.9 7.8 %collective-permute-done.4 = bf16[32,512]{1,0:T(8,128)(2,1)S(1)} collective-permute-done((bf16[32,512]{1,0:T(8,128)(2,1)S(1)}, bf16[32,512]{1,0:T(8,128)(2,1)S(1)}, u32[]{:S(2)}, u32[]{:S(2)}) %collective-permute-start.4) | collective-permute-done | bytes 32800 | tf_op jit(solution)/shard_map/ppermute | solution.py:364
  126.7 0.0 copy-start.5
  126.7 1.1 copy-done.5
  127.9 1.1 copy-done.7
  129.0 1.0 copy-done.11
  130.1 0.4 merge.1
  130.5 1.4 copy-done.2
  131.9 4.7 %collective-permute-start.5 = (bf16[32,512]{1,0:T(8,128)(2,1)S(1)}, bf16[32,512]{1,0:T(8,128)(2,1)S(1)}, u32[]{:S(2)}, u32[]{:S(2)}) collective-permute-start(bf16[32,512]{1,0:T(8,128)(2,1)S(1)} %multiply_convert_fusion), channel_id=1, source_target_pairs={{0,12},{4,0},{8,4},{12,8},{16,28},{20,16},{24,20},{28,24},{1,13},{... | collective-permute-start | bytes 98312 | tf_op jit(solution)/shard_map/ppermute | solution.py:335
  136.6 0.4 collective-permute-start.7
  136.9 4.7 %all-to-all-start.3 = ((bf16[4,2048,128]{2,1,0:T(8,128)(2,1)}), bf16[4,2048,128]{2,1,0:T(8,128)(2,1)S(1)}, u32[]{:S(2)}, u32[]{:S(2)}) async-start(bf16[4,2048,128]{2,1,0:T(8,128)(2,1)} %copy-done.2), calls=%async_computation.3 | async-start | bytes 4194304 | tf_op jit(solution)/shard_map/all_to_all | solution.py:357
  141.8 1.8 %collective-permute-start.8 = (bf16[4,32,512]{2,1,0:T(8,128)(2,1)S(1)}, bf16[4,32,512]{2,1,0:T(8,128)(2,1)S(1)}, u32[]{:S(2)}, u32[]{:S(2)}) collective-permute-start(bf16[4,32,512]{2,1,0:T(8,128)(2,1)S(1)} %constant_dynamic-slice_fusion), channel_id=1, source_target_pairs={{0,3},{1,0},{2,1},{3,2},{4,7},{5,4},{6,5},{7,6},{8,11},{9,8},{10,9... | collective-permute-start | bytes 393224 | tf_op jit(solution)/shard_map/ppermute | solution.py:335
  143.7 1.7 %collective-permute-start.10 = (bf16[4,32,512]{2,1,0:T(8,128)(2,1)S(1)}, bf16[4,32,512]{2,1,0:T(8,128)(2,1)S(1)}, u32[]{:S(2)}, u32[]{:S(2)}) collective-permute-start(bf16[4,32,512]{2,1,0:T(8,128)(2,1)S(1)} %constant_dynamic-slice_fusion), channel_id=1, source_target_pairs={{0,1},{1,2},{2,3},{3,0},{4,5},{5,6},{6,7},{7,4},{8,9},{9,10},{10,1... | collective-permute-start | bytes 393224 | tf_op jit(solution)/shard_map/ppermute | solution.py:335
  145.4 1.3 collective-permute-done.8
  146.7 2.4 %collective-permute-done.9 = bf16[4,32,512]{2,1,0:T(8,128)(2,1)S(1)} collective-permute-done((bf16[4,32,512]{2,1,0:T(8,128)(2,1)S(1)}, bf16[4,32,512]{2,1,0:T(8,128)(2,1)S(1)}, u32[]{:S(2)}, u32[]{:S(2)}) %collective-permute-start.9) | collective-permute-done | bytes 131104 | tf_op jit(solution)/shard_map/ppermute | solution.py:335
  149.1 0.0 copy-start.8
  149.1 0.5 collective-permute-done.10
  149.7 1.1 dynamic-slice_convert_fusion
  150.8 15.8 %all-to-all-done.3.y_ref = bf16[4,2048,128]{2,1,0:T(8,128)(2,1)S(1)} async-done(((bf16[4,2048,128]{2,1,0:T(8,128)(2,1)}), bf16[4,2048,128]{2,1,0:T(8,128)(2,1)S(1)}, u32[]{:S(2)}, u32[]{:S(2)}) %all-to-all-start.3) | async-done | bytes 2097184 | tf_op jit(solution)/shard_map/all_to_all | solution.py:357
  166.7 2.3 %unpack.1 = (bf16[512,512]{1,0:T(8,128)(2,1)}, bf16[512,512]{1,0:T(8,128)(2,1)}, bf16[512,512]{1,0:T(8,128)(2,1)}, bf16[512,512]{1,0:T(8,128)(2,1)}) custom-call(bf16[4,2048,128]{2,1,0:T(8,128)(2,1)S(1)} %all-to-all-done.3.y_ref, bf16[512,512]{1,0:T(8,128)(2,1)S(1)} %copy-done.8), custom_call_target="tpu_custom_call" | custom-call | flops 268435 | bytes 4194 | tf_op jit(solution)/shard_map/unpack/pallas_call | solution.py:508
  (56 shorter events, 0.3 us)
Async XLA Ops:
  0.6 0.7 copy-start.17
  3.7 21.9 %copy-start.19 = (bf16[1,512,512]{2,1,0:T(8,128)(2,1)S(1)}, bf16[1,512,512]{2,1,0:T(8,128)(2,1)}, u32[]{:S(2)}) copy-start(bf16[1,512,512]{2,1,0:T(8,128)(2,1)} %param.10) | copy-start | bytes 1572868
  25.5 9.6 %copy-start = (bf16[4,1552,128]{2,1,0:T(8,128)(2,1)}, bf16[4,1552,128]{2,1,0:T(8,128)(2,1)S(1)}, u32[]{:S(2)}) copy-start(bf16[4,1552,128]{2,1,0:T(8,128)(2,1)S(1)} %all_to_all.20.x_ref) | copy-start | bytes 4767748
  25.6 9.4 %copy-start.14 = (s32[4,3]{1,0:T(4,128)}, s32[4,3]{1,0:T(4,128)S(1)}, u32[]{:S(2)}) copy-start(s32[4,3]{1,0:T(4,128)S(1)} %convert_reduce_fusion.near_ref) | copy-start | bytes 148
  27.3 45.7 %all-to-all-start.1 = ((bf16[4,512,512]{2,1,0:T(8,128)(2,1)}), bf16[4,512,512]{2,1,0:T(8,128)(2,1)}, u32[]{:S(2)}, u32[]{:S(2)}) async-start(bf16[4,512,512]{2,1,0:T(8,128)(2,1)} %broadcast_in_dim.20), calls=%async_computation.1 | async-start | bytes 4194304 | tf_op jit(solution)/shard_map/all_to_all | solution.py:357
  32.7 40.3 %collective-permute-start = (bf16[3,1024,128]{2,1,0:T(8,128)(2,1)S(1)}, bf16[3,1024,128]{2,1,0:T(8,128)(2,1)S(1)}, u32[]{:S(2)}, u32[]{:S(2)}) collective-permute-start(bf16[3,1024,128]{2,1,0:T(8,128)(2,1)S(1)} %constant_dynamic-slice_fusion.1), channel_id=1, source_target_pairs={{0,16},{4,20},{8,24},{12,28},{16,0},{20,4},{24,8},{28,12},{1,17},{... | collective-permute-start | bytes 2359304 | tf_op jit(solution)/shard_map/ppermute | solution.py:364
  42.7 1.1 copy-start.10
  43.7 0.6 copy-start.16
  73.0 0.9 copy-start.18
  88.1 3.9 %copy-start.20 = (bf16[128,512]{1,0:T(8,128)(2,1)S(1)}, bf16[128,512]{1,0:T(8,128)(2,1)}, u32[]{:S(2)}) copy-start(bf16[128,512]{1,0:T(8,128)(2,1)} %get-tuple-element.34) | copy-start | bytes 393220
  88.1 6.2 %copy-start.1 = (bf16[4,1552,128]{2,1,0:T(8,128)(2,1)S(1)}, bf16[4,1552,128]{2,1,0:T(8,128)(2,1)}, u32[]{:S(2)}) copy-start(bf16[4,1552,128]{2,1,0:T(8,128)(2,1)} %copy-done) | copy-start | bytes 4767748
  88.1 6.2 %copy-start.12 = (f32[8,1,512]{2,1,0:T(1,128)S(1)}, f32[8,1,512]{2,1,0:T(1,128)}, u32[]{:S(2)}) copy-start(f32[8,1,512]{2,1,0:T(1,128)} %get-tuple-element.41.lse_ref) | copy-start | bytes 49156
  88.1 6.2 %copy-start.13 = (f32[8,1,512]{2,1,0:T(1,128)S(1)}, f32[8,1,512]{2,1,0:T(1,128)}, u32[]{:S(2)}) copy-start(f32[8,1,512]{2,1,0:T(1,128)} %get-tuple-element.37.delta_ref) | copy-start | bytes 49156
  88.1 6.2 %copy-start.15 = (s32[4,3]{1,0:T(4,128)S(1)}, s32[4,3]{1,0:T(4,128)}, u32[]{:S(2)}) copy-start(s32[4,3]{1,0:T(4,128)} %copy-done.14) | copy-start | bytes 148
  88.1 38.6 %all-to-all-start.2 = ((bf16[2,3,1024,128]{3,2,1,0:T(8,128)(2,1)}), bf16[2,3,1024,128]{3,2,1,0:T(8,128)(2,1)S(1)}, u32[]{:S(2)}, u32[]{:S(2)}) async-start(bf16[2,3,1024,128]{3,2,1,0:T(8,128)(2,1)} %get-tuple-element.40), calls=%async_computation.2 | async-start | bytes 3145728 | tf_op jit(solution)/shard_map/all_to_all | solution.py:368
  92.0 14.2 %collective-permute-start.1 = (bf16[32,512]{1,0:T(8,128)(2,1)S(1)}, bf16[32,512]{1,0:T(8,128)(2,1)S(1)}, u32[]{:S(2)}, u32[]{:S(2)}) collective-permute-start(bf16[32,512]{1,0:T(8,128)(2,1)S(1)} %get-tuple-element.53), channel_id=1, source_target_pairs={{0,1},{1,2},{2,3},{3,0},{4,5},{5,6},{6,7},{7,4},{8,9},{9,10},{10,1... | collective-permute-start | bytes 98312 | tf_op jit(solution)/shard_map/ppermute | solution.py:325
  93.0 13.1 %collective-permute-start.2 = (bf16[32,512]{1,0:T(8,128)(2,1)S(1)}, bf16[32,512]{1,0:T(8,128)(2,1)S(1)}, u32[]{:S(2)}, u32[]{:S(2)}) collective-permute-start(bf16[32,512]{1,0:T(8,128)(2,1)S(1)} %get-tuple-element.55), channel_id=1, source_target_pairs={{0,2},{1,3},{2,0},{3,1},{4,6},{5,7},{6,4},{7,5},{8,10},{9,11},{10,... | collective-permute-start | bytes 98312 | tf_op jit(solution)/shard_map/ppermute | solution.py:325
  94.3 11.9 %collective-permute-start.3 = (bf16[32,512]{1,0:T(8,128)(2,1)S(1)}, bf16[32,512]{1,0:T(8,128)(2,1)S(1)}, u32[]{:S(2)}, u32[]{:S(2)}) collective-permute-start(bf16[32,512]{1,0:T(8,128)(2,1)S(1)} %get-tuple-element.54), channel_id=1, source_target_pairs={{0,3},{1,0},{2,1},{3,2},{4,7},{5,4},{6,5},{7,6},{8,11},{9,8},{10,9... | collective-permute-start | bytes 98312 | tf_op jit(solution)/shard_map/ppermute | solution.py:325
  94.3 1.2 copy-start.3
  95.5 1.0 copy-start.9
  105.3 0.9 copy-start.4
  106.2 20.5 %collective-permute-start.4 = (bf16[32,512]{1,0:T(8,128)(2,1)S(1)}, bf16[32,512]{1,0:T(8,128)(2,1)S(1)}, u32[]{:S(2)}, u32[]{:S(2)}) collective-permute-start(bf16[32,512]{1,0:T(8,128)(2,1)S(1)} %fusion.1), channel_id=1, source_target_pairs={{0,16},{4,20},{8,24},{12,28},{16,0},{20,4},{24,8},{28,12},{1,17},{... | collective-permute-start | bytes 98312 | tf_op jit(solution)/shard_map/ppermute | solution.py:364
  118.0 0.9 copy-start.6
  126.7 1.1 copy-start.5
  127.9 1.1 copy-start.7
  129.0 1.0 copy-start.11
  130.5 1.4 copy-start.2
  131.9 9.8 %collective-permute-start.5 = (bf16[32,512]{1,0:T(8,128)(2,1)S(1)}, bf16[32,512]{1,0:T(8,128)(2,1)S(1)}, u32[]{:S(2)}, u32[]{:S(2)}) collective-permute-start(bf16[32,512]{1,0:T(8,128)(2,1)S(1)} %multiply_convert_fusion), channel_id=1, source_target_pairs={{0,12},{4,0},{8,4},{12,8},{16,28},{20,16},{24,20},{28,24},{1,13},{... | collective-permute-start | bytes 98312 | tf_op jit(solution)/shard_map/ppermute | solution.py:335
  136.6 5.1 %collective-permute-start.6 = (bf16[32,512]{1,0:T(8,128)(2,1)S(1)}, bf16[32,512]{1,0:T(8,128)(2,1)S(1)}, u32[]{:S(2)}, u32[]{:S(2)}) collective-permute-start(bf16[32,512]{1,0:T(8,128)(2,1)S(1)} %multiply_convert_fusion), channel_id=1, source_target_pairs={{0,8},{4,12},{8,0},{12,4},{16,24},{20,28},{24,16},{28,20},{1,9},{5... | collective-permute-start | bytes 98312 | tf_op jit(solution)/shard_map/ppermute | solution.py:335
  136.6 5.1 %collective-permute-start.7 = (bf16[32,512]{1,0:T(8,128)(2,1)S(1)}, bf16[32,512]{1,0:T(8,128)(2,1)S(1)}, u32[]{:S(2)}, u32[]{:S(2)}) collective-permute-start(bf16[32,512]{1,0:T(8,128)(2,1)S(1)} %multiply_convert_fusion), channel_id=1, source_target_pairs={{0,4},{4,8},{8,12},{12,0},{16,20},{20,24},{24,28},{28,16},{1,5},{5... | collective-permute-start | bytes 98312 | tf_op jit(solution)/shard_map/ppermute | solution.py:335
  136.9 29.7 %all-to-all-start.3 = ((bf16[4,2048,128]{2,1,0:T(8,128)(2,1)}), bf16[4,2048,128]{2,1,0:T(8,128)(2,1)S(1)}, u32[]{:S(2)}, u32[]{:S(2)}) async-start(bf16[4,2048,128]{2,1,0:T(8,128)(2,1)} %copy-done.2), calls=%async_computation.3 | async-start | bytes 4194304 | tf_op jit(solution)/shard_map/all_to_all | solution.py:357
  141.8 4.9 %collective-permute-start.8 = (bf16[4,32,512]{2,1,0:T(8,128)(2,1)S(1)}, bf16[4,32,512]{2,1,0:T(8,128)(2,1)S(1)}, u32[]{:S(2)}, u32[]{:S(2)}) collective-permute-start(bf16[4,32,512]{2,1,0:T(8,128)(2,1)S(1)} %constant_dynamic-slice_fusion), channel_id=1, source_target_pairs={{0,3},{1,0},{2,1},{3,2},{4,7},{5,4},{6,5},{7,6},{8,11},{9,8},{10,9... | collective-permute-start | bytes 393224 | tf_op jit(solution)/shard_map/ppermute | solution.py:335
  143.7 5.4 %collective-permute-start.9 = (bf16[4,32,512]{2,1,0:T(8,128)(2,1)S(1)}, bf16[4,32,512]{2,1,0:T(8,128)(2,1)S(1)}, u32[]{:S(2)}, u32[]{:S(2)}) collective-permute-start(bf16[4,32,512]{2,1,0:T(8,128)(2,1)S(1)} %constant_dynamic-slice_fusion), channel_id=1, source_target_pairs={{0,2},{1,3},{2,0},{3,1},{4,6},{5,7},{6,4},{7,5},{8,10},{9,11},{10,... | collective-permute-start | bytes 393224 | tf_op jit(solution)/shard_map/ppermute | solution.py:335
  143.7 5.9 %collective-permute-start.10 = (bf16[4,32,512]{2,1,0:T(8,128)(2,1)S(1)}, bf16[4,32,512]{2,1,0:T(8,128)(2,1)S(1)}, u32[]{:S(2)}, u32[]{:S(2)}) collective-permute-start(bf16[4,32,512]{2,1,0:T(8,128)(2,1)S(1)} %constant_dynamic-slice_fusion), channel_id=1, source_target_pairs={{0,1},{1,2},{2,3},{3,0},{4,5},{5,6},{6,7},{7,4},{8,9},{9,10},{10,1... | collective-permute-start | bytes 393224 | tf_op jit(solution)/shard_map/ppermute | solution.py:335
  149.1 17.6 %copy-start.8 = (bf16[512,512]{1,0:T(8,128)(2,1)S(1)}, bf16[512,512]{1,0:T(8,128)(2,1)}, u32[]{:S(2)}) copy-start(bf16[512,512]{1,0:T(8,128)(2,1)} %w_ref.3) | copy-start | bytes 1572868

commit v5 on v4

--- a/solution.py
+++ b/solution.py
@@ -33,7 +33,7 @@
 
 
 def pack_kernel(near_ref, *refs):
-    sources, out_ref, held, arrived = refs[:3], refs[3], refs[4:7], refs[7]
+    sources, (out_ref, spread_ref, *direct), held, arrived = refs[:5], refs[5:-6], refs[-6:-1], refs[-1]
     copies = [
         pltpu.make_async_copy(source, target, arrived.at[i])
         for i, (source, target) in enumerate(zip(sources, held))
@@ -42,7 +42,7 @@
         copy.start()
     for copy in copies:
         copy.wait()
-    q_ref, k_ref, v_ref = held
+    q_ref, k_ref, v_ref, g_ref, w_ref = held
     rows = q_ref.shape[0]
     width = q_ref.shape[1] // HEADS
     half = rows // 2
@@ -51,24 +51,35 @@
     offsets = jnp.zeros((16, 2 * width), F32)
     for e in range(NBR):
         offsets = jnp.where(line == e, (near_ref[0, e] - here + REACH).astype(F32), offsets)
+    d_attn = lax.dot_general(
+        g_ref[...], w_ref[...], (((1,), (1,)), ((), ())), preferred_element_type=F32
+    ).astype(BF16)
     for h in range(HEADS):
         to, i = divmod(h, MINE)
         cols = slice(h * width, (h + 1) * width)
         at_q = MINE * rows + i * half
+        at_d = MINE * (rows + half) + i * half
         out_ref[to, i * rows : (i + 1) * rows, :] = jnp.concatenate(
             [k_ref[:, cols], v_ref[:, cols]], axis=1
         )
         out_ref[to, at_q : at_q + half, :] = jnp.concatenate(
             [q_ref[:half, cols], q_ref[half:, cols]], axis=1
         )
-        out_ref[to, MINE * (rows + half) :, :] = offsets.astype(BF16)
+        out_ref[to, at_d : at_d + half, :] = jnp.concatenate(
+            [d_attn[:half, cols], d_attn[half:, cols]], axis=1
+        )
+        out_ref[to, MINE * (rows + 2 * half) :, :] = offsets.astype(BF16)
+    for to in range(GROUP):
+        spread_ref[to] = g_ref[...]
+    for by, ref in enumerate(direct):
+        ref[...] = out_ref[(here % GROUP) ^ by, : MINE * rows, :]
 
 
 def list_units(near_ref, patch_of, block_of, count, first, outside, right=0, base=0):
     for p in range(GROUP):
         if not outside:
             patch_of[count] = first + p
-            block_of[count] = first + p
+            block_of[count] = base + p
             count = count + 1
         for e in range(NBR):
             t = p + near_ref[p, e] - REACH
@@ -79,7 +90,7 @@
                 block_of[count] = base + jnp.where(t < 0, t + REACH, t - GROUP + right)
             else:
                 want = jnp.logical_and(inside, t != p)
-                block_of[count] = first + t
+                block_of[count] = base + t
             count = count + jnp.where(want, 1, 0)
     return count
 
@@ -154,13 +165,13 @@
         q_scr[at + p, width:, :] = jnp.zeros_like(turned)
 
 
-def fill_back(x_ref, d_ref, head, rows, width, d_scr, back_scr, at=0):
+def fill_back(x_ref, head, rows, width, d_scr, back_scr, at=0):
     half = rows // 2
     start = MINE * rows + head * half
     blank = jnp.zeros((half, width), BF16)
     for p in range(GROUP):
         q_pair = x_ref[p, start : start + half, :]
-        d_pair = d_ref[p, head * half : (head + 1) * half, :]
+        d_pair = x_ref[p, start + MINE * half : start + (MINE + 1) * half, :]
         back_scr[at + p, :half, :] = jnp.concatenate([q_pair[:, :width], blank], axis=1)
         back_scr[at + p, half:rows, :] = jnp.concatenate([q_pair[:, width:], blank], axis=1)
         back_scr[at + p, rows : rows + half, :] = jnp.concatenate([blank, d_pair[:, :width]], axis=1)
@@ -170,83 +181,82 @@
         d_scr[at + p, width:, :] = d_turned * BF16(1.0 / math.sqrt(width))
 
 
-def near_kernel(near_ref, x_ref, o_ref, m_ref, s0, s1, before_scr, top_scr, q_scr, v_scr, patch_of, block_of):
-    rows, width = s0.shape[0], x_ref.shape[2] // 2
-    total = jnp.int32(0)
+def attend_kernel(alone, near_ref, x_ref, *refs):
+    halos, refs = refs[: GROUP if alone else 1], refs[GROUP if alone else 1 :]
+    (attn_ref, lse_ref, delta_ref, dq_ref, out_ref, acc, s0, s1, before_scr, top_scr, m_scr, o_scr, q_scr, d_scr, back_scr, v_scr, k_scr, kv_scr, patch_of, block_of, far_patch, far_block) = refs
+    rows, width = q_scr.shape[2], x_ref.shape[2] // 2
+    half, halo = rows // 2, REACH if alone else 2 * REACH
+    blocks = GROUP + halo
+    right = halo - REACH
+    other = 1 - lax.axis_index("seg") // GROUP if alone else 0
+    for b in range(GROUP):
+        kv_scr[b] = x_ref[b, : MINE * rows, :]
+    for b in range(halo):
+        if alone:
+            by = (b + 1 - other) ^ (lax.axis_index("seg") % GROUP)
+            for k in range(GROUP):
+
+                @pl.when(by == k)
+                def _():
+                    kv_scr[GROUP + b] = halos[k][...]
+
+        else:
+            kv_scr[GROUP + b] = halos[0][b]
+    total, far_total = jnp.int32(0), jnp.int32(0)
     for i in range(MINE):
-        total = list_units(near_ref, patch_of, block_of, total, i * GROUP, False)
+        base = i * blocks
+        total = list_units(near_ref, patch_of, block_of, total, i * GROUP, False, 0, base)
+        total = list_units(near_ref, patch_of, block_of, total, i * GROUP, True, right, base + GROUP)
+        far_total = list_units(
+            near_ref, far_patch, far_block, far_total, i * GROUP, True, right, base + GROUP
+        )
         fill_q(x_ref, i, rows, width, q_scr, i * GROUP)
-        for b in range(GROUP):
-            turned = x_ref[b, i * rows : (i + 1) * rows, :].T
-            v_scr[i * GROUP + b, :width, :] = turned[width:]
-            v_scr[i * GROUP + b, width:, :] = jnp.ones((v_scr.shape[1] - width, rows), BF16)
-    o_ref[...] = jnp.zeros_like(o_ref)
-    m_ref[...] = jnp.full_like(m_ref, -jnp.inf)
+        fill_back(x_ref, i, rows, width, d_scr, back_scr, i * GROUP)
+        for b in range(blocks):
+            turned = kv_scr[b, i * rows : (i + 1) * rows, :].T
+            v_scr[base + b, :width, :] = turned[width:]
+            v_scr[base + b, width:, :] = jnp.ones((v_scr.shape[1] - width, rows), BF16)
+            if b >= GROUP:
+                k_scr[base + b] = turned[:width]
+    o_scr[...] = jnp.zeros_like(o_scr)
+    m_scr[...] = jnp.full_like(m_scr, -jnp.inf)
 
     def keys(b):
-        return x_ref[b % GROUP, pl.ds(pl.multiple_of(b // GROUP * rows, rows), rows), :]
-
-    mix_units(total, patch_of, block_of, keys, q_scr, v_scr, (s0, s1), before_scr, top_scr, m_ref, o_ref)
-
-
-def far_kernel(right, near_ref, x_ref, g_ref, w_ref, halo_ref, o_in, m_in, attn_ref, lse_ref, delta_ref, dq_ref, d_ref, term_ref, out_ref, acc, s0, s1, before_scr, top_scr, m_scr, o_scr, q_scr, d_scr, back_scr, v_scr, k_scr, patch_of, block_of):
-    rows, width = q_scr.shape[2], x_ref.shape[2] // 2
-    half, halo = rows // 2, halo_ref.shape[0]
-    me = lax.axis_index("seg")
-    other = 1 - me // GROUP if out_ref.shape[0] == 2 else 0
-    place = me % GROUP * MINE * width
-    mine = w_ref[pl.ds(pl.multiple_of(place, MINE * width), MINE * width), :]
-    for p in range(GROUP):
-        d_attn = lax.dot_general(
-            mine, g_ref[p], (((1,), (1,)), ((), ())), preferred_element_type=F32
-        ).astype(BF16)
-        for i in range(MINE):
-            d_ref[p, i * half : (i + 1) * half, :] = beside(d_attn[i * width : (i + 1) * width])
-    total = jnp.int32(0)
-    for i in range(MINE):
-        total = list_units(near_ref, patch_of, block_of, total, i * GROUP, True, right, i * halo)
-        fill_q(x_ref, i, rows, width, q_scr, i * GROUP)
-        fill_back(x_ref, d_ref, i, rows, width, d_scr, back_scr, i * GROUP)
-        for b in range(halo):
-            turned = halo_ref[b, i * rows : (i + 1) * rows, :].T
-            k_scr[i * halo + b] = turned[:width]
-            v_scr[i * halo + b, :width, :] = turned[width:]
-            v_scr[i * halo + b, width:, :] = jnp.ones((v_scr.shape[1] - width, rows), BF16)
-    o_scr[...] = o_in[...]
-    m_scr[...] = m_in[...]
-
-    def keys(b):
-        return halo_ref[b % halo, pl.ds(pl.multiple_of(b // halo * rows, rows), rows), :]
+        return kv_scr[b % blocks, pl.ds(pl.multiple_of(b // blocks * rows, rows), rows), :]
 
     firsts = (s0.at[:, :rows], s1.at[:, :rows])
     mix_units(total, patch_of, block_of, keys, q_scr, v_scr, firsts, before_scr, top_scr, m_scr, o_scr)
-    attns = []
     for p in range(MINE * GROUP):
         sums = o_scr[p, width : width + 1, :]
         attn = (o_scr[p, :width, :] * (1.0 / sums)).astype(BF16)
-        attns.append(attn)
         attn_ref[p % GROUP, p // GROUP * half : (p // GROUP + 1) * half, :] = beside(attn)
         lse_ref[p] = m_scr[p] + jnp.log(sums)
         product = d_scr[p, width:, :].astype(F32) * attn.astype(F32)
         delta_ref[p] = jnp.sum(product, axis=0, keepdims=True)
+    for i in range(MINE):
+        for b in range(halo):
+            acc[i * blocks + GROUP + b] = jnp.zeros(acc.shape[1:], F32)
+    dq_ref[...] = jnp.zeros_like(dq_ref)
+    back_units(far_total, far_patch, far_block, keys, q_scr, d_scr, back_scr, k_scr, (s0, s1), lse_ref, delta_ref, dq_ref, acc)
+    for i in range(MINE):
+        for b in range(halo):
+            out_ref[b, i * rows : (i + 1) * rows, :] = acc[i * blocks + GROUP + b].astype(BF16)
+
+
+def term_kernel(attn_ref, g_ref, term_ref):
+    half = attn_ref.shape[1] // MINE
     term = jnp.zeros(term_ref.shape, F32)
     for p in range(GROUP):
-        rows_here = jnp.concatenate([attns[i * GROUP + p] for i in range(MINE)], axis=0)
-        term = term + mm(rows_here, g_ref[p])
+        turned = [halves(attn_ref[p, i * half : (i + 1) * half, :]) for i in range(MINE)]
+        term = term + mm(jnp.concatenate(turned, axis=0), g_ref[p])
     term_ref[...] = term.astype(BF16)
-    acc[...] = jnp.zeros_like(acc)
-    dq_ref[...] = jnp.zeros_like(dq_ref)
-    back_units(total, patch_of, block_of, keys, q_scr, d_scr, back_scr, k_scr, (s0, s1), lse_ref, delta_ref, dq_ref, acc)
-    for i in range(MINE):
-        for b in range(halo):
-            out_ref[other, b, i * rows : (i + 1) * rows, :] = acc[i * halo + b].astype(BF16)
-
-
-def own_kernel(head, near_ref, x_ref, d_ref, lse_ref, delta_ref, dq_in, out_ref, acc, s0, s1, dq_scr, q_scr, d_scr, back_scr, k_scr, patch_of, block_of):
+
+
+def own_kernel(head, near_ref, x_ref, lse_ref, delta_ref, dq_in, out_ref, acc, s0, s1, dq_scr, q_scr, d_scr, back_scr, k_scr, patch_of, block_of):
     rows, width = q_scr.shape[2], x_ref.shape[2] // 2
     total = list_units(near_ref, patch_of, block_of, jnp.int32(0), 0, False)
     fill_q(x_ref, head, rows, width, q_scr, 0)
-    fill_back(x_ref, d_ref, head, rows, width, d_scr, back_scr)
+    fill_back(x_ref, head, rows, width, d_scr, back_scr)
     mine = slice(head * rows, (head + 1) * rows)
     for b in range(GROUP):
         k_scr[b] = x_ref[b, mine, :].T[:width]
@@ -271,10 +281,10 @@
             out_ref[p, i * each : (i + 1) * each, :] = owns[i][p]
         mine = slice(i * each, i * each + rows)
         other = 1 - lax.axis_index("seg") // GROUP if alone else 0
-        for side in range(back_ref.shape[1] // REACH):
+        for side in range(back_ref.shape[0] // REACH):
             start = other if alone else 1 - side
             for j in range(REACH):
-                term = back_ref[other, side * REACH + j, i * rows : (i + 1) * rows, :].astype(F32)
+                term = back_ref[side * REACH + j, i * rows : (i + 1) * rows, :].astype(F32)
                 here = out_ref[start + j, mine, :].astype(F32)
                 out_ref[start + j, mine, :] = (here + term).astype(BF16)
 
@@ -378,65 +388,58 @@
             name=name,
         )
 
-    packed = pl.pallas_call(
+    packed, spread, *direct = pl.pallas_call(
         pack_kernel,
-        in_specs=[smem] + [pl.BlockSpec(memory_space=pltpu.HBM)] * 3,
-        scratch_shapes=[pltpu.VMEM((rows, model), BF16)] * 3 + [pltpu.SemaphoreType.DMA((3,))],
-        out_shape=jax.ShapeDtypeStruct((GROUP, MINE * (rows + half) + 16, wide), BF16),
-        compiler_params=params(),
+        in_specs=[smem] + [pl.BlockSpec(memory_space=pltpu.HBM)] * 5,
+        scratch_shapes=[pltpu.VMEM((rows, model), BF16)] * 4
+        + [pltpu.VMEM((model, model), BF16), pltpu.SemaphoreType.DMA((5,))],
+        out_shape=[
+            jax.ShapeDtypeStruct((GROUP, MINE * (rows + 2 * half) + 16, wide), BF16),
+            jax.ShapeDtypeStruct((GROUP, rows, model), BF16),
+        ]
+        + [jax.ShapeDtypeStruct((MINE * rows, wide), BF16)] * (GROUP if alone else 0),
+        compiler_params=params(60),
         cost_estimate=cost(2 * rows * model * model, 10 * rows * model),
         name="pack",
-    )(neighbours[0], *(in_hbm(a) for a in (queries[0], key_rows[0], value_rows[0])))
+    )(
+        neighbours[0],
+        *(in_hbm(a) for a in (queries[0], key_rows[0], value_rows[0], grad_out[0], w_out)),
+    )
     x = swap(packed)
-    at = MINE * (rows + half)
+    if alone:
+        border = [g * GROUP + i for g in range(2) for i in range(1 - g, 1 - g + REACH)]
+        beyond = [
+            lax.ppermute(array, "seg", [(s, (s + GROUP) % seg ^ by) for s in border])
+            for by, array in enumerate(direct)
+        ]
+    else:
+        kv = x[:, : MINE * rows]
+        beyond = [
+            jnp.concatenate([shifted(kv[1:], GROUP), shifted(kv[:REACH], -GROUP)], axis=0)
+        ]
+    at = MINE * (rows + 2 * half)
     near = x[:, at : at + NBR, 0].astype(jnp.int32)
-    copies = jnp.broadcast_to(grad_out, (GROUP, rows, model))
-    x, near, copies = lax.optimization_barrier((x, near, copies))
-    kv = x[:, : MINE * rows]
-    if alone:
-        first = 1 - lax.axis_index("seg") // GROUP
-        beyond = lax.dynamic_slice_in_dim(kv, first, REACH, 0)
-        beyond = across(beyond)
-    else:
-        beyond = jnp.concatenate([shifted(kv[1:], GROUP), shifted(kv[:REACH], -GROUP)], axis=0)
-    grads_here = swap(copies)
+    x, near, beyond, spread = lax.optimization_barrier((x, near, beyond, spread))
+    grads_here = swap(spread)
 
     lists = lambda count: [pltpu.SMEM((count + 8,), jnp.int32)] * 2
     sheet = pltpu.VMEM((rows, rows), F32)
     double = pltpu.VMEM((rows, 2 * rows), F32)
     lines = lambda count: pltpu.VMEM((count, 1, rows), F32)
     patches = MINE * GROUP
-    o_state, m_state = call(
-        near_kernel,
-        "near",
-        [((patches, width + ones, rows), F32), ((patches, 1, rows), F32)],
-        [
-            sheet,
-            sheet,
-            lines(MINE * most),
-            lines(MINE * most),
-            pltpu.VMEM((patches, wide, rows), BF16),
-            pltpu.VMEM((patches, width + ones, rows), BF16),
-        ]
-        + lists(MINE * most),
-        20 * unit_cost * 512,
-        20 * unit_cost,
-    )(near, x)
-
-    attn, lse, delta, dq, d, w_term, far = call(
-        functools.partial(far_kernel, halo - REACH),
-        "far",
+    blocks = GROUP + halo
+    attn, lse, delta, dq, far = call(
+        functools.partial(attend_kernel, alone),
+        "attend",
         [
             ((GROUP, MINE * half, wide), BF16),
             ((patches, 1, rows), F32),
             ((patches, 1, rows), F32),
             ((patches, width, rows), F32),
-            ((GROUP, MINE * half, wide), BF16),
-            ((MINE * width, model), BF16),
-            ((2 if alone else 1, halo, MINE * rows, wide), BF16),
+            ((halo, MINE * rows, wide), BF16),
         ],
         [
-            pltpu.VMEM((MINE * halo, rows, wide), F32),
+            pltpu.VMEM((MINE * blocks, rows, wide), F32),
             double,
             double,
             lines(MINE * most),
@@ -446,20 +449,21 @@
             pltpu.VMEM((patches, wide, rows), BF16),
             pltpu.VMEM((patches, wide, rows), BF16),
             pltpu.VMEM((patches, 2 * rows, wide), BF16),
-            pltpu.VMEM((MINE * halo, width + ones, rows), BF16),
-            pltpu.VMEM((MINE * halo, width, rows), BF16),
+            pltpu.VMEM((MINE * blocks, width + ones, rows), BF16),
+            pltpu.VMEM((MINE * blocks, width, rows), BF16),
+            pltpu.VMEM((blocks, MINE * rows, wide), BF16),
         ]
+        + lists(MINE * most)
         + lists(MINE * most),
         6 * unit_cost * 1536,
         12 * unit_cost,
         60,
-    )(near, x, grads_here, w_out, beyond, o_state, m_state)
+    )(near, x, *beyond)
     if alone:
-        back = between(far)
+        back = across(far)
     else:
-        far = far[0]
         back = jnp.concatenate([shifted(far[:REACH], -GROUP), shifted(far[REACH:], GROUP)], axis=0)
-        back = back[None]
+
     def own_terms(i, lse, delta, dq):
         return call(
             functools.partial(own_kernel, i),
@@ -478,9 +482,12 @@
             + lists(most),
             10 * unit_cost * 1280,
             10 * unit_cost,
-        )(near, x, d, lse, delta, dq)[0]
+        )(near, x, lse, delta, dq)[0]
 
     part = MINE * width // samples
+    (w_term,) = call(
+        term_kernel, "term", [((MINE * width, model), BF16)], [], 2 * rows * model * model
+    )(attn, grads_here)
     w_part = exchange(w_term.reshape(samples, part, model), "sample")
     w_part = jnp.sum(w_part.astype(F32), axis=0).astype(BF16)
     own0 = own_terms(0, lse, delta, dq)

time: 169 us -> 162 us (0.959)
  the two profiles are of different devices: /device:TPU:13 before, /device:TPU:0 now
where the time goes in v5:
time: 162 us; the launch traced here: 160 us
  waiting for transfers between devices  65.4 us (40%)
  Pallas kernels  44.4 us (27%)
  starting transfers between devices  43 us (27%)
  local copies, waits for them, and re-layouts  4.56 us (3%)
  other arithmetic  2.04 us (1%)
    all_to_all x3, waiting for transfers between devices, swap(): return lax.all_to_all(array, 'seg', 0, 0, axis_index_groups=split)  48.3 us
    pallas_call x2, Pallas kernels, own_terms(): call(functools.partial(own_kernel, i), f'own{i}', [((GROUP, rows + half,...  18.7 us
    all_to_all x3, starting transfers between devices, swap(): return lax.all_to_all(array, 'seg', 0, 0, axis_index_groups=split)  17.4 us
    pallas_call x1, Pallas kernels, body(): call(functools.partial(attend_kernel, alone), 'attend', [((GROUP, MINE *...  15.5 us
    ppermute x4, waiting for transfers between devices, body(): lax.ppermute(array, 'seg', [(s, (s + GROUP) % seg ^ by) for s in border])  8.22 us
    ppermute x3, starting transfers between devices, exchange(): lax.ppermute(piece, axis, around(count, by))  8.06 us
    ppermute x2, starting transfers between devices, across(): lax.ppermute(array, 'seg', [(s, (s + GROUP) % seg) for s in range(seg)])  6.8 us
    ppermute x6, starting transfers between devices, gathered(): arrived.append(lax.ppermute(piece, axis, pairs))  6.16 us
  transfers between devices with their start and end apart: 18, of which 7 were waited for; matrix products, arithmetic and copies ran while one was open for 1% of the time, Pallas kernels for 23%

profile of v5, /device:TPU:0, one launch (start us, length us, event | category | flops | bytes accessed | tf_op | source)
XLA Modules:
  0.0 160.4 jit_solution(5663727498263722126)
XLA Ops:
  0.6 5.4 %pack.1 = (bf16[4,2064,128]{2,1,0:T(8,128)(2,1)}, bf16[4,512,512]{2,1,0:T(8,128)(2,1)}, bf16[1024,128]{1,0:T(8,128)(2,1)}, bf16[1024,128]{1,0:T(8,128)(2,1)}, bf...) custom-call(s32[1,3]{1,0:T(1,128)} %bitcast.60, bf16[512,512]{1,0:T(8,128)(2,1)} %bitcast.56, ...), custom_call_target="tpu_custom_call" | custom-call | flops 268435 | bytes 2621 | tf_op jit(solution)/shard_map/pack/pallas_call | solution.py:391
  6.1 0.0 copy-start.14
  6.1 5.4 %all-to-all-start = ((bf16[4,2064,128]{2,1,0:T(8,128)(2,1)}), bf16[4,2064,128]{2,1,0:T(8,128)(2,1)S(1)}, u32[]{:S(2)}, u32[]{:S(2)}) async-start(bf16[4,2064,128]{2,1,0:T(8,128)(2,1)} %get-tuple-element.35), calls=%async_computation | async-start | bytes 4227072 | tf_op jit(solution)/shard_map/all_to_all | solution.py:367
  11.4 1.3 collective-permute-start
  12.7 1.3 collective-permute-start.1
  14.0 1.3 collective-permute-start.2
  15.3 0.7 collective-permute-start.3
  16.0 31.7 %all-to-all-done.x_ref = bf16[4,2064,128]{2,1,0:T(8,128)(2,1)S(1)} async-done(((bf16[4,2064,128]{2,1,0:T(8,128)(2,1)}), bf16[4,2064,128]{2,1,0:T(8,128)(2,1)S(1)}, u32[]{:S(2)}, u32[]{:S(2)}) %all-to-all-start) | async-done | bytes 2113568 | tf_op jit(solution)/shard_map/all_to_all | solution.py:367
  47.8 0.9 convert_reduce_fusion.near_ref
  48.7 0.0 collective-permute-done.refs_0_
  48.7 0.0 collective-permute-done.1.refs_1_
  48.7 8.2 %collective-permute-done.2.refs_2_ = bf16[1024,128]{1,0:T(8,128)(2,1)S(1)} collective-permute-done((bf16[1024,128]{1,0:T(8,128)(2,1)}, bf16[1024,128]{1,0:T(8,128)(2,1)S(1)}, u32[]{:S(2)}, u32[]{:S(2)}) %collective-permute-start.2) | collective-permute-done | bytes 262176 | tf_op jit(solution)/shard_map/ppermute | solution.py:412
  56.9 0.7 copy-done.12
  57.6 0.1 copy-done.13
  57.7 7.9 %all-to-all-start.1 = ((bf16[4,512,512]{2,1,0:T(8,128)(2,1)}), bf16[4,512,512]{2,1,0:T(8,128)(2,1)}, u32[]{:S(2)}, u32[]{:S(2)}) async-start(bf16[4,512,512]{2,1,0:T(8,128)(2,1)} %get-tuple-element.48), calls=%async_computation.1 | async-start | bytes 4194304 | tf_op jit(solution)/shard_map/all_to_all | solution.py:367
  65.5 15.5 %attend.1 = (bf16[4,512,128]{2,1,0:T(8,128)(2,1)}, f32[8,1,512]{2,1,0:T(1,128)}, f32[8,1,512]{2,1,0:T(1,128)}, f32[8,64,512]{2,1,0:T(8,128)}, bf16[3,1024,128]{2,1,0:T(8,128)(2,1)}) custom-call(s32[4,3]{1,0:T(4,128)} %convert_reduce_fusion.near_ref, bf16[4,2064,128]{2,1,0:T(8,128)(2,1)} %copy-done, bf16[1024,128]{1,0:T(8,128)(2,1)} %copy-done.10, ...), custom_call_target="tpu_custom_call" | custom-call | flops 2415919 | bytes 4194 | tf_op jit(solution)/shard_map/attend/pallas_call | solution.py:431
  81.0 6.7 %collective-permute-start.8 = (bf16[3,1024,128]{2,1,0:T(8,128)(2,1)}, bf16[3,1024,128]{2,1,0:T(8,128)(2,1)S(1)}, u32[]{:S(2)}, u32[]{:S(2)}) collective-permute-start(bf16[3,1024,128]{2,1,0:T(8,128)(2,1)} %get-tuple-element.53), channel_id=1, source_target_pairs={{0,16},{4,20},{8,24},{12,28},{16,0},{20,4},{24,8},{28,12},{1,17},{... | collective-permute-start | bytes 2359304 | tf_op jit(solution)/shard_map/ppermute | solution.py:374
  87.7 2.4 %all-to-all-done.1.g_ref = bf16[4,512,512]{2,1,0:T(8,128)(2,1)} async-done(((bf16[4,512,512]{2,1,0:T(8,128)(2,1)}), bf16[4,512,512]{2,1,0:T(8,128)(2,1)}, u32[]{:S(2)}, u32[]{:S(2)}) %all-to-all-start.1) | async-done | bytes 2097184 | tf_op jit(solution)/shard_map/all_to_all | solution.py:367
  90.1 1.0 copy-done.5
  91.2 2.1 %term.1 = bf16[128,512]{1,0:T(8,128)(2,1)S(1)} custom-call(bf16[4,512,128]{2,1,0:T(8,128)(2,1)S(1)} %copy-done.5, bf16[4,512,512]{2,1,0:T(8,128)(2,1)} %all-to-all-done.1.g_ref), custom_call_target="tpu_custom_call" | custom-call | flops 268435 | bytes 4194 | tf_op jit(solution)/shard_map/term/pallas_call | solution.py:488
  93.3 0.1 collective-permute-start.4
  93.4 1.7 %collective-permute-start.6 = (bf16[32,512]{1,0:T(8,128)(2,1)S(1)}, bf16[32,512]{1,0:T(8,128)(2,1)S(1)}, u32[]{:S(2)}, u32[]{:S(2)}) collective-permute-start(bf16[32,512]{1,0:T(8,128)(2,1)S(1)} %get-tuple-element.66), channel_id=1, source_target_pairs={{0,3},{1,0},{2,1},{3,2},{4,7},{5,4},{6,5},{7,6},{8,11},{9,8},{10,9... | collective-permute-start | bytes 98312 | tf_op jit(solution)/shard_map/ppermute | solution.py:335
  95.1 6.3 %collective-permute-start.5 = (bf16[32,512]{1,0:T(8,128)(2,1)S(1)}, bf16[32,512]{1,0:T(8,128)(2,1)S(1)}, u32[]{:S(2)}, u32[]{:S(2)}) collective-permute-start(bf16[32,512]{1,0:T(8,128)(2,1)S(1)} %get-tuple-element.67), channel_id=1, source_target_pairs={{0,2},{1,3},{2,0},{3,1},{4,6},{5,7},{6,4},{7,5},{8,10},{9,11},{10,... | collective-permute-start | bytes 98312 | tf_op jit(solution)/shard_map/ppermute | solution.py:335
  101.4 0.0 copy-start.3
  101.4 1.2 copy-done.3
  102.6 9.4 %own0.1.refs_0_ = bf16[4,768,128]{2,1,0:T(8,128)(2,1)S(1)} custom-call(s32[4,3]{1,0:T(4,128)S(1)} %copy-done.9, bf16[4,2064,128]{2,1,0:T(8,128)(2,1)S(1)} %copy-done.1, f32[8,1,512]{2,1,0:T(1,128)S(1)} %copy-done.7, f32[8,1,512]{2,1,0:T(1,128)S(1)} %copy-done.8, f32[8,64,512]{2,1,0:T(8,128)S(1)} %copy-done.3), custom_call_target="tpu_custom_call" | custom-call | flops 3355443 | bytes 4194 | tf_op jit(solution)/shard_map/own0/pallas_call | solution.py:468
  112.1 0.0 collective-permute-done.6
  112.1 0.0 collective-permute-done.5
  112.1 0.0 copy-start.6
  112.1 0.1 collective-permute-start.7
  112.2 9.3 %own1.1.refs_1_ = bf16[4,768,128]{2,1,0:T(8,128)(2,1)S(1)} custom-call(s32[4,3]{1,0:T(4,128)S(1)} %copy-done.9, bf16[4,2064,128]{2,1,0:T(8,128)(2,1)S(1)} %copy-done.1, f32[8,1,512]{2,1,0:T(1,128)S(1)} %copy-done.7, f32[8,1,512]{2,1,0:T(1,128)S(1)} %copy-done.8, f32[8,64,512]{2,1,0:T(8,128)S(1)} %copy-done.3), custom_call_target="tpu_custom_call" | custom-call | flops 3355443 | bytes 4194 | tf_op jit(solution)/shard_map/own1/pallas_call | solution.py:468
  121.4 3.1 %collective-permute-done.7 = bf16[32,512]{1,0:T(8,128)(2,1)S(1)} collective-permute-done((bf16[32,512]{1,0:T(8,128)(2,1)S(1)}, bf16[32,512]{1,0:T(8,128)(2,1)S(1)}, u32[]{:S(2)}, u32[]{:S(2)}) %collective-permute-start.7) | collective-permute-done | bytes 32800 | tf_op jit(solution)/shard_map/ppermute | solution.py:374
  124.5 0.0 collective-permute-done.8.refs_2_
  124.6 0.4 merge.1
  125.0 1.3 copy-done.2
  126.4 0.6 collective-permute-start.9
  127.0 1.5 collective-permute-start.11
  128.4 0.6 collective-permute-start.10
  129.0 4.2 %all-to-all-start.2 = ((bf16[4,2048,128]{2,1,0:T(8,128)(2,1)}), bf16[4,2048,128]{2,1,0:T(8,128)(2,1)S(1)}, u32[]{:S(2)}, u32[]{:S(2)}) async-start(bf16[4,2048,128]{2,1,0:T(8,128)(2,1)} %copy-done.2), calls=%async_computation.2 | async-start | bytes 4194304 | tf_op jit(solution)/shard_map/all_to_all | solution.py:367
  133.2 0.0 collective-permute-done.10
  133.3 0.0 copy-start.4
  133.4 3.0 %collective-permute-start.12 = (bf16[4,32,512]{2,1,0:T(8,128)(2,1)S(1)}, bf16[4,32,512]{2,1,0:T(8,128)(2,1)S(1)}, u32[]{:S(2)}, u32[]{:S(2)}) collective-permute-start(bf16[4,32,512]{2,1,0:T(8,128)(2,1)S(1)} %constant_dynamic-slice_fusion), channel_id=1, source_target_pairs={{0,3},{1,0},{2,1},{3,2},{4,7},{5,4},{6,5},{7,6},{8,11},{9,8},{10,9... | collective-permute-start | bytes 393224 | tf_op jit(solution)/shard_map/ppermute | solution.py:345
  136.4 0.5 collective-permute-start.13
  136.9 2.2 %collective-permute-done.12 = bf16[4,32,512]{2,1,0:T(8,128)(2,1)S(1)} collective-permute-done((bf16[4,32,512]{2,1,0:T(8,128)(2,1)S(1)}, bf16[4,32,512]{2,1,0:T(8,128)(2,1)S(1)}, u32[]{:S(2)}, u32[]{:S(2)}) %collective-permute-start.12) | collective-permute-done | bytes 131104 | tf_op jit(solution)/shard_map/ppermute | solution.py:345
  139.1 3.6 %collective-permute-done.13 = bf16[4,32,512]{2,1,0:T(8,128)(2,1)S(1)} collective-permute-done((bf16[4,32,512]{2,1,0:T(8,128)(2,1)S(1)}, bf16[4,32,512]{2,1,0:T(8,128)(2,1)S(1)}, u32[]{:S(2)}, u32[]{:S(2)}) %collective-permute-start.13) | collective-permute-done | bytes 131104 | tf_op jit(solution)/shard_map/ppermute | solution.py:345
  142.9 1.1 dynamic-slice_convert_fusion
  144.0 14.1 %all-to-all-done.2.y_ref = bf16[4,2048,128]{2,1,0:T(8,128)(2,1)S(1)} async-done(((bf16[4,2048,128]{2,1,0:T(8,128)(2,1)}), bf16[4,2048,128]{2,1,0:T(8,128)(2,1)S(1)}, u32[]{:S(2)}, u32[]{:S(2)}) %all-to-all-start.2) | async-done | bytes 2097184 | tf_op jit(solution)/shard_map/all_to_all | solution.py:367
  158.1 2.3 %unpack.1 = (bf16[512,512]{1,0:T(8,128)(2,1)}, bf16[512,512]{1,0:T(8,128)(2,1)}, bf16[512,512]{1,0:T(8,128)(2,1)}, bf16[512,512]{1,0:T(8,128)(2,1)}) custom-call(bf16[4,2048,128]{2,1,0:T(8,128)(2,1)S(1)} %all-to-all-done.2.y_ref, bf16[512,512]{1,0:T(8,128)(2,1)S(1)} %copy-done.4), custom_call_target="tpu_custom_call" | custom-call | flops 268435 | bytes 4194 | tf_op jit(solution)/shard_map/unpack/pallas_call | solution.py:515
  (48 shorter events, 0.3 us)
Async XLA Ops:
  6.1 9.3 %copy-start.14 = (bf16[1024,128]{1,0:T(8,128)(2,1)S(1)}, bf16[1024,128]{1,0:T(8,128)(2,1)}, u32[]{:S(2)}) copy-start(bf16[1024,128]{1,0:T(8,128)(2,1)} %get-tuple-element.39) | copy-start | bytes 786436
  6.1 41.7 %all-to-all-start = ((bf16[4,2064,128]{2,1,0:T(8,128)(2,1)}), bf16[4,2064,128]{2,1,0:T(8,128)(2,1)S(1)}, u32[]{:S(2)}, u32[]{:S(2)}) async-start(bf16[4,2064,128]{2,1,0:T(8,128)(2,1)} %get-tuple-element.35), calls=%async_computation | async-start | bytes 4227072 | tf_op jit(solution)/shard_map/all_to_all | solution.py:367
  11.4 37.2 %collective-permute-start = (bf16[1024,128]{1,0:T(8,128)(2,1)}, bf16[1024,128]{1,0:T(8,128)(2,1)S(1)}, u32[]{:S(2)}, u32[]{:S(2)}) collective-permute-start(bf16[1024,128]{1,0:T(8,128)(2,1)} %get-tuple-element.36), channel_id=1, source_target_pairs={{4,20},{8,24},{12,28},{16,0},{20,4},{24,8},{5,21},{9,25},{13,29},{... | collective-permute-start | bytes 786440 | tf_op jit(solution)/shard_map/ppermute | solution.py:412
  12.7 35.9 %collective-permute-start.1 = (bf16[1024,128]{1,0:T(8,128)(2,1)}, bf16[1024,128]{1,0:T(8,128)(2,1)S(1)}, u32[]{:S(2)}, u32[]{:S(2)}) collective-permute-start(bf16[1024,128]{1,0:T(8,128)(2,1)} %get-tuple-element.37), channel_id=1, source_target_pairs={{4,16},{8,28},{12,24},{16,4},{20,0},{24,12},{5,17},{9,29},{13,25},... | collective-permute-start | bytes 786440 | tf_op jit(solution)/shard_map/ppermute | solution.py:412
  14.0 42.9 %collective-permute-start.2 = (bf16[1024,128]{1,0:T(8,128)(2,1)}, bf16[1024,128]{1,0:T(8,128)(2,1)S(1)}, u32[]{:S(2)}, u32[]{:S(2)}) collective-permute-start(bf16[1024,128]{1,0:T(8,128)(2,1)} %get-tuple-element.38), channel_id=1, source_target_pairs={{4,28},{8,16},{12,20},{16,8},{20,12},{24,0},{5,29},{9,17},{13,21},... | collective-permute-start | bytes 786440 | tf_op jit(solution)/shard_map/ppermute | solution.py:412
  15.3 41.5 %collective-permute-start.3 = (bf16[1024,128]{1,0:T(8,128)(2,1)S(1)}, bf16[1024,128]{1,0:T(8,128)(2,1)S(1)}, u32[]{:S(2)}, u32[]{:S(2)}) collective-permute-start(bf16[1024,128]{1,0:T(8,128)(2,1)S(1)} %copy-done.14), channel_id=1, source_target_pairs={{4,24},{8,20},{12,16},{16,12},{20,8},{24,4},{5,25},{9,21},{13,17},... | collective-permute-start | bytes 786440 | tf_op jit(solution)/shard_map/ppermute | solution.py:412
  47.8 9.1 %copy-start = (bf16[4,2064,128]{2,1,0:T(8,128)(2,1)}, bf16[4,2064,128]{2,1,0:T(8,128)(2,1)S(1)}, u32[]{:S(2)}) copy-start(bf16[4,2064,128]{2,1,0:T(8,128)(2,1)S(1)} %all-to-all-done.x_ref) | copy-start | bytes 6340612
  48.7 8.2 %copy-start.10 = (bf16[1024,128]{1,0:T(8,128)(2,1)}, bf16[1024,128]{1,0:T(8,128)(2,1)S(1)}, u32[]{:S(2)}) copy-start(bf16[1024,128]{1,0:T(8,128)(2,1)S(1)} %collective-permute-done.refs_0_) | copy-start | bytes 786436
  48.7 8.2 %copy-start.11 = (bf16[1024,128]{1,0:T(8,128)(2,1)}, bf16[1024,128]{1,0:T(8,128)(2,1)S(1)}, u32[]{:S(2)}) copy-start(bf16[1024,128]{1,0:T(8,128)(2,1)S(1)} %collective-permute-done.1.refs_1_) | copy-start | bytes 786436
  56.9 0.7 copy-start.12
  56.9 0.8 copy-start.13
  57.7 32.5 %all-to-all-start.1 = ((bf16[4,512,512]{2,1,0:T(8,128)(2,1)}), bf16[4,512,512]{2,1,0:T(8,128)(2,1)}, u32[]{:S(2)}, u32[]{:S(2)}) async-start(bf16[4,512,512]{2,1,0:T(8,128)(2,1)} %get-tuple-element.48), calls=%async_computation.1 | async-start | bytes 4194304 | tf_op jit(solution)/shard_map/all_to_all | solution.py:367
  65.5 35.8 %copy-start.9 = (s32[4,3]{1,0:T(4,128)S(1)}, s32[4,3]{1,0:T(4,128)}, u32[]{:S(2)}) copy-start(s32[4,3]{1,0:T(4,128)} %convert_reduce_fusion.near_ref) | copy-start | bytes 148
  81.0 20.4 %copy-start.1 = (bf16[4,2064,128]{2,1,0:T(8,128)(2,1)S(1)}, bf16[4,2064,128]{2,1,0:T(8,128)(2,1)}, u32[]{:S(2)}) copy-start(bf16[4,2064,128]{2,1,0:T(8,128)(2,1)} %copy-done) | copy-start | bytes 6340612
  81.0 43.5 %collective-permute-start.8 = (bf16[3,1024,128]{2,1,0:T(8,128)(2,1)}, bf16[3,1024,128]{2,1,0:T(8,128)(2,1)S(1)}, u32[]{:S(2)}, u32[]{:S(2)}) collective-permute-start(bf16[3,1024,128]{2,1,0:T(8,128)(2,1)} %get-tuple-element.53), channel_id=1, source_target_pairs={{0,16},{4,20},{8,24},{12,28},{16,0},{20,4},{24,8},{28,12},{1,17},{... | collective-permute-start | bytes 2359304 | tf_op jit(solution)/shard_map/ppermute | solution.py:374
  90.1 1.0 copy-start.5
  91.2 10.2 %copy-start.7 = (f32[8,1,512]{2,1,0:T(1,128)S(1)}, f32[8,1,512]{2,1,0:T(1,128)}, u32[]{:S(2)}) copy-start(f32[8,1,512]{2,1,0:T(1,128)} %get-tuple-element.54.lse_ref) | copy-start | bytes 49156
  91.2 10.2 %copy-start.8 = (f32[8,1,512]{2,1,0:T(1,128)S(1)}, f32[8,1,512]{2,1,0:T(1,128)}, u32[]{:S(2)}) copy-start(f32[8,1,512]{2,1,0:T(1,128)} %get-tuple-element.50.delta_ref) | copy-start | bytes 49156
  93.3 18.8 %collective-permute-start.4 = (bf16[32,512]{1,0:T(8,128)(2,1)S(1)}, bf16[32,512]{1,0:T(8,128)(2,1)S(1)}, u32[]{:S(2)}, u32[]{:S(2)}) collective-permute-start(bf16[32,512]{1,0:T(8,128)(2,1)S(1)} %get-tuple-element.65), channel_id=1, source_target_pairs={{0,1},{1,2},{2,3},{3,0},{4,5},{5,6},{6,7},{7,4},{8,9},{9,10},{10,1... | collective-permute-start | bytes 98312 | tf_op jit(solution)/shard_map/ppermute | solution.py:335
  93.4 18.7 %collective-permute-start.6 = (bf16[32,512]{1,0:T(8,128)(2,1)S(1)}, bf16[32,512]{1,0:T(8,128)(2,1)S(1)}, u32[]{:S(2)}, u32[]{:S(2)}) collective-permute-start(bf16[32,512]{1,0:T(8,128)(2,1)S(1)} %get-tuple-element.66), channel_id=1, source_target_pairs={{0,3},{1,0},{2,1},{3,2},{4,7},{5,4},{6,5},{7,6},{8,11},{9,8},{10,9... | collective-permute-start | bytes 98312 | tf_op jit(solution)/shard_map/ppermute | solution.py:335
  95.1 17.0 %collective-permute-start.5 = (bf16[32,512]{1,0:T(8,128)(2,1)S(1)}, bf16[32,512]{1,0:T(8,128)(2,1)S(1)}, u32[]{:S(2)}, u32[]{:S(2)}) collective-permute-start(bf16[32,512]{1,0:T(8,128)(2,1)S(1)} %get-tuple-element.67), channel_id=1, source_target_pairs={{0,2},{1,3},{2,0},{3,1},{4,6},{5,7},{6,4},{7,5},{8,10},{9,11},{10,... | collective-permute-start | bytes 98312 | tf_op jit(solution)/shard_map/ppermute | solution.py:335
  101.4 1.2 copy-start.3
  112.1 12.5 %copy-start.6 = (bf16[4,512,128]{2,1,0:T(8,128)(2,1)S(1)}, bf16[4,512,128]{2,1,0:T(8,128)(2,1)}, u32[]{:S(2)}) copy-start(bf16[4,512,128]{2,1,0:T(8,128)(2,1)} %get-tuple-element.47.attn_ref.refs_3_) | copy-start | bytes 1572868
  112.1 12.4 %collective-permute-start.7 = (bf16[32,512]{1,0:T(8,128)(2,1)S(1)}, bf16[32,512]{1,0:T(8,128)(2,1)S(1)}, u32[]{:S(2)}, u32[]{:S(2)}) collective-permute-start(bf16[32,512]{1,0:T(8,128)(2,1)S(1)} %fusion.1), channel_id=1, source_target_pairs={{0,16},{4,20},{8,24},{12,28},{16,0},{20,4},{24,8},{28,12},{1,17},{... | collective-permute-start | bytes 98312 | tf_op jit(solution)/shard_map/ppermute | solution.py:374
  125.0 1.4 copy-start.2
  126.4 6.8 %collective-permute-start.9 = (bf16[32,512]{1,0:T(8,128)(2,1)S(1)}, bf16[32,512]{1,0:T(8,128)(2,1)S(1)}, u32[]{:S(2)}, u32[]{:S(2)}) collective-permute-start(bf16[32,512]{1,0:T(8,128)(2,1)S(1)} %multiply_convert_fusion), channel_id=1, source_target_pairs={{0,12},{4,0},{8,4},{12,8},{16,28},{20,16},{24,20},{28,24},{1,13},{... | collective-permute-start | bytes 98312 | tf_op jit(solution)/shard_map/ppermute | solution.py:345
  127.0 6.3 %collective-permute-start.11 = (bf16[32,512]{1,0:T(8,128)(2,1)S(1)}, bf16[32,512]{1,0:T(8,128)(2,1)S(1)}, u32[]{:S(2)}, u32[]{:S(2)}) collective-permute-start(bf16[32,512]{1,0:T(8,128)(2,1)S(1)} %multiply_convert_fusion), channel_id=1, source_target_pairs={{0,4},{4,8},{8,12},{12,0},{16,20},{20,24},{24,28},{28,16},{1,5},{5... | collective-permute-start | bytes 98312 | tf_op jit(solution)/shard_map/ppermute | solution.py:345
  128.4 4.8 %collective-permute-start.10 = (bf16[32,512]{1,0:T(8,128)(2,1)S(1)}, bf16[32,512]{1,0:T(8,128)(2,1)S(1)}, u32[]{:S(2)}, u32[]{:S(2)}) collective-permute-start(bf16[32,512]{1,0:T(8,128)(2,1)S(1)} %multiply_convert_fusion), channel_id=1, source_target_pairs={{0,8},{4,12},{8,0},{12,4},{16,24},{20,28},{24,16},{28,20},{1,9},{5... | collective-permute-start | bytes 98312 | tf_op jit(solution)/shard_map/ppermute | solution.py:345
  129.0 29.1 %all-to-all-start.2 = ((bf16[4,2048,128]{2,1,0:T(8,128)(2,1)}), bf16[4,2048,128]{2,1,0:T(8,128)(2,1)S(1)}, u32[]{:S(2)}, u32[]{:S(2)}) async-start(bf16[4,2048,128]{2,1,0:T(8,128)(2,1)} %copy-done.2), calls=%async_computation.2 | async-start | bytes 4194304 | tf_op jit(solution)/shard_map/all_to_all | solution.py:367
  133.3 24.8 %copy-start.4 = (bf16[512,512]{1,0:T(8,128)(2,1)S(1)}, bf16[512,512]{1,0:T(8,128)(2,1)}, u32[]{:S(2)}) copy-start(bf16[512,512]{1,0:T(8,128)(2,1)} %w_ref.1) | copy-start | bytes 1572868
  133.4 5.7 %collective-permute-start.12 = (bf16[4,32,512]{2,1,0:T(8,128)(2,1)S(1)}, bf16[4,32,512]{2,1,0:T(8,128)(2,1)S(1)}, u32[]{:S(2)}, u32[]{:S(2)}) collective-permute-start(bf16[4,32,512]{2,1,0:T(8,128)(2,1)S(1)} %constant_dynamic-slice_fusion), channel_id=1, source_target_pairs={{0,3},{1,0},{2,1},{3,2},{4,7},{5,4},{6,5},{7,6},{8,11},{9,8},{10,9... | collective-permute-start | bytes 393224 | tf_op jit(solution)/shard_map/ppermute | solution.py:345
  136.4 6.4 %collective-permute-start.14 = (bf16[4,32,512]{2,1,0:T(8,128)(2,1)S(1)}, bf16[4,32,512]{2,1,0:T(8,128)(2,1)S(1)}, u32[]{:S(2)}, u32[]{:S(2)}) collective-permute-start(bf16[4,32,512]{2,1,0:T(8,128)(2,1)S(1)} %constant_dynamic-slice_fusion), channel_id=1, source_target_pairs={{0,1},{1,2},{2,3},{3,0},{4,5},{5,6},{6,7},{7,4},{8,9},{9,10},{10,1... | collective-permute-start | bytes 393224 | tf_op jit(solution)/shard_map/ppermute | solution.py:345
  136.4 6.3 %collective-permute-start.13 = (bf16[4,32,512]{2,1,0:T(8,128)(2,1)S(1)}, bf16[4,32,512]{2,1,0:T(8,128)(2,1)S(1)}, u32[]{:S(2)}, u32[]{:S(2)}) collective-permute-start(bf16[4,32,512]{2,1,0:T(8,128)(2,1)S(1)} %constant_dynamic-slice_fusion), channel_id=1, source_target_pairs={{0,2},{1,3},{2,0},{3,1},{4,6},{5,7},{6,4},{7,5},{8,10},{9,11},{10,... | collective-permute-start | bytes 393224 | tf_op jit(solution)/shard_map/ppermute | solution.py:345

commit v6 on v5

--- a/solution.py
+++ b/solution.py
@@ -33,7 +33,7 @@
 
 
 def pack_kernel(near_ref, *refs):
-    sources, (out_ref, spread_ref, *direct), held, arrived = refs[:5], refs[5:-6], refs[-6:-1], refs[-1]
+    sources, (out_ref, *direct), held, arrived = refs[:5], refs[5:-6], refs[-6:-1], refs[-1]
     copies = [
         pltpu.make_async_copy(source, target, arrived.at[i])
         for i, (source, target) in enumerate(zip(sources, held))
@@ -69,8 +69,6 @@
             [d_attn[:half, cols], d_attn[half:, cols]], axis=1
         )
         out_ref[to, MINE * (rows + 2 * half) :, :] = offsets.astype(BF16)
-    for to in range(GROUP):
-        spread_ref[to] = g_ref[...]
     for by, ref in enumerate(direct):
         ref[...] = out_ref[(here % GROUP) ^ by, : MINE * rows, :]
 
@@ -243,12 +241,14 @@
             out_ref[b, i * rows : (i + 1) * rows, :] = acc[i * blocks + GROUP + b].astype(BF16)
 
 
-def term_kernel(attn_ref, g_ref, term_ref):
+def term_kernel(attn_ref, *refs):
+    grads, term_ref = refs[:GROUP], refs[GROUP]
     half = attn_ref.shape[1] // MINE
     term = jnp.zeros(term_ref.shape, F32)
-    for p in range(GROUP):
+    for by in range(GROUP):
+        p = (lax.axis_index("seg") % GROUP) ^ by
         turned = [halves(attn_ref[p, i * half : (i + 1) * half, :]) for i in range(MINE)]
-        term = term + mm(jnp.concatenate(turned, axis=0), g_ref[p])
+        term = term + mm(jnp.concatenate(turned, axis=0), grads[by][...])
     term_ref[...] = term.astype(BF16)
 
 
@@ -388,14 +388,13 @@
             name=name,
         )
 
-    packed, spread, *direct = pl.pallas_call(
+    packed, *direct = pl.pallas_call(
         pack_kernel,
         in_specs=[smem] + [pl.BlockSpec(memory_space=pltpu.HBM)] * 5,
         scratch_shapes=[pltpu.VMEM((rows, model), BF16)] * 4
         + [pltpu.VMEM((model, model), BF16), pltpu.SemaphoreType.DMA((5,))],
         out_shape=[
             jax.ShapeDtypeStruct((GROUP, MINE * (rows + 2 * half) + 16, wide), BF16),
-            jax.ShapeDtypeStruct((GROUP, rows, model), BF16),
         ]
         + [jax.ShapeDtypeStruct((MINE * rows, wide), BF16)] * (GROUP if alone else 0),
         compiler_params=params(60),
@@ -419,8 +418,10 @@
         ]
     at = MINE * (rows + 2 * half)
     near = x[:, at : at + NBR, 0].astype(jnp.int32)
-    x, near, beyond, spread = lax.optimization_barrier((x, near, beyond, spread))
-    grads_here = swap(spread)
+    x, near, beyond, grad_in = lax.optimization_barrier((x, near, beyond, grad_out[0]))
+    grads_here = [grad_in] + [
+        lax.ppermute(grad_in, "seg", [(s, s ^ by) for s in range(seg)]) for by in range(1, GROUP)
+    ]
 
     lists = lambda count: [pltpu.SMEM((count + 8,), jnp.int32)] * 2
     sheet = pltpu.VMEM((rows, rows), F32)
@@ -487,7 +488,7 @@
     part = MINE * width // samples
     (w_term,) = call(
         term_kernel, "term", [((MINE * width, model), BF16)], [], 2 * rows * model * model
-    )(attn, grads_here)
+    )(attn, *grads_here)
     w_part = exchange(w_term.reshape(samples, part, model), "sample")
     w_part = jnp.sum(w_part.astype(F32), axis=0).astype(BF16)
     own0 = own_terms(0, lse, delta, dq)

time: 162 us -> 157 us (0.969)
  starting transfers between devices: 43 us -> 36.9 us
  waiting for transfers between devices: 65.4 us -> 63.4 us
  local copies, waits for them, and re-layouts: 4.56 us -> 6.56 us
    all_to_all x3 -> x2, starting transfers between devices: 17.4 us -> 9.38 us  [swap(): return lax.all_to_all(array, 'seg', 0, 0, axis_index_groups=split)]
    ppermute x0 -> x3, starting transfers between devices: none -> 7.34 us  [body(): lax.ppermute(grad_in, 'seg', [(s, s ^ by) for s in range(seg)])]
    ppermute x3, starting transfers between devices: 8.06 us -> 2.59 us  [exchange(): lax.ppermute(piece, axis, around(count, by))]
    all_to_all x3 -> x2, waiting for transfers between devices: 48.3 us -> 44.1 us  [swap(): return lax.all_to_all(array, 'seg', 0, 0, axis_index_groups=split)]
    pallas_call x1, Pallas kernels: 15.5 us -> 19.1 us  [body(): call(functools.partial(attend_kernel, alone), 'attend', [((GROUP, MINE *...]
    ppermute x6, starting transfers between devices: 6.16 us -> 4.53 us  [gathered(): arrived.append(lax.ppermute(piece, axis, pairs))]
    unnamed x43 -> x41, local copies, waits for them, and re-layouts: 4.51 us -> 5.87 us
  transfers between devices with their start and end apart: 18 -> 20, of which waited for: 7 -> 7; matrix products, arithmetic and copies ran while one was open for 1% -> 2% of each run, Pallas kernels for 23% -> 24%
where the time goes in v6:
time: 157 us; the launch traced here: 156 us
  waiting for transfers between devices  63.4 us (40%)
  Pallas kernels  45.7 us (29%)
  starting transfers between devices  36.9 us (24%)
  local copies, waits for them, and re-layouts  6.56 us (4%)
  other arithmetic  2.87 us (2%)
    all_to_all x2, waiting for transfers between devices, swap(): return lax.all_to_all(array, 'seg', 0, 0, axis_index_groups=split)  44.1 us
    pallas_call x1, Pallas kernels, body(): call(functools.partial(attend_kernel, alone), 'attend', [((GROUP, MINE *...  19.1 us
    pallas_call x2, Pallas kernels, own_terms(): call(functools.partial(own_kernel, i), f'own{i}', [((GROUP, rows + half,...  17.3 us
    all_to_all x2, starting transfers between devices, swap(): return lax.all_to_all(array, 'seg', 0, 0, axis_index_groups=split)  9.38 us
    ppermute x4, waiting for transfers between devices, body(): lax.ppermute(array, 'seg', [(s, (s + GROUP) % seg ^ by) for s in border])  8.22 us
    ppermute x2, starting transfers between devices, across(): lax.ppermute(array, 'seg', [(s, (s + GROUP) % seg) for s in range(seg)])  7.85 us
    ppermute x3, starting transfers between devices, body(): lax.ppermute(grad_in, 'seg', [(s, s ^ by) for s in range(seg)])  7.34 us
    ppermute x6, waiting for transfers between devices, gathered(): arrived.append(lax.ppermute(piece, axis, pairs))  7.31 us
  transfers between devices with their start and end apart: 20, of which 7 were waited for; matrix products, arithmetic and copies ran while one was open for 2% of the time, Pallas kernels for 24%

profile of v6, /device:TPU:0, one launch (start us, length us, event | category | flops | bytes accessed | tf_op | source)
XLA Modules:
  0.0 156.4 jit_solution(17513468547403543734)
XLA Ops:
  0.6 4.7 %pack.1 = (bf16[4,2064,128]{2,1,0:T(8,128)(2,1)}, bf16[1024,128]{1,0:T(8,128)(2,1)}, bf16[1024,128]{1,0:T(8,128)(2,1)}, bf16[1024,128]{1,0:T(8,128)(2,1)}, bf16[1024,128]{1,0:T(8,128)(2,1)}) custom-call(s32[1,3]{1,0:T(1,128)} %bitcast.64, bf16[512,512]{1,0:T(8,128)(2,1)} %bitcast.61, bf16[512,512]{1,0:T(8,128)(2,1)} %bitcast.62, bf16[512,512]{1,0:T(8,128)(2,1)} %bitcast.63, ...), custom_call_target="tpu_custom_call" | custom-call | flops 268435 | bytes 2621 | tf_op jit(solution)/shard_map/pack/pallas_call | solution.py:391
  5.3 0.0 copy-start.7
  5.3 5.4 %all-to-all-start = ((bf16[4,2064,128]{2,1,0:T(8,128)(2,1)}), bf16[4,2064,128]{2,1,0:T(8,128)(2,1)S(1)}, u32[]{:S(2)}, u32[]{:S(2)}) async-start(bf16[4,2064,128]{2,1,0:T(8,128)(2,1)} %get-tuple-element.34), calls=%async_computation | async-start | bytes 4227072 | tf_op jit(solution)/shard_map/all_to_all | solution.py:367
  10.7 1.3 collective-permute-start
  12.0 1.3 collective-permute-start.1
  13.3 1.3 collective-permute-start.2
  14.6 1.4 collective-permute-start.3
  16.0 31.1 %all-to-all-done.x_ref = bf16[4,2064,128]{2,1,0:T(8,128)(2,1)S(1)} async-done(((bf16[4,2064,128]{2,1,0:T(8,128)(2,1)}), bf16[4,2064,128]{2,1,0:T(8,128)(2,1)S(1)}, u32[]{:S(2)}, u32[]{:S(2)}) %all-to-all-start) | async-done | bytes 2113568 | tf_op jit(solution)/shard_map/all_to_all | solution.py:367
  47.0 0.9 convert_reduce_fusion.near_ref
  47.9 0.0 collective-permute-done.refs_0_
  47.9 8.2 %collective-permute-done.2.refs_2_ = bf16[1024,128]{1,0:T(8,128)(2,1)S(1)} collective-permute-done((bf16[1024,128]{1,0:T(8,128)(2,1)}, bf16[1024,128]{1,0:T(8,128)(2,1)S(1)}, u32[]{:S(2)}, u32[]{:S(2)}) %collective-permute-start.2) | collective-permute-done | bytes 262176 | tf_op jit(solution)/shard_map/ppermute | solution.py:411
  56.1 5.9 %collective-permute-start.4 = (bf16[512,512]{1,0:T(8,128)(2,1)S(1)}, bf16[512,512]{1,0:T(8,128)(2,1)}, u32[]{:S(2)}, u32[]{:S(2)}) collective-permute-start(bf16[512,512]{1,0:T(8,128)(2,1)S(1)} %bitcast.54), channel_id=1, source_target_pairs={{0,4},{4,0},{8,12},{12,8},{16,20},{20,16},{24,28},{28,24},{1,5},{5... | collective-permute-start | bytes 1572872 | tf_op jit(solution)/shard_map/ppermute | solution.py:423
  62.0 1.5 collective-permute-start.5
  63.5 19.1 %attend.1 = (bf16[4,512,128]{2,1,0:T(8,128)(2,1)}, f32[8,1,512]{2,1,0:T(1,128)}, f32[8,1,512]{2,1,0:T(1,128)}, f32[8,64,512]{2,1,0:T(8,128)}, bf16[3,1024,128]{2,1,0:T(8,128)(2,1)}) custom-call(s32[4,3]{1,0:T(4,128)} %convert_reduce_fusion.near_ref, bf16[4,2064,128]{2,1,0:T(8,128)(2,1)} %copy-done, bf16[1024,128]{1,0:T(8,128)(2,1)} %copy-done.11, ...), custom_call_target="tpu_custom_call" | custom-call | flops 2415919 | bytes 4194 | tf_op jit(solution)/shard_map/attend/pallas_call | solution.py:432
  82.7 2.7 %collective-permute-start.11 = (bf16[3,1024,128]{2,1,0:T(8,128)(2,1)}, bf16[3,1024,128]{2,1,0:T(8,128)(2,1)S(1)}, u32[]{:S(2)}, u32[]{:S(2)}) collective-permute-start(bf16[3,1024,128]{2,1,0:T(8,128)(2,1)} %get-tuple-element.51), channel_id=1, source_target_pairs={{0,16},{4,20},{8,24},{12,28},{16,0},{20,4},{24,8},{28,12},{1,17},{... | collective-permute-start | bytes 2359304 | tf_op jit(solution)/shard_map/ppermute | solution.py:374
  85.3 0.0 collective-permute-done.6.refs_3_
  85.3 1.0 copy-done.5
  86.4 1.8 %term.1 = bf16[128,512]{1,0:T(8,128)(2,1)S(1)} custom-call(bf16[4,512,128]{2,1,0:T(8,128)(2,1)S(1)} %copy-done.5, bf16[512,512]{1,0:T(8,128)(2,1)S(1)} %bitcast.57, bf16[512,512]{1,0:T(8,128)(2,1)} %collective-permute-done.4.refs_1_, bf16[512,512]{1,0:T(8,128)(2,1)} %collective-permute-done.5.refs_2_, bf16[512,512]{1,0:T(8,128)(2,1)} %collective-permute-done.6.refs_3_), custom_call_target="tpu_custom_call" | custom-call | flops 268435 | bytes 4194 | tf_op jit(solution)/shard_map/term/pallas_call | solution.py:489
  88.2 0.7 dynamic-slice_bitcast_fusion.2
  88.9 2.0 %collective-permute-start.9 = (bf16[32,512]{1,0:T(8,128)(2,1)}, bf16[32,512]{1,0:T(8,128)(2,1)}, u32[]{:S(2)}, u32[]{:S(2)}) collective-permute-start(bf16[32,512]{1,0:T(8,128)(2,1)} %get-tuple-element.64), channel_id=1, source_target_pairs={{0,3},{1,0},{2,1},{3,2},{4,7},{5,4},{6,5},{7,6},{8,11},{9,8},{10,9... | collective-permute-start | bytes 98312 | tf_op jit(solution)/shard_map/ppermute | solution.py:335
  90.9 0.3 collective-permute-start.8
  91.2 0.2 collective-permute-start.7
  91.5 1.2 copy-done.3
  92.7 0.7 copy-done.8
  93.4 0.7 copy-done.9
  94.1 0.7 copy-done.10
  94.8 8.7 %own0.1.refs_0_ = bf16[4,768,128]{2,1,0:T(8,128)(2,1)S(1)} custom-call(s32[4,3]{1,0:T(4,128)S(1)} %copy-done.10, bf16[4,2064,128]{2,1,0:T(8,128)(2,1)S(1)} %copy-done.1, f32[8,1,512]{2,1,0:T(1,128)S(1)} %copy-done.8, f32[8,1,512]{2,1,0:T(1,128)S(1)} %copy-done.9, f32[8,64,512]{2,1,0:T(8,128)S(1)} %copy-done.3), custom_call_target="tpu_custom_call" | custom-call | flops 3355443 | bytes 4194 | tf_op jit(solution)/shard_map/own0/pallas_call | solution.py:469
  103.5 0.0 copy-start.6
  103.6 0.9 fusion.1
  104.4 5.2 %collective-permute-start.10 = (bf16[32,512]{1,0:T(8,128)(2,1)S(1)}, bf16[32,512]{1,0:T(8,128)(2,1)S(1)}, u32[]{:S(2)}, u32[]{:S(2)}) collective-permute-start(bf16[32,512]{1,0:T(8,128)(2,1)S(1)} %fusion.1), channel_id=1, source_target_pairs={{0,16},{4,20},{8,24},{12,28},{16,0},{20,4},{24,8},{28,12},{1,17},{... | collective-permute-start | bytes 98312 | tf_op jit(solution)/shard_map/ppermute | solution.py:374
  109.6 8.5 %own1.1.refs_1_ = bf16[4,768,128]{2,1,0:T(8,128)(2,1)S(1)} custom-call(s32[4,3]{1,0:T(4,128)S(1)} %copy-done.10, bf16[4,2064,128]{2,1,0:T(8,128)(2,1)S(1)} %copy-done.1, f32[8,1,512]{2,1,0:T(1,128)S(1)} %copy-done.8, f32[8,1,512]{2,1,0:T(1,128)S(1)} %copy-done.9, f32[8,64,512]{2,1,0:T(8,128)S(1)} %copy-done.3), custom_call_target="tpu_custom_call" | custom-call | flops 3355443 | bytes 4194 | tf_op jit(solution)/shard_map/own1/pallas_call | solution.py:469
  118.2 3.7 %collective-permute-done.10 = bf16[32,512]{1,0:T(8,128)(2,1)S(1)} collective-permute-done((bf16[32,512]{1,0:T(8,128)(2,1)S(1)}, bf16[32,512]{1,0:T(8,128)(2,1)S(1)}, u32[]{:S(2)}, u32[]{:S(2)}) %collective-permute-start.10) | collective-permute-done | bytes 32800 | tf_op jit(solution)/shard_map/ppermute | solution.py:374
  121.9 0.4 merge.1
  122.4 1.3 copy-done.2
  123.7 0.1 collective-permute-start.12
  123.8 1.8 %collective-permute-start.13 = (bf16[32,512]{1,0:T(8,128)(2,1)S(1)}, bf16[32,512]{1,0:T(8,128)(2,1)S(1)}, u32[]{:S(2)}, u32[]{:S(2)}) collective-permute-start(bf16[32,512]{1,0:T(8,128)(2,1)S(1)} %multiply_convert_fusion), channel_id=1, source_target_pairs={{0,8},{4,12},{8,0},{12,4},{16,24},{20,28},{24,16},{28,20},{1,9},{5... | collective-permute-start | bytes 98312 | tf_op jit(solution)/shard_map/ppermute | solution.py:345
  125.6 0.2 collective-permute-start.14
  125.8 4.0 %all-to-all-start.1 = ((bf16[4,2048,128]{2,1,0:T(8,128)(2,1)}), bf16[4,2048,128]{2,1,0:T(8,128)(2,1)S(1)}, u32[]{:S(2)}, u32[]{:S(2)}) async-start(bf16[4,2048,128]{2,1,0:T(8,128)(2,1)} %copy-done.2), calls=%async_computation.1 | async-start | bytes 4194304 | tf_op jit(solution)/shard_map/all_to_all | solution.py:367
  129.9 0.6 collective-permute-done.14
  130.5 0.0 copy-start.4
  130.6 0.1 collective-permute-start.15
  130.6 2.3 %collective-permute-start.16 = (bf16[4,32,512]{2,1,0:T(8,128)(2,1)S(1)}, bf16[4,32,512]{2,1,0:T(8,128)(2,1)S(1)}, u32[]{:S(2)}, u32[]{:S(2)}) collective-permute-start(bf16[4,32,512]{2,1,0:T(8,128)(2,1)S(1)} %constant_dynamic-slice_fusion), channel_id=1, source_target_pairs={{0,2},{1,3},{2,0},{3,1},{4,6},{5,7},{6,4},{7,5},{8,10},{9,11},{10,... | collective-permute-start | bytes 393224 | tf_op jit(solution)/shard_map/ppermute | solution.py:345
  132.9 0.2 collective-permute-start.17
  133.1 0.1 collective-permute-done.15
  133.2 6.6 %collective-permute-done.16 = bf16[4,32,512]{2,1,0:T(8,128)(2,1)S(1)} collective-permute-done((bf16[4,32,512]{2,1,0:T(8,128)(2,1)S(1)}, bf16[4,32,512]{2,1,0:T(8,128)(2,1)S(1)}, u32[]{:S(2)}, u32[]{:S(2)}) %collective-permute-start.16) | collective-permute-done | bytes 131104 | tf_op jit(solution)/shard_map/ppermute | solution.py:345
  139.9 1.1 dynamic-slice_convert_fusion
  141.0 13.0 %all-to-all-done.1.y_ref = bf16[4,2048,128]{2,1,0:T(8,128)(2,1)S(1)} async-done(((bf16[4,2048,128]{2,1,0:T(8,128)(2,1)}), bf16[4,2048,128]{2,1,0:T(8,128)(2,1)S(1)}, u32[]{:S(2)}, u32[]{:S(2)}) %all-to-all-start.1) | async-done | bytes 2097184 | tf_op jit(solution)/shard_map/all_to_all | solution.py:367
  154.1 2.3 %unpack.1 = (bf16[512,512]{1,0:T(8,128)(2,1)}, bf16[512,512]{1,0:T(8,128)(2,1)}, bf16[512,512]{1,0:T(8,128)(2,1)}, bf16[512,512]{1,0:T(8,128)(2,1)}) custom-call(bf16[4,2048,128]{2,1,0:T(8,128)(2,1)S(1)} %all-to-all-done.1.y_ref, bf16[512,512]{1,0:T(8,128)(2,1)S(1)} %copy-done.4), custom_call_target="tpu_custom_call" | custom-call | flops 268435 | bytes 4194 | tf_op jit(solution)/shard_map/unpack/pallas_call | solution.py:516
  (50 shorter events, 0.2 us)
Async XLA Ops:
  5.3 50.8 %copy-start.7 = (bf16[1,512,512]{2,1,0:T(8,128)(2,1)S(1)}, bf16[1,512,512]{2,1,0:T(8,128)(2,1)}, u32[]{:S(2)}) copy-start(bf16[1,512,512]{2,1,0:T(8,128)(2,1)} %param.10) | copy-start | bytes 1572868
  5.3 41.7 %all-to-all-start = ((bf16[4,2064,128]{2,1,0:T(8,128)(2,1)}), bf16[4,2064,128]{2,1,0:T(8,128)(2,1)S(1)}, u32[]{:S(2)}, u32[]{:S(2)}) async-start(bf16[4,2064,128]{2,1,0:T(8,128)(2,1)} %get-tuple-element.34), calls=%async_computation | async-start | bytes 4227072 | tf_op jit(solution)/shard_map/all_to_all | solution.py:367
  10.7 37.2 %collective-permute-start = (bf16[1024,128]{1,0:T(8,128)(2,1)}, bf16[1024,128]{1,0:T(8,128)(2,1)S(1)}, u32[]{:S(2)}, u32[]{:S(2)}) collective-permute-start(bf16[1024,128]{1,0:T(8,128)(2,1)} %get-tuple-element.35), channel_id=1, source_target_pairs={{4,20},{8,24},{12,28},{16,0},{20,4},{24,8},{5,21},{9,25},{13,29},{... | collective-permute-start | bytes 786440 | tf_op jit(solution)/shard_map/ppermute | solution.py:411
  12.0 35.9 %collective-permute-start.1 = (bf16[1024,128]{1,0:T(8,128)(2,1)}, bf16[1024,128]{1,0:T(8,128)(2,1)S(1)}, u32[]{:S(2)}, u32[]{:S(2)}) collective-permute-start(bf16[1024,128]{1,0:T(8,128)(2,1)} %get-tuple-element.36), channel_id=1, source_target_pairs={{4,16},{8,28},{12,24},{16,4},{20,0},{24,12},{5,17},{9,29},{13,25},... | collective-permute-start | bytes 786440 | tf_op jit(solution)/shard_map/ppermute | solution.py:411
  13.3 42.8 %collective-permute-start.2 = (bf16[1024,128]{1,0:T(8,128)(2,1)}, bf16[1024,128]{1,0:T(8,128)(2,1)S(1)}, u32[]{:S(2)}, u32[]{:S(2)}) collective-permute-start(bf16[1024,128]{1,0:T(8,128)(2,1)} %get-tuple-element.37), channel_id=1, source_target_pairs={{4,28},{8,16},{12,20},{16,8},{20,12},{24,0},{5,29},{9,17},{13,21},... | collective-permute-start | bytes 786440 | tf_op jit(solution)/shard_map/ppermute | solution.py:411
  14.6 41.6 %collective-permute-start.3 = (bf16[1024,128]{1,0:T(8,128)(2,1)}, bf16[1024,128]{1,0:T(8,128)(2,1)}, u32[]{:S(2)}, u32[]{:S(2)}) collective-permute-start(bf16[1024,128]{1,0:T(8,128)(2,1)} %get-tuple-element.38), channel_id=1, source_target_pairs={{4,24},{8,20},{12,16},{16,12},{20,8},{24,4},{5,25},{9,21},{13,17},... | collective-permute-start | bytes 786440 | tf_op jit(solution)/shard_map/ppermute | solution.py:411
  47.0 16.5 %copy-start = (bf16[4,2064,128]{2,1,0:T(8,128)(2,1)}, bf16[4,2064,128]{2,1,0:T(8,128)(2,1)S(1)}, u32[]{:S(2)}) copy-start(bf16[4,2064,128]{2,1,0:T(8,128)(2,1)S(1)} %all-to-all-done.x_ref) | copy-start | bytes 6340612
  47.9 15.6 %copy-start.11 = (bf16[1024,128]{1,0:T(8,128)(2,1)}, bf16[1024,128]{1,0:T(8,128)(2,1)S(1)}, u32[]{:S(2)}) copy-start(bf16[1024,128]{1,0:T(8,128)(2,1)S(1)} %collective-permute-done.refs_0_) | copy-start | bytes 786436
  47.9 15.6 %copy-start.12 = (bf16[1024,128]{1,0:T(8,128)(2,1)}, bf16[1024,128]{1,0:T(8,128)(2,1)S(1)}, u32[]{:S(2)}) copy-start(bf16[1024,128]{1,0:T(8,128)(2,1)S(1)} %collective-permute-done.1.refs_1_) | copy-start | bytes 786436
  56.1 7.4 %copy-start.13 = (bf16[1024,128]{1,0:T(8,128)(2,1)}, bf16[1024,128]{1,0:T(8,128)(2,1)S(1)}, u32[]{:S(2)}) copy-start(bf16[1024,128]{1,0:T(8,128)(2,1)S(1)} %collective-permute-done.2.refs_2_) | copy-start | bytes 786436
  56.1 29.2 %collective-permute-start.4 = (bf16[512,512]{1,0:T(8,128)(2,1)S(1)}, bf16[512,512]{1,0:T(8,128)(2,1)}, u32[]{:S(2)}, u32[]{:S(2)}) collective-permute-start(bf16[512,512]{1,0:T(8,128)(2,1)S(1)} %bitcast.54), channel_id=1, source_target_pairs={{0,4},{4,0},{8,12},{12,8},{16,20},{20,16},{24,28},{28,24},{1,5},{5... | collective-permute-start | bytes 1572872 | tf_op jit(solution)/shard_map/ppermute | solution.py:423
  62.0 23.3 %collective-permute-start.5 = (bf16[512,512]{1,0:T(8,128)(2,1)S(1)}, bf16[512,512]{1,0:T(8,128)(2,1)}, u32[]{:S(2)}, u32[]{:S(2)}) collective-permute-start(bf16[512,512]{1,0:T(8,128)(2,1)S(1)} %bitcast.55), channel_id=1, source_target_pairs={{0,8},{4,12},{8,0},{12,4},{16,24},{20,28},{24,16},{28,20},{1,9},{5... | collective-permute-start | bytes 1572872 | tf_op jit(solution)/shard_map/ppermute | solution.py:423
  63.5 21.9 %collective-permute-start.6 = (bf16[512,512]{1,0:T(8,128)(2,1)S(1)}, bf16[512,512]{1,0:T(8,128)(2,1)}, u32[]{:S(2)}, u32[]{:S(2)}) collective-permute-start(bf16[512,512]{1,0:T(8,128)(2,1)S(1)} %bitcast.56), channel_id=1, source_target_pairs={{0,12},{4,8},{8,4},{12,0},{16,28},{20,24},{24,20},{28,16},{1,13},{... | collective-permute-start | bytes 1572872 | tf_op jit(solution)/shard_map/ppermute | solution.py:423
  82.7 8.8 %copy-start.1 = (bf16[4,2064,128]{2,1,0:T(8,128)(2,1)S(1)}, bf16[4,2064,128]{2,1,0:T(8,128)(2,1)}, u32[]{:S(2)}) copy-start(bf16[4,2064,128]{2,1,0:T(8,128)(2,1)} %copy-done) | copy-start | bytes 6340612
  82.7 39.3 %collective-permute-start.11 = (bf16[3,1024,128]{2,1,0:T(8,128)(2,1)}, bf16[3,1024,128]{2,1,0:T(8,128)(2,1)S(1)}, u32[]{:S(2)}, u32[]{:S(2)}) collective-permute-start(bf16[3,1024,128]{2,1,0:T(8,128)(2,1)} %get-tuple-element.51), channel_id=1, source_target_pairs={{0,16},{4,20},{8,24},{12,28},{16,0},{20,4},{24,8},{28,12},{1,17},{... | collective-permute-start | bytes 2359304 | tf_op jit(solution)/shard_map/ppermute | solution.py:374
  85.3 1.0 copy-start.5
  88.9 14.7 %collective-permute-start.9 = (bf16[32,512]{1,0:T(8,128)(2,1)}, bf16[32,512]{1,0:T(8,128)(2,1)}, u32[]{:S(2)}, u32[]{:S(2)}) collective-permute-start(bf16[32,512]{1,0:T(8,128)(2,1)} %get-tuple-element.64), channel_id=1, source_target_pairs={{0,3},{1,0},{2,1},{3,2},{4,7},{5,4},{6,5},{7,6},{8,11},{9,8},{10,9... | collective-permute-start | bytes 98312 | tf_op jit(solution)/shard_map/ppermute | solution.py:335
  90.9 12.7 %collective-permute-start.8 = (bf16[32,512]{1,0:T(8,128)(2,1)}, bf16[32,512]{1,0:T(8,128)(2,1)}, u32[]{:S(2)}, u32[]{:S(2)}) collective-permute-start(bf16[32,512]{1,0:T(8,128)(2,1)} %get-tuple-element.65), channel_id=1, source_target_pairs={{0,2},{1,3},{2,0},{3,1},{4,6},{5,7},{6,4},{7,5},{8,10},{9,11},{10,... | collective-permute-start | bytes 98312 | tf_op jit(solution)/shard_map/ppermute | solution.py:335
  91.2 12.3 %collective-permute-start.7 = (bf16[32,512]{1,0:T(8,128)(2,1)}, bf16[32,512]{1,0:T(8,128)(2,1)}, u32[]{:S(2)}, u32[]{:S(2)}) collective-permute-start(bf16[32,512]{1,0:T(8,128)(2,1)} %get-tuple-element.63), channel_id=1, source_target_pairs={{0,1},{1,2},{2,3},{3,0},{4,5},{5,6},{6,7},{7,4},{8,9},{9,10},{10,1... | collective-permute-start | bytes 98312 | tf_op jit(solution)/shard_map/ppermute | solution.py:335
  91.5 1.2 copy-start.3
  92.7 0.7 copy-start.8
  93.4 0.7 copy-start.9
  94.1 0.7 copy-start.10
  103.5 18.4 %copy-start.6 = (bf16[4,512,128]{2,1,0:T(8,128)(2,1)S(1)}, bf16[4,512,128]{2,1,0:T(8,128)(2,1)}, u32[]{:S(2)}) copy-start(bf16[4,512,128]{2,1,0:T(8,128)(2,1)} %get-tuple-element.45.attn_ref.refs_3_) | copy-start | bytes 1572868
  104.4 17.5 %collective-permute-start.10 = (bf16[32,512]{1,0:T(8,128)(2,1)S(1)}, bf16[32,512]{1,0:T(8,128)(2,1)S(1)}, u32[]{:S(2)}, u32[]{:S(2)}) collective-permute-start(bf16[32,512]{1,0:T(8,128)(2,1)S(1)} %fusion.1), channel_id=1, source_target_pairs={{0,16},{4,20},{8,24},{12,28},{16,0},{20,4},{24,8},{28,12},{1,17},{... | collective-permute-start | bytes 98312 | tf_op jit(solution)/shard_map/ppermute | solution.py:374
  122.4 1.4 copy-start.2
  123.7 6.1 %collective-permute-start.12 = (bf16[32,512]{1,0:T(8,128)(2,1)S(1)}, bf16[32,512]{1,0:T(8,128)(2,1)S(1)}, u32[]{:S(2)}, u32[]{:S(2)}) collective-permute-start(bf16[32,512]{1,0:T(8,128)(2,1)S(1)} %multiply_convert_fusion), channel_id=1, source_target_pairs={{0,12},{4,0},{8,4},{12,8},{16,28},{20,16},{24,20},{28,24},{1,13},{... | collective-permute-start | bytes 98312 | tf_op jit(solution)/shard_map/ppermute | solution.py:345
  123.8 6.0 %collective-permute-start.13 = (bf16[32,512]{1,0:T(8,128)(2,1)S(1)}, bf16[32,512]{1,0:T(8,128)(2,1)S(1)}, u32[]{:S(2)}, u32[]{:S(2)}) collective-permute-start(bf16[32,512]{1,0:T(8,128)(2,1)S(1)} %multiply_convert_fusion), channel_id=1, source_target_pairs={{0,8},{4,12},{8,0},{12,4},{16,24},{20,28},{24,16},{28,20},{1,9},{5... | collective-permute-start | bytes 98312 | tf_op jit(solution)/shard_map/ppermute | solution.py:345
  125.6 4.8 %collective-permute-start.14 = (bf16[32,512]{1,0:T(8,128)(2,1)S(1)}, bf16[32,512]{1,0:T(8,128)(2,1)S(1)}, u32[]{:S(2)}, u32[]{:S(2)}) collective-permute-start(bf16[32,512]{1,0:T(8,128)(2,1)S(1)} %multiply_convert_fusion), channel_id=1, source_target_pairs={{0,4},{4,8},{8,12},{12,0},{16,20},{20,24},{24,28},{28,16},{1,5},{5... | collective-permute-start | bytes 98312 | tf_op jit(solution)/shard_map/ppermute | solution.py:345
  125.8 28.3 %all-to-all-start.1 = ((bf16[4,2048,128]{2,1,0:T(8,128)(2,1)}), bf16[4,2048,128]{2,1,0:T(8,128)(2,1)S(1)}, u32[]{:S(2)}, u32[]{:S(2)}) async-start(bf16[4,2048,128]{2,1,0:T(8,128)(2,1)} %copy-done.2), calls=%async_computation.1 | async-start | bytes 4194304 | tf_op jit(solution)/shard_map/all_to_all | solution.py:367
  130.5 23.6 %copy-start.4 = (bf16[512,512]{1,0:T(8,128)(2,1)S(1)}, bf16[512,512]{1,0:T(8,128)(2,1)}, u32[]{:S(2)}) copy-start(bf16[512,512]{1,0:T(8,128)(2,1)} %w_ref.1) | copy-start | bytes 1572868
  130.6 2.6 %collective-permute-start.15 = (bf16[4,32,512]{2,1,0:T(8,128)(2,1)S(1)}, bf16[4,32,512]{2,1,0:T(8,128)(2,1)S(1)}, u32[]{:S(2)}, u32[]{:S(2)}) collective-permute-start(bf16[4,32,512]{2,1,0:T(8,128)(2,1)S(1)} %constant_dynamic-slice_fusion), channel_id=1, source_target_pairs={{0,3},{1,0},{2,1},{3,2},{4,7},{5,4},{6,5},{7,6},{8,11},{9,8},{10,9... | collective-permute-start | bytes 393224 | tf_op jit(solution)/shard_map/ppermute | solution.py:345
  130.6 9.2 %collective-permute-start.16 = (bf16[4,32,512]{2,1,0:T(8,128)(2,1)S(1)}, bf16[4,32,512]{2,1,0:T(8,128)(2,1)S(1)}, u32[]{:S(2)}, u32[]{:S(2)}) collective-permute-start(bf16[4,32,512]{2,1,0:T(8,128)(2,1)S(1)} %constant_dynamic-slice_fusion), channel_id=1, source_target_pairs={{0,2},{1,3},{2,0},{3,1},{4,6},{5,7},{6,4},{7,5},{8,10},{9,11},{10,... | collective-permute-start | bytes 393224 | tf_op jit(solution)/shard_map/ppermute | solution.py:345
  132.9 6.9 %collective-permute-start.17 = (bf16[4,32,512]{2,1,0:T(8,128)(2,1)S(1)}, bf16[4,32,512]{2,1,0:T(8,128)(2,1)S(1)}, u32[]{:S(2)}, u32[]{:S(2)}) collective-permute-start(bf16[4,32,512]{2,1,0:T(8,128)(2,1)S(1)} %constant_dynamic-slice_fusion), channel_id=1, source_target_pairs={{0,1},{1,2},{2,3},{3,0},{4,5},{5,6},{6,7},{7,4},{8,9},{9,10},{10,1... | collective-permute-start | bytes 393224 | tf_op jit(solution)/shard_map/ppermute | solution.py:345

commit v7 on v6

--- a/solution.py
+++ b/solution.py
@@ -135,7 +135,7 @@
     in_turn(total, enter, leave)
 
 
-def back_units(total, patch_of, block_of, keys, q_scr, d_scr, back_scr, k_scr, pairs, lse_ref, delta_ref, dq_ref, acc):
+def back_units(total, patch_of, block_of, keys, q_scr, d_scr, back_scr, k_scr, pairs, stat_ref, dq_ref, acc):
     rows = q_scr.shape[2]
 
     def enter(u, slot):
@@ -145,8 +145,8 @@
 
     def leave(u, slot, then):
         b, p = block_of[u], patch_of[u]
-        prob = jnp.exp(pairs[slot][:, :rows] - lse_ref[p])
-        ds = (prob * (pairs[slot][:, rows:] - delta_ref[p])).astype(BF16)
+        prob = jnp.exp(pairs[slot][:, :rows] - stat_ref[p, :1])
+        ds = (prob * (pairs[slot][:, rows:] - stat_ref[p, 1:])).astype(BF16)
         then()
         dq_ref[p] += mm(k_scr[b], ds)
         acc[b] += mm(jnp.concatenate([ds, prob.astype(BF16)], axis=1), back_scr[p])
@@ -181,7 +181,7 @@
 
 def attend_kernel(alone, near_ref, x_ref, *refs):
     halos, refs = refs[: GROUP if alone else 1], refs[GROUP if alone else 1 :]
-    (attn_ref, lse_ref, delta_ref, dq_ref, out_ref, acc, s0, s1, before_scr, top_scr, m_scr, o_scr, q_scr, d_scr, back_scr, v_scr, k_scr, kv_scr, patch_of, block_of, far_patch, far_block) = refs
+    (attn_ref, stat_ref, dq_ref, out_ref, acc, s0, s1, before_scr, top_scr, m_scr, o_scr, q_scr, d_scr, back_scr, v_scr, k_scr, kv_scr, patch_of, block_of, far_patch, far_block) = refs
     rows, width = q_scr.shape[2], x_ref.shape[2] // 2
     half, halo = rows // 2, REACH if alone else 2 * REACH
     blocks = GROUP + halo
@@ -228,14 +228,14 @@
         sums = o_scr[p, width : width + 1, :]
         attn = (o_scr[p, :width, :] * (1.0 / sums)).astype(BF16)
         attn_ref[p % GROUP, p // GROUP * half : (p // GROUP + 1) * half, :] = beside(attn)
-        lse_ref[p] = m_scr[p] + jnp.log(sums)
+        stat_ref[p, :1] = m_scr[p] + jnp.log(sums)
         product = d_scr[p, width:, :].astype(F32) * attn.astype(F32)
-        delta_ref[p] = jnp.sum(product, axis=0, keepdims=True)
+        stat_ref[p, 1:] = jnp.sum(product, axis=0, keepdims=True)
     for i in range(MINE):
         for b in range(halo):
             acc[i * blocks + GROUP + b] = jnp.zeros(acc.shape[1:], F32)
     dq_ref[...] = jnp.zeros_like(dq_ref)
-    back_units(far_total, far_patch, far_block, keys, q_scr, d_scr, back_scr, k_scr, (s0, s1), lse_ref, delta_ref, dq_ref, acc)
+    back_units(far_total, far_patch, far_block, keys, q_scr, d_scr, back_scr, k_scr, (s0, s1), stat_ref, dq_ref, acc)
     for i in range(MINE):
         for b in range(halo):
             out_ref[b, i * rows : (i + 1) * rows, :] = acc[i * blocks + GROUP + b].astype(BF16)
@@ -252,7 +252,7 @@
     term_ref[...] = term.astype(BF16)
 
 
-def own_kernel(head, near_ref, x_ref, lse_ref, delta_ref, dq_in, out_ref, acc, s0, s1, dq_scr, q_scr, d_scr, back_scr, k_scr, patch_of, block_of):
+def own_kernel(head, near_ref, x_ref, stat_ref, dq_in, out_ref, acc, s0, s1, dq_scr, q_scr, d_scr, back_scr, k_scr, patch_of, block_of):
     rows, width = q_scr.shape[2], x_ref.shape[2] // 2
     total = list_units(near_ref, patch_of, block_of, jnp.int32(0), 0, False)
     fill_q(x_ref, head, rows, width, q_scr, 0)
@@ -264,7 +264,7 @@
     acc[...] = jnp.zeros_like(acc)
     dq_scr[...] = dq_in[head * GROUP : (head + 1) * GROUP]
     keys = lambda b: x_ref[b, mine, :]
-    back_units(total, patch_of, block_of, keys, q_scr, d_scr, back_scr, k_scr, (s0, s1), lse_ref.at[own], delta_ref.at[own], dq_scr, acc)
+    back_units(total, patch_of, block_of, keys, q_scr, d_scr, back_scr, k_scr, (s0, s1), stat_ref.at[own], dq_scr, acc)
     for p in range(GROUP):
         out_ref[p, :rows, :] = acc[p].astype(BF16)
         out_ref[p, rows:, :] = beside(dq_scr[p].astype(BF16))
@@ -429,13 +429,12 @@
     lines = lambda count: pltpu.VMEM((count, 1, rows), F32)
     patches = MINE * GROUP
     blocks = GROUP + halo
-    attn, lse, delta, dq, far = call(
+    attn, stat, dq, far = call(
         functools.partial(attend_kernel, alone),
         "attend",
         [
             ((GROUP, MINE * half, wide), BF16),
-            ((patches, 1, rows), F32),
-            ((patches, 1, rows), F32),
+            ((patches, 2, rows), F32),
             ((patches, width, rows), F32),
             ((halo, MINE * rows, wide), BF16),
         ],
@@ -465,7 +464,7 @@
     else:
         back = jnp.concatenate([shifted(far[:REACH], -GROUP), shifted(far[REACH:], GROUP)], axis=0)
 
-    def own_terms(i, lse, delta, dq):
+    def own_terms(i, stat, dq):
         return call(
             functools.partial(own_kernel, i),
             f"own{i}",
@@ -483,7 +482,7 @@
             + lists(most),
             10 * unit_cost * 1280,
             10 * unit_cost,
-        )(near, x, lse, delta, dq)[0]
+        )(near, x, stat, dq)[0]
 
     part = MINE * width // samples
     (w_term,) = call(
@@ -491,9 +490,9 @@
     )(attn, *grads_here)
     w_part = exchange(w_term.reshape(samples, part, model), "sample")
     w_part = jnp.sum(w_part.astype(F32), axis=0).astype(BF16)
-    own0 = own_terms(0, lse, delta, dq)
-    w_part, lse, own0 = lax.optimization_barrier((w_part, lse, own0))
-    own1 = own_terms(1, lse, delta, dq)
+    own0 = own_terms(0, stat, dq)
+    w_part, stat, own0 = lax.optimization_barrier((w_part, stat, own0))
+    own1 = own_terms(1, stat, dq)
     if alone:
         w_part = w_part.astype(F32) + across(w_part).astype(F32)
     else:

time: 157 us -> 156 us (level)
  the two profiles are of different devices: /device:TPU:0 before, /device:TPU:13 now
where the time goes in v7:
time: 156 us
  Pallas kernels  52.1 us (33%)
  starting transfers between devices  50.7 us (32%)
  waiting for transfers between devices  43.3 us (28%)
  local copies, waits for them, and re-layouts  5.98 us (4%)
  other arithmetic  2.86 us (2%)
    all_to_all x2, waiting for transfers between devices, swap(): return lax.all_to_all(array, 'seg', 0, 0, axis_index_groups=split)  36.9 us
    pallas_call x1, Pallas kernels, body(): call(functools.partial(attend_kernel, alone), 'attend', [((GROUP, MINE *...  22.6 us
    pallas_call x2, Pallas kernels, own_terms(): call(functools.partial(own_kernel, i), f'own{i}', [((GROUP, rows + half,...  20.2 us
    ppermute x3, starting transfers between devices, body(): lax.ppermute(grad_in, 'seg', [(s, s ^ by) for s in range(seg)])  16.4 us
    ppermute x4, starting transfers between devices, body(): lax.ppermute(array, 'seg', [(s, (s + GROUP) % seg ^ by) for s in border])  12.4 us
    all_to_all x2, starting transfers between devices, swap(): return lax.all_to_all(array, 'seg', 0, 0, axis_index_groups=split)  8.61 us
    ppermute x6, starting transfers between devices, gathered(): arrived.append(lax.ppermute(piece, axis, pairs))  8.3 us
    unnamed x39, local copies, waits for them, and re-layouts  5.31 us
  transfers between devices with their start and end apart: 20, of which 5 were waited for; matrix products, arithmetic and copies ran while one was open for 2% of the time, Pallas kernels for 29%

profile of v7, /device:TPU:13, one launch (start us, length us, event | category | flops | bytes accessed | tf_op | source)
XLA Modules:
  0.0 156.0 jit_solution(14881455769039767166)
XLA Ops:
  0.6 4.7 %pack.1 = (bf16[4,2064,128]{2,1,0:T(8,128)(2,1)}, bf16[1024,128]{1,0:T(8,128)(2,1)}, bf16[1024,128]{1,0:T(8,128)(2,1)}, bf16[1024,128]{1,0:T(8,128)(2,1)}, bf16[1024,128]{1,0:T(8,128)(2,1)}) custom-call(s32[1,3]{1,0:T(1,128)} %bitcast.64, bf16[512,512]{1,0:T(8,128)(2,1)} %bitcast.61, bf16[512,512]{1,0:T(8,128)(2,1)} %bitcast.62, bf16[512,512]{1,0:T(8,128)(2,1)} %bitcast.63, ...), custom_call_target="tpu_custom_call" | custom-call | flops 268435 | bytes 2621 | tf_op jit(solution)/shard_map/pack/pallas_call | solution.py:391
  5.3 0.0 copy-start.7
  5.3 3.9 %all-to-all-start = ((bf16[4,2064,128]{2,1,0:T(8,128)(2,1)}), bf16[4,2064,128]{2,1,0:T(8,128)(2,1)S(1)}, u32[]{:S(2)}, u32[]{:S(2)}) async-start(bf16[4,2064,128]{2,1,0:T(8,128)(2,1)} %get-tuple-element.33), calls=%async_computation | async-start | bytes 4227072 | tf_op jit(solution)/shard_map/all_to_all | solution.py:367
  9.2 4.2 %collective-permute-start = (bf16[1024,128]{1,0:T(8,128)(2,1)}, bf16[1024,128]{1,0:T(8,128)(2,1)S(1)}, u32[]{:S(2)}, u32[]{:S(2)}) collective-permute-start(bf16[1024,128]{1,0:T(8,128)(2,1)} %get-tuple-element.34), channel_id=1, source_target_pairs={{4,20},{8,24},{12,28},{16,0},{20,4},{24,8},{5,21},{9,25},{13,29},{... | collective-permute-start | bytes 786440 | tf_op jit(solution)/shard_map/ppermute | solution.py:411
  13.4 2.2 %collective-permute-start.1 = (bf16[1024,128]{1,0:T(8,128)(2,1)}, bf16[1024,128]{1,0:T(8,128)(2,1)S(1)}, u32[]{:S(2)}, u32[]{:S(2)}) collective-permute-start(bf16[1024,128]{1,0:T(8,128)(2,1)} %get-tuple-element.35), channel_id=1, source_target_pairs={{4,16},{8,28},{12,24},{16,4},{20,0},{24,12},{5,17},{9,29},{13,25},... | collective-permute-start | bytes 786440 | tf_op jit(solution)/shard_map/ppermute | solution.py:411
  15.6 4.0 %collective-permute-start.2 = (bf16[1024,128]{1,0:T(8,128)(2,1)}, bf16[1024,128]{1,0:T(8,128)(2,1)S(1)}, u32[]{:S(2)}, u32[]{:S(2)}) collective-permute-start(bf16[1024,128]{1,0:T(8,128)(2,1)} %get-tuple-element.36), channel_id=1, source_target_pairs={{4,28},{8,16},{12,20},{16,8},{20,12},{24,0},{5,29},{9,17},{13,21},... | collective-permute-start | bytes 786440 | tf_op jit(solution)/shard_map/ppermute | solution.py:411
  19.6 2.0 %collective-permute-start.3 = (bf16[1024,128]{1,0:T(8,128)(2,1)}, bf16[1024,128]{1,0:T(8,128)(2,1)}, u32[]{:S(2)}, u32[]{:S(2)}) collective-permute-start(bf16[1024,128]{1,0:T(8,128)(2,1)} %get-tuple-element.37), channel_id=1, source_target_pairs={{4,24},{8,20},{12,16},{16,12},{20,8},{24,4},{5,25},{9,21},{13,17},... | collective-permute-start | bytes 786440 | tf_op jit(solution)/shard_map/ppermute | solution.py:411
  21.6 21.1 %all-to-all-done.x_ref = bf16[4,2064,128]{2,1,0:T(8,128)(2,1)S(1)} async-done(((bf16[4,2064,128]{2,1,0:T(8,128)(2,1)}), bf16[4,2064,128]{2,1,0:T(8,128)(2,1)S(1)}, u32[]{:S(2)}, u32[]{:S(2)}) %all-to-all-start) | async-done | bytes 2113568 | tf_op jit(solution)/shard_map/all_to_all | solution.py:367
  42.7 0.9 convert_reduce_fusion.near_ref
  43.6 0.0 collective-permute-done.refs_0_
  43.6 0.0 collective-permute-done.1.refs_1_
  43.6 0.0 copy-start.12
  43.6 0.0 collective-permute-done.3.refs_3_
  43.6 15.2 %collective-permute-start.4 = (bf16[512,512]{1,0:T(8,128)(2,1)S(1)}, bf16[512,512]{1,0:T(8,128)(2,1)}, u32[]{:S(2)}, u32[]{:S(2)}) collective-permute-start(bf16[512,512]{1,0:T(8,128)(2,1)S(1)} %bitcast.54), channel_id=1, source_target_pairs={{0,4},{4,0},{8,12},{12,8},{16,20},{20,16},{24,28},{28,24},{1,5},{5... | collective-permute-start | bytes 1572872 | tf_op jit(solution)/shard_map/ppermute | solution.py:423
  58.8 0.5 collective-permute-start.5
  59.3 0.7 collective-permute-start.6
  60.0 22.6 %attend.1 = (bf16[4,512,128]{2,1,0:T(8,128)(2,1)}, f32[8,2,512]{2,1,0:T(2,128)}, f32[8,64,512]{2,1,0:T(8,128)}, bf16[3,1024,128]{2,1,0:T(8,128)(2,1)}) custom-call(s32[4,3]{1,0:T(4,128)} %convert_reduce_fusion.near_ref, bf16[4,2064,128]{2,1,0:T(8,128)(2,1)} %copy-done, bf16[1024,128]{1,0:T(8,128)(2,1)} %copy-done.10, bf16[1024,128]{1,0:T(8,128)(2,1)} %copy-done.11, ...), custom_call_target="tpu_custom_call" | custom-call | flops 2415919 | bytes 4194 | tf_op jit(solution)/shard_map/attend/pallas_call | solution.py:432
  82.7 0.0 collective-permute-start.11
  82.7 0.0 collective-permute-done.5.refs_2_
  82.7 0.0 copy-start.5
  82.8 1.2 copy-done.5
  83.9 1.8 %term.1 = bf16[128,512]{1,0:T(8,128)(2,1)S(1)} custom-call(bf16[4,512,128]{2,1,0:T(8,128)(2,1)S(1)} %copy-done.5, bf16[512,512]{1,0:T(8,128)(2,1)S(1)} %bitcast.57, bf16[512,512]{1,0:T(8,128)(2,1)} %collective-permute-done.4.refs_1_, bf16[512,512]{1,0:T(8,128)(2,1)} %collective-permute-done.5.refs_2_, bf16[512,512]{1,0:T(8,128)(2,1)} %collective-permute-done.6.refs_3_), custom_call_target="tpu_custom_call" | custom-call | flops 268435 | bytes 4194 | tf_op jit(solution)/shard_map/term/pallas_call | solution.py:488
  85.8 0.6 dynamic-slice_bitcast_fusion.2
  86.4 1.3 collective-permute-start.9
  87.7 3.3 %collective-permute-start.8 = (bf16[32,512]{1,0:T(8,128)(2,1)}, bf16[32,512]{1,0:T(8,128)(2,1)}, u32[]{:S(2)}, u32[]{:S(2)}) collective-permute-start(bf16[32,512]{1,0:T(8,128)(2,1)} %get-tuple-element.63), channel_id=1, source_target_pairs={{0,2},{1,3},{2,0},{3,1},{4,6},{5,7},{6,4},{7,5},{8,10},{9,11},{10,... | collective-permute-start | bytes 98312 | tf_op jit(solution)/shard_map/ppermute | solution.py:335
  91.1 1.2 copy-done.3
  92.3 0.8 copy-done.8
  93.0 0.7 copy-done.9
  93.7 10.2 %own0.1.refs_0_ = bf16[4,768,128]{2,1,0:T(8,128)(2,1)S(1)} custom-call(s32[4,3]{1,0:T(4,128)S(1)} %copy-done.9, bf16[4,2064,128]{2,1,0:T(8,128)(2,1)S(1)} %copy-done.1, f32[8,2,512]{2,1,0:T(2,128)S(1)} %copy-done.8, f32[8,64,512]{2,1,0:T(8,128)S(1)} %copy-done.3), custom_call_target="tpu_custom_call" | custom-call | flops 3355443 | bytes 4194 | tf_op jit(solution)/shard_map/own0/pallas_call | solution.py:468
  103.9 0.0 copy-start.6
  104.0 0.9 fusion.1
  104.8 0.4 collective-permute-start.10
  105.3 10.0 %own1.1.refs_1_ = bf16[4,768,128]{2,1,0:T(8,128)(2,1)S(1)} custom-call(s32[4,3]{1,0:T(4,128)S(1)} %copy-done.9, bf16[4,2064,128]{2,1,0:T(8,128)(2,1)S(1)} %copy-done.1, f32[8,2,512]{2,1,0:T(2,128)S(1)} %copy-done.8, f32[8,64,512]{2,1,0:T(8,128)S(1)} %copy-done.3), custom_call_target="tpu_custom_call" | custom-call | flops 3355443 | bytes 4194 | tf_op jit(solution)/shard_map/own1/pallas_call | solution.py:468
  115.3 1.7 %collective-permute-done.10 = bf16[32,512]{1,0:T(8,128)(2,1)S(1)} collective-permute-done((bf16[32,512]{1,0:T(8,128)(2,1)S(1)}, bf16[32,512]{1,0:T(8,128)(2,1)S(1)}, u32[]{:S(2)}, u32[]{:S(2)}) %collective-permute-start.10) | collective-permute-done | bytes 32800 | tf_op jit(solution)/shard_map/ppermute | solution.py:374
  117.0 0.4 merge.1
  117.5 1.3 copy-done.2
  118.8 4.8 %collective-permute-start.12 = (bf16[32,512]{1,0:T(8,128)(2,1)S(1)}, bf16[32,512]{1,0:T(8,128)(2,1)S(1)}, u32[]{:S(2)}, u32[]{:S(2)}) collective-permute-start(bf16[32,512]{1,0:T(8,128)(2,1)S(1)} %multiply_convert_fusion), channel_id=1, source_target_pairs={{0,12},{4,0},{8,4},{12,8},{16,28},{20,16},{24,20},{28,24},{1,13},{... | collective-permute-start | bytes 98312 | tf_op jit(solution)/shard_map/ppermute | solution.py:345
  123.6 0.4 collective-permute-start.14
  124.0 4.7 %all-to-all-start.1 = ((bf16[4,2048,128]{2,1,0:T(8,128)(2,1)}), bf16[4,2048,128]{2,1,0:T(8,128)(2,1)S(1)}, u32[]{:S(2)}, u32[]{:S(2)}) async-start(bf16[4,2048,128]{2,1,0:T(8,128)(2,1)} %copy-done.2), calls=%async_computation.1 | async-start | bytes 4194304 | tf_op jit(solution)/shard_map/all_to_all | solution.py:367
  128.8 0.0 copy-start.4
  128.9 0.9 collective-permute-start.15
  129.8 2.1 %collective-permute-start.16 = (bf16[4,32,512]{2,1,0:T(8,128)(2,1)S(1)}, bf16[4,32,512]{2,1,0:T(8,128)(2,1)S(1)}, u32[]{:S(2)}, u32[]{:S(2)}) collective-permute-start(bf16[4,32,512]{2,1,0:T(8,128)(2,1)S(1)} %constant_dynamic-slice_fusion), channel_id=1, source_target_pairs={{0,2},{1,3},{2,0},{3,1},{4,6},{5,7},{6,4},{7,5},{8,10},{9,11},{10,... | collective-permute-start | bytes 393224 | tf_op jit(solution)/shard_map/ppermute | solution.py:345
  132.0 0.0 collective-permute-start.17
  132.0 4.2 %collective-permute-done.15 = bf16[4,32,512]{2,1,0:T(8,128)(2,1)S(1)} collective-permute-done((bf16[4,32,512]{2,1,0:T(8,128)(2,1)S(1)}, bf16[4,32,512]{2,1,0:T(8,128)(2,1)S(1)}, u32[]{:S(2)}, u32[]{:S(2)}) %collective-permute-start.15) | collective-permute-done | bytes 131104 | tf_op jit(solution)/shard_map/ppermute | solution.py:345
  136.2 0.5 collective-permute-done.17
  136.8 1.1 dynamic-slice_convert_fusion
  137.9 15.8 %all-to-all-done.1.y_ref = bf16[4,2048,128]{2,1,0:T(8,128)(2,1)S(1)} async-done(((bf16[4,2048,128]{2,1,0:T(8,128)(2,1)}), bf16[4,2048,128]{2,1,0:T(8,128)(2,1)S(1)}, u32[]{:S(2)}, u32[]{:S(2)}) %all-to-all-start.1) | async-done | bytes 2097184 | tf_op jit(solution)/shard_map/all_to_all | solution.py:367
  153.7 2.3 %unpack.1 = (bf16[512,512]{1,0:T(8,128)(2,1)}, bf16[512,512]{1,0:T(8,128)(2,1)}, bf16[512,512]{1,0:T(8,128)(2,1)}, bf16[512,512]{1,0:T(8,128)(2,1)}) custom-call(bf16[4,2048,128]{2,1,0:T(8,128)(2,1)S(1)} %all-to-all-done.1.y_ref, bf16[512,512]{1,0:T(8,128)(2,1)S(1)} %copy-done.4), custom_call_target="tpu_custom_call" | custom-call | flops 268435 | bytes 4194 | tf_op jit(solution)/shard_map/unpack/pallas_call | solution.py:515
  (48 shorter events, 0.2 us)
Async XLA Ops:
  5.3 38.3 %copy-start.7 = (bf16[1,512,512]{2,1,0:T(8,128)(2,1)S(1)}, bf16[1,512,512]{2,1,0:T(8,128)(2,1)}, u32[]{:S(2)}) copy-start(bf16[1,512,512]{2,1,0:T(8,128)(2,1)} %param.10) | copy-start | bytes 1572868
  5.3 37.4 %all-to-all-start = ((bf16[4,2064,128]{2,1,0:T(8,128)(2,1)}), bf16[4,2064,128]{2,1,0:T(8,128)(2,1)S(1)}, u32[]{:S(2)}, u32[]{:S(2)}) async-start(bf16[4,2064,128]{2,1,0:T(8,128)(2,1)} %get-tuple-element.33), calls=%async_computation | async-start | bytes 4227072 | tf_op jit(solution)/shard_map/all_to_all | solution.py:367
  9.2 34.3 %collective-permute-start = (bf16[1024,128]{1,0:T(8,128)(2,1)}, bf16[1024,128]{1,0:T(8,128)(2,1)S(1)}, u32[]{:S(2)}, u32[]{:S(2)}) collective-permute-start(bf16[1024,128]{1,0:T(8,128)(2,1)} %get-tuple-element.34), channel_id=1, source_target_pairs={{4,20},{8,24},{12,28},{16,0},{20,4},{24,8},{5,21},{9,25},{13,29},{... | collective-permute-start | bytes 786440 | tf_op jit(solution)/shard_map/ppermute | solution.py:411
  13.4 30.1 %collective-permute-start.1 = (bf16[1024,128]{1,0:T(8,128)(2,1)}, bf16[1024,128]{1,0:T(8,128)(2,1)S(1)}, u32[]{:S(2)}, u32[]{:S(2)}) collective-permute-start(bf16[1024,128]{1,0:T(8,128)(2,1)} %get-tuple-element.35), channel_id=1, source_target_pairs={{4,16},{8,28},{12,24},{16,4},{20,0},{24,12},{5,17},{9,29},{13,25},... | collective-permute-start | bytes 786440 | tf_op jit(solution)/shard_map/ppermute | solution.py:411
  15.6 27.9 %collective-permute-start.2 = (bf16[1024,128]{1,0:T(8,128)(2,1)}, bf16[1024,128]{1,0:T(8,128)(2,1)S(1)}, u32[]{:S(2)}, u32[]{:S(2)}) collective-permute-start(bf16[1024,128]{1,0:T(8,128)(2,1)} %get-tuple-element.36), channel_id=1, source_target_pairs={{4,28},{8,16},{12,20},{16,8},{20,12},{24,0},{5,29},{9,17},{13,21},... | collective-permute-start | bytes 786440 | tf_op jit(solution)/shard_map/ppermute | solution.py:411
  19.6 24.0 %collective-permute-start.3 = (bf16[1024,128]{1,0:T(8,128)(2,1)}, bf16[1024,128]{1,0:T(8,128)(2,1)}, u32[]{:S(2)}, u32[]{:S(2)}) collective-permute-start(bf16[1024,128]{1,0:T(8,128)(2,1)} %get-tuple-element.37), channel_id=1, source_target_pairs={{4,24},{8,20},{12,16},{16,12},{20,8},{24,4},{5,25},{9,21},{13,17},... | collective-permute-start | bytes 786440 | tf_op jit(solution)/shard_map/ppermute | solution.py:411
  42.7 17.3 %copy-start = (bf16[4,2064,128]{2,1,0:T(8,128)(2,1)}, bf16[4,2064,128]{2,1,0:T(8,128)(2,1)S(1)}, u32[]{:S(2)}) copy-start(bf16[4,2064,128]{2,1,0:T(8,128)(2,1)S(1)} %all-to-all-done.x_ref) | copy-start | bytes 6340612
  43.6 16.5 %copy-start.10 = (bf16[1024,128]{1,0:T(8,128)(2,1)}, bf16[1024,128]{1,0:T(8,128)(2,1)S(1)}, u32[]{:S(2)}) copy-start(bf16[1024,128]{1,0:T(8,128)(2,1)S(1)} %collective-permute-done.refs_0_) | copy-start | bytes 786436
  43.6 16.5 %copy-start.11 = (bf16[1024,128]{1,0:T(8,128)(2,1)}, bf16[1024,128]{1,0:T(8,128)(2,1)S(1)}, u32[]{:S(2)}) copy-start(bf16[1024,128]{1,0:T(8,128)(2,1)S(1)} %collective-permute-done.1.refs_1_) | copy-start | bytes 786436
  43.6 16.4 %copy-start.12 = (bf16[1024,128]{1,0:T(8,128)(2,1)}, bf16[1024,128]{1,0:T(8,128)(2,1)S(1)}, u32[]{:S(2)}) copy-start(bf16[1024,128]{1,0:T(8,128)(2,1)S(1)} %collective-permute-done.2.refs_2_) | copy-start | bytes 786436
  43.6 39.1 %collective-permute-start.4 = (bf16[512,512]{1,0:T(8,128)(2,1)S(1)}, bf16[512,512]{1,0:T(8,128)(2,1)}, u32[]{:S(2)}, u32[]{:S(2)}) collective-permute-start(bf16[512,512]{1,0:T(8,128)(2,1)S(1)} %bitcast.54), channel_id=1, source_target_pairs={{0,4},{4,0},{8,12},{12,8},{16,20},{20,16},{24,28},{28,24},{1,5},{5... | collective-permute-start | bytes 1572872 | tf_op jit(solution)/shard_map/ppermute | solution.py:423
  58.8 23.9 %collective-permute-start.5 = (bf16[512,512]{1,0:T(8,128)(2,1)S(1)}, bf16[512,512]{1,0:T(8,128)(2,1)}, u32[]{:S(2)}, u32[]{:S(2)}) collective-permute-start(bf16[512,512]{1,0:T(8,128)(2,1)S(1)} %bitcast.55), channel_id=1, source_target_pairs={{0,8},{4,12},{8,0},{12,4},{16,24},{20,28},{24,16},{28,20},{1,9},{5... | collective-permute-start | bytes 1572872 | tf_op jit(solution)/shard_map/ppermute | solution.py:423
  59.3 23.4 %collective-permute-start.6 = (bf16[512,512]{1,0:T(8,128)(2,1)S(1)}, bf16[512,512]{1,0:T(8,128)(2,1)}, u32[]{:S(2)}, u32[]{:S(2)}) collective-permute-start(bf16[512,512]{1,0:T(8,128)(2,1)S(1)} %bitcast.56), channel_id=1, source_target_pairs={{0,12},{4,8},{8,4},{12,0},{16,28},{20,24},{24,20},{28,16},{1,13},{... | collective-permute-start | bytes 1572872 | tf_op jit(solution)/shard_map/ppermute | solution.py:423
  82.7 8.4 %copy-start.1 = (bf16[4,2064,128]{2,1,0:T(8,128)(2,1)S(1)}, bf16[4,2064,128]{2,1,0:T(8,128)(2,1)}, u32[]{:S(2)}) copy-start(bf16[4,2064,128]{2,1,0:T(8,128)(2,1)} %copy-done) | copy-start | bytes 6340612
  82.7 34.3 %collective-permute-start.11 = (bf16[3,1024,128]{2,1,0:T(8,128)(2,1)}, bf16[3,1024,128]{2,1,0:T(8,128)(2,1)S(1)}, u32[]{:S(2)}, u32[]{:S(2)}) collective-permute-start(bf16[3,1024,128]{2,1,0:T(8,128)(2,1)} %get-tuple-element.49), channel_id=1, source_target_pairs={{0,16},{4,20},{8,24},{12,28},{16,0},{20,4},{24,8},{28,12},{1,17},{... | collective-permute-start | bytes 2359304 | tf_op jit(solution)/shard_map/ppermute | solution.py:374
  82.7 1.2 copy-start.5
  86.4 17.5 %collective-permute-start.9 = (bf16[32,512]{1,0:T(8,128)(2,1)}, bf16[32,512]{1,0:T(8,128)(2,1)}, u32[]{:S(2)}, u32[]{:S(2)}) collective-permute-start(bf16[32,512]{1,0:T(8,128)(2,1)} %get-tuple-element.62), channel_id=1, source_target_pairs={{0,3},{1,0},{2,1},{3,2},{4,7},{5,4},{6,5},{7,6},{8,11},{9,8},{10,9... | collective-permute-start | bytes 98312 | tf_op jit(solution)/shard_map/ppermute | solution.py:335
  87.7 16.2 %collective-permute-start.8 = (bf16[32,512]{1,0:T(8,128)(2,1)}, bf16[32,512]{1,0:T(8,128)(2,1)}, u32[]{:S(2)}, u32[]{:S(2)}) collective-permute-start(bf16[32,512]{1,0:T(8,128)(2,1)} %get-tuple-element.63), channel_id=1, source_target_pairs={{0,2},{1,3},{2,0},{3,1},{4,6},{5,7},{6,4},{7,5},{8,10},{9,11},{10,... | collective-permute-start | bytes 98312 | tf_op jit(solution)/shard_map/ppermute | solution.py:335
  91.1 12.9 %collective-permute-start.7 = (bf16[32,512]{1,0:T(8,128)(2,1)}, bf16[32,512]{1,0:T(8,128)(2,1)}, u32[]{:S(2)}, u32[]{:S(2)}) collective-permute-start(bf16[32,512]{1,0:T(8,128)(2,1)} %get-tuple-element.61), channel_id=1, source_target_pairs={{0,1},{1,2},{2,3},{3,0},{4,5},{5,6},{6,7},{7,4},{8,9},{9,10},{10,1... | collective-permute-start | bytes 98312 | tf_op jit(solution)/shard_map/ppermute | solution.py:335
  91.1 1.2 copy-start.3
  92.3 0.8 copy-start.8
  93.0 0.7 copy-start.9
  103.9 13.1 %copy-start.6 = (bf16[4,512,128]{2,1,0:T(8,128)(2,1)S(1)}, bf16[4,512,128]{2,1,0:T(8,128)(2,1)}, u32[]{:S(2)}) copy-start(bf16[4,512,128]{2,1,0:T(8,128)(2,1)} %get-tuple-element.44.attn_ref.refs_3_) | copy-start | bytes 1572868
  104.8 12.2 %collective-permute-start.10 = (bf16[32,512]{1,0:T(8,128)(2,1)S(1)}, bf16[32,512]{1,0:T(8,128)(2,1)S(1)}, u32[]{:S(2)}, u32[]{:S(2)}) collective-permute-start(bf16[32,512]{1,0:T(8,128)(2,1)S(1)} %fusion.1), channel_id=1, source_target_pairs={{0,16},{4,20},{8,24},{12,28},{16,0},{20,4},{24,8},{28,12},{1,17},{... | collective-permute-start | bytes 98312 | tf_op jit(solution)/shard_map/ppermute | solution.py:374
  117.5 1.3 copy-start.2
  118.8 9.9 %collective-permute-start.12 = (bf16[32,512]{1,0:T(8,128)(2,1)S(1)}, bf16[32,512]{1,0:T(8,128)(2,1)S(1)}, u32[]{:S(2)}, u32[]{:S(2)}) collective-permute-start(bf16[32,512]{1,0:T(8,128)(2,1)S(1)} %multiply_convert_fusion), channel_id=1, source_target_pairs={{0,12},{4,0},{8,4},{12,8},{16,28},{20,16},{24,20},{28,24},{1,13},{... | collective-permute-start | bytes 98312 | tf_op jit(solution)/shard_map/ppermute | solution.py:345
  123.6 5.1 %collective-permute-start.13 = (bf16[32,512]{1,0:T(8,128)(2,1)S(1)}, bf16[32,512]{1,0:T(8,128)(2,1)S(1)}, u32[]{:S(2)}, u32[]{:S(2)}) collective-permute-start(bf16[32,512]{1,0:T(8,128)(2,1)S(1)} %multiply_convert_fusion), channel_id=1, source_target_pairs={{0,8},{4,12},{8,0},{12,4},{16,24},{20,28},{24,16},{28,20},{1,9},{5... | collective-permute-start | bytes 98312 | tf_op jit(solution)/shard_map/ppermute | solution.py:345
  123.6 5.1 %collective-permute-start.14 = (bf16[32,512]{1,0:T(8,128)(2,1)S(1)}, bf16[32,512]{1,0:T(8,128)(2,1)S(1)}, u32[]{:S(2)}, u32[]{:S(2)}) collective-permute-start(bf16[32,512]{1,0:T(8,128)(2,1)S(1)} %multiply_convert_fusion), channel_id=1, source_target_pairs={{0,4},{4,8},{8,12},{12,0},{16,20},{20,24},{24,28},{28,16},{1,5},{5... | collective-permute-start | bytes 98312 | tf_op jit(solution)/shard_map/ppermute | solution.py:345
  124.0 29.7 %all-to-all-start.1 = ((bf16[4,2048,128]{2,1,0:T(8,128)(2,1)}), bf16[4,2048,128]{2,1,0:T(8,128)(2,1)S(1)}, u32[]{:S(2)}, u32[]{:S(2)}) async-start(bf16[4,2048,128]{2,1,0:T(8,128)(2,1)} %copy-done.2), calls=%async_computation.1 | async-start | bytes 4194304 | tf_op jit(solution)/shard_map/all_to_all | solution.py:367
  128.8 24.9 %copy-start.4 = (bf16[512,512]{1,0:T(8,128)(2,1)S(1)}, bf16[512,512]{1,0:T(8,128)(2,1)}, u32[]{:S(2)}) copy-start(bf16[512,512]{1,0:T(8,128)(2,1)} %w_ref.1) | copy-start | bytes 1572868
  128.9 7.3 %collective-permute-start.15 = (bf16[4,32,512]{2,1,0:T(8,128)(2,1)S(1)}, bf16[4,32,512]{2,1,0:T(8,128)(2,1)S(1)}, u32[]{:S(2)}, u32[]{:S(2)}) collective-permute-start(bf16[4,32,512]{2,1,0:T(8,128)(2,1)S(1)} %constant_dynamic-slice_fusion), channel_id=1, source_target_pairs={{0,3},{1,0},{2,1},{3,2},{4,7},{5,4},{6,5},{7,6},{8,11},{9,8},{10,9... | collective-permute-start | bytes 393224 | tf_op jit(solution)/shard_map/ppermute | solution.py:345
  129.8 6.4 %collective-permute-start.16 = (bf16[4,32,512]{2,1,0:T(8,128)(2,1)S(1)}, bf16[4,32,512]{2,1,0:T(8,128)(2,1)S(1)}, u32[]{:S(2)}, u32[]{:S(2)}) collective-permute-start(bf16[4,32,512]{2,1,0:T(8,128)(2,1)S(1)} %constant_dynamic-slice_fusion), channel_id=1, source_target_pairs={{0,2},{1,3},{2,0},{3,1},{4,6},{5,7},{6,4},{7,5},{8,10},{9,11},{10,... | collective-permute-start | bytes 393224 | tf_op jit(solution)/shard_map/ppermute | solution.py:345
  132.0 4.7 %collective-permute-start.17 = (bf16[4,32,512]{2,1,0:T(8,128)(2,1)S(1)}, bf16[4,32,512]{2,1,0:T(8,128)(2,1)S(1)}, u32[]{:S(2)}, u32[]{:S(2)}) collective-permute-start(bf16[4,32,512]{2,1,0:T(8,128)(2,1)S(1)} %constant_dynamic-slice_fusion), channel_id=1, source_target_pairs={{0,1},{1,2},{2,3},{3,0},{4,5},{5,6},{6,7},{7,4},{8,9},{9,10},{10,1... | collective-permute-start | bytes 393224 | tf_op jit(solution)/shard_map/ppermute | solution.py:345

commit v8 on v7

--- a/solution.py
+++ b/solution.py
@@ -408,9 +408,9 @@
     if alone:
         border = [g * GROUP + i for g in range(2) for i in range(1 - g, 1 - g + REACH)]
         beyond = [
-            lax.ppermute(array, "seg", [(s, (s + GROUP) % seg ^ by) for s in border])
-            for by, array in enumerate(direct)
-        ]
+            lax.ppermute(direct[by], "seg", [(s, (s + GROUP) % seg ^ by) for s in border])
+            for by in reversed(range(GROUP))
+        ][::-1]
     else:
         kv = x[:, : MINE * rows]
         beyond = [

time: 156 us -> 157 us (level)
  the two profiles are of different devices: /device:TPU:13 before, /device:TPU:0 now
where the time goes in v8:
time: 157 us; the launch traced here: 156 us
  waiting for transfers between devices  60.3 us (38%)
  Pallas kernels  45.5 us (29%)
  starting transfers between devices  40.1 us (26%)
  local copies, waits for them, and re-layouts  5.84 us (4%)
  other arithmetic  2.86 us (2%)
    all_to_all x2, waiting for transfers between devices, swap(): return lax.all_to_all(array, 'seg', 0, 0, axis_index_groups=split)  44.6 us
    pallas_call x2, Pallas kernels, own_terms(): call(functools.partial(own_kernel, i), f'own{i}', [((GROUP, rows + half,...  18.6 us
    pallas_call x1, Pallas kernels, body(): call(functools.partial(attend_kernel, alone), 'attend', [((GROUP, MINE *...  17.6 us
    ppermute x2, starting transfers between devices, across(): lax.ppermute(array, 'seg', [(s, (s + GROUP) % seg) for s in range(seg)])  13.5 us
    all_to_all x2, starting transfers between devices, swap(): return lax.all_to_all(array, 'seg', 0, 0, axis_index_groups=split)  9.55 us
    ppermute x4, waiting for transfers between devices, body(): lax.ppermute(direct[by], 'seg', [(s, (s + GROUP) % seg ^ by) for s in bor...  8.23 us
    ppermute x6, waiting for transfers between devices, gathered(): arrived.append(lax.ppermute(piece, axis, pairs))  7.48 us
    ppermute x3, starting transfers between devices, body(): lax.ppermute(grad_in, 'seg', [(s, s ^ by) for s in range(seg)])  7.34 us
  transfers between devices with their start and end apart: 20, of which 7 were waited for; matrix products, arithmetic and copies ran while one was open for 2% of the time, Pallas kernels for 24%

profile of v8, /device:TPU:0, one launch (start us, length us, event | category | flops | bytes accessed | tf_op | source)
XLA Modules:
  0.0 155.6 jit_solution(14881455769039767166)
XLA Ops:
  0.6 4.7 %pack.1 = (bf16[4,2064,128]{2,1,0:T(8,128)(2,1)}, bf16[1024,128]{1,0:T(8,128)(2,1)}, bf16[1024,128]{1,0:T(8,128)(2,1)}, bf16[1024,128]{1,0:T(8,128)(2,1)}, bf16[1024,128]{1,0:T(8,128)(2,1)}) custom-call(s32[1,3]{1,0:T(1,128)} %bitcast.64, bf16[512,512]{1,0:T(8,128)(2,1)} %bitcast.61, bf16[512,512]{1,0:T(8,128)(2,1)} %bitcast.62, bf16[512,512]{1,0:T(8,128)(2,1)} %bitcast.63, ...), custom_call_target="tpu_custom_call" | custom-call | flops 268435 | bytes 2621 | tf_op jit(solution)/shard_map/pack/pallas_call | solution.py:391
  5.3 0.0 copy-start.7
  5.3 5.4 %all-to-all-start = ((bf16[4,2064,128]{2,1,0:T(8,128)(2,1)}), bf16[4,2064,128]{2,1,0:T(8,128)(2,1)S(1)}, u32[]{:S(2)}, u32[]{:S(2)}) async-start(bf16[4,2064,128]{2,1,0:T(8,128)(2,1)} %get-tuple-element.33), calls=%async_computation | async-start | bytes 4227072 | tf_op jit(solution)/shard_map/all_to_all | solution.py:367
  10.7 1.3 collective-permute-start
  12.0 1.3 collective-permute-start.1
  13.3 1.3 collective-permute-start.2
  14.6 1.4 collective-permute-start.3
  16.0 31.1 %all-to-all-done.x_ref = bf16[4,2064,128]{2,1,0:T(8,128)(2,1)S(1)} async-done(((bf16[4,2064,128]{2,1,0:T(8,128)(2,1)}), bf16[4,2064,128]{2,1,0:T(8,128)(2,1)S(1)}, u32[]{:S(2)}, u32[]{:S(2)}) %all-to-all-start) | async-done | bytes 2113568 | tf_op jit(solution)/shard_map/all_to_all | solution.py:367
  47.0 0.9 convert_reduce_fusion.near_ref
  47.9 0.0 collective-permute-done.refs_0_
  47.9 0.0 collective-permute-done.1.refs_1_
  47.9 8.2 %collective-permute-done.2.refs_2_ = bf16[1024,128]{1,0:T(8,128)(2,1)S(1)} collective-permute-done((bf16[1024,128]{1,0:T(8,128)(2,1)}, bf16[1024,128]{1,0:T(8,128)(2,1)S(1)}, u32[]{:S(2)}, u32[]{:S(2)}) %collective-permute-start.2) | collective-permute-done | bytes 262176 | tf_op jit(solution)/shard_map/ppermute | solution.py:411
  56.1 0.0 collective-permute-done.3.refs_3_
  56.1 5.9 %collective-permute-start.4 = (bf16[512,512]{1,0:T(8,128)(2,1)S(1)}, bf16[512,512]{1,0:T(8,128)(2,1)}, u32[]{:S(2)}, u32[]{:S(2)}) collective-permute-start(bf16[512,512]{1,0:T(8,128)(2,1)S(1)} %bitcast.54), channel_id=1, source_target_pairs={{0,4},{4,0},{8,12},{12,8},{16,20},{20,16},{24,28},{28,24},{1,5},{5... | collective-permute-start | bytes 1572872 | tf_op jit(solution)/shard_map/ppermute | solution.py:423
  62.0 1.5 collective-permute-start.5
  63.5 17.6 %attend.1 = (bf16[4,512,128]{2,1,0:T(8,128)(2,1)}, f32[8,2,512]{2,1,0:T(2,128)}, f32[8,64,512]{2,1,0:T(8,128)}, bf16[3,1024,128]{2,1,0:T(8,128)(2,1)}) custom-call(s32[4,3]{1,0:T(4,128)} %convert_reduce_fusion.near_ref, bf16[4,2064,128]{2,1,0:T(8,128)(2,1)} %copy-done, bf16[1024,128]{1,0:T(8,128)(2,1)} %copy-done.10, bf16[1024,128]{1,0:T(8,128)(2,1)} %copy-done.11, ...), custom_call_target="tpu_custom_call" | custom-call | flops 2415919 | bytes 4194 | tf_op jit(solution)/shard_map/attend/pallas_call | solution.py:432
  81.2 6.2 %collective-permute-start.11 = (bf16[3,1024,128]{2,1,0:T(8,128)(2,1)}, bf16[3,1024,128]{2,1,0:T(8,128)(2,1)S(1)}, u32[]{:S(2)}, u32[]{:S(2)}) collective-permute-start(bf16[3,1024,128]{2,1,0:T(8,128)(2,1)} %get-tuple-element.49), channel_id=1, source_target_pairs={{0,16},{4,20},{8,24},{12,28},{16,0},{20,4},{24,8},{28,12},{1,17},{... | collective-permute-start | bytes 2359304 | tf_op jit(solution)/shard_map/ppermute | solution.py:374
  87.4 0.0 collective-permute-done.4.refs_1_
  87.4 0.0 copy-start.5
  87.4 1.0 copy-done.5
  88.4 1.8 %term.1 = bf16[128,512]{1,0:T(8,128)(2,1)S(1)} custom-call(bf16[4,512,128]{2,1,0:T(8,128)(2,1)S(1)} %copy-done.5, bf16[512,512]{1,0:T(8,128)(2,1)S(1)} %bitcast.57, bf16[512,512]{1,0:T(8,128)(2,1)} %collective-permute-done.4.refs_1_, bf16[512,512]{1,0:T(8,128)(2,1)} %collective-permute-done.5.refs_2_, bf16[512,512]{1,0:T(8,128)(2,1)} %collective-permute-done.6.refs_3_), custom_call_target="tpu_custom_call" | custom-call | flops 268435 | bytes 4194 | tf_op jit(solution)/shard_map/term/pallas_call | solution.py:488
  90.3 0.6 dynamic-slice_bitcast_fusion.2
  90.9 0.9 collective-permute-start.8
  91.8 0.2 collective-permute-start.7
  92.1 1.2 copy-done.3
  93.3 0.8 copy-done.8
  94.1 0.7 copy-done.9
  94.7 9.4 %own0.1.refs_0_ = bf16[4,768,128]{2,1,0:T(8,128)(2,1)S(1)} custom-call(s32[4,3]{1,0:T(4,128)S(1)} %copy-done.9, bf16[4,2064,128]{2,1,0:T(8,128)(2,1)S(1)} %copy-done.1, f32[8,2,512]{2,1,0:T(2,128)S(1)} %copy-done.8, f32[8,64,512]{2,1,0:T(8,128)S(1)} %copy-done.3), custom_call_target="tpu_custom_call" | custom-call | flops 3355443 | bytes 4194 | tf_op jit(solution)/shard_map/own0/pallas_call | solution.py:468
  104.1 0.0 copy-start.6
  104.2 0.9 fusion.1
  105.0 7.3 %collective-permute-start.10 = (bf16[32,512]{1,0:T(8,128)(2,1)S(1)}, bf16[32,512]{1,0:T(8,128)(2,1)S(1)}, u32[]{:S(2)}, u32[]{:S(2)}) collective-permute-start(bf16[32,512]{1,0:T(8,128)(2,1)S(1)} %fusion.1), channel_id=1, source_target_pairs={{0,16},{4,20},{8,24},{12,28},{16,0},{20,4},{24,8},{28,12},{1,17},{... | collective-permute-start | bytes 98312 | tf_op jit(solution)/shard_map/ppermute | solution.py:374
  112.3 9.2 %own1.1.refs_1_ = bf16[4,768,128]{2,1,0:T(8,128)(2,1)S(1)} custom-call(s32[4,3]{1,0:T(4,128)S(1)} %copy-done.9, bf16[4,2064,128]{2,1,0:T(8,128)(2,1)S(1)} %copy-done.1, f32[8,2,512]{2,1,0:T(2,128)S(1)} %copy-done.8, f32[8,64,512]{2,1,0:T(8,128)S(1)} %copy-done.3), custom_call_target="tpu_custom_call" | custom-call | flops 3355443 | bytes 4194 | tf_op jit(solution)/shard_map/own1/pallas_call | solution.py:468
  121.6 0.4 merge.1
  122.0 1.3 copy-done.2
  123.4 0.1 collective-permute-start.12
  123.4 2.6 %collective-permute-start.13 = (bf16[32,512]{1,0:T(8,128)(2,1)S(1)}, bf16[32,512]{1,0:T(8,128)(2,1)S(1)}, u32[]{:S(2)}, u32[]{:S(2)}) collective-permute-start(bf16[32,512]{1,0:T(8,128)(2,1)S(1)} %multiply_convert_fusion), channel_id=1, source_target_pairs={{0,8},{4,12},{8,0},{12,4},{16,24},{20,28},{24,16},{28,20},{1,9},{5... | collective-permute-start | bytes 98312 | tf_op jit(solution)/shard_map/ppermute | solution.py:345
  126.0 4.2 %all-to-all-start.1 = ((bf16[4,2048,128]{2,1,0:T(8,128)(2,1)}), bf16[4,2048,128]{2,1,0:T(8,128)(2,1)S(1)}, u32[]{:S(2)}, u32[]{:S(2)}) async-start(bf16[4,2048,128]{2,1,0:T(8,128)(2,1)} %copy-done.2), calls=%async_computation.1 | async-start | bytes 4194304 | tf_op jit(solution)/shard_map/all_to_all | solution.py:367
  130.3 0.6 collective-permute-done.14
  130.9 0.0 copy-start.4
  130.9 0.1 collective-permute-start.15
  131.0 0.5 collective-permute-start.16
  131.5 0.2 collective-permute-start.17
  131.7 3.2 %collective-permute-done.15 = bf16[4,32,512]{2,1,0:T(8,128)(2,1)S(1)} collective-permute-done((bf16[4,32,512]{2,1,0:T(8,128)(2,1)S(1)}, bf16[4,32,512]{2,1,0:T(8,128)(2,1)S(1)}, u32[]{:S(2)}, u32[]{:S(2)}) %collective-permute-start.15) | collective-permute-done | bytes 131104 | tf_op jit(solution)/shard_map/ppermute | solution.py:345
  134.9 2.8 %collective-permute-done.16 = bf16[4,32,512]{2,1,0:T(8,128)(2,1)S(1)} collective-permute-done((bf16[4,32,512]{2,1,0:T(8,128)(2,1)S(1)}, bf16[4,32,512]{2,1,0:T(8,128)(2,1)S(1)}, u32[]{:S(2)}, u32[]{:S(2)}) %collective-permute-start.16) | collective-permute-done | bytes 131104 | tf_op jit(solution)/shard_map/ppermute | solution.py:345
  137.7 0.9 collective-permute-done.17
  138.7 1.1 dynamic-slice_convert_fusion
  139.8 13.5 %all-to-all-done.1.y_ref = bf16[4,2048,128]{2,1,0:T(8,128)(2,1)S(1)} async-done(((bf16[4,2048,128]{2,1,0:T(8,128)(2,1)}), bf16[4,2048,128]{2,1,0:T(8,128)(2,1)S(1)}, u32[]{:S(2)}, u32[]{:S(2)}) %all-to-all-start.1) | async-done | bytes 2097184 | tf_op jit(solution)/shard_map/all_to_all | solution.py:367
  153.3 2.3 %unpack.1 = (bf16[512,512]{1,0:T(8,128)(2,1)}, bf16[512,512]{1,0:T(8,128)(2,1)}, bf16[512,512]{1,0:T(8,128)(2,1)}, bf16[512,512]{1,0:T(8,128)(2,1)}) custom-call(bf16[4,2048,128]{2,1,0:T(8,128)(2,1)S(1)} %all-to-all-done.1.y_ref, bf16[512,512]{1,0:T(8,128)(2,1)S(1)} %copy-done.4), custom_call_target="tpu_custom_call" | custom-call | flops 268435 | bytes 4194 | tf_op jit(solution)/shard_map/unpack/pallas_call | solution.py:515
  (48 shorter events, 0.2 us)
Async XLA Ops:
  5.3 50.8 %copy-start.7 = (bf16[1,512,512]{2,1,0:T(8,128)(2,1)S(1)}, bf16[1,512,512]{2,1,0:T(8,128)(2,1)}, u32[]{:S(2)}) copy-start(bf16[1,512,512]{2,1,0:T(8,128)(2,1)} %param.10) | copy-start | bytes 1572868
  5.3 41.7 %all-to-all-start = ((bf16[4,2064,128]{2,1,0:T(8,128)(2,1)}), bf16[4,2064,128]{2,1,0:T(8,128)(2,1)S(1)}, u32[]{:S(2)}, u32[]{:S(2)}) async-start(bf16[4,2064,128]{2,1,0:T(8,128)(2,1)} %get-tuple-element.33), calls=%async_computation | async-start | bytes 4227072 | tf_op jit(solution)/shard_map/all_to_all | solution.py:367
  10.7 37.2 %collective-permute-start = (bf16[1024,128]{1,0:T(8,128)(2,1)}, bf16[1024,128]{1,0:T(8,128)(2,1)S(1)}, u32[]{:S(2)}, u32[]{:S(2)}) collective-permute-start(bf16[1024,128]{1,0:T(8,128)(2,1)} %get-tuple-element.34), channel_id=1, source_target_pairs={{4,20},{8,24},{12,28},{16,0},{20,4},{24,8},{5,21},{9,25},{13,29},{... | collective-permute-start | bytes 786440 | tf_op jit(solution)/shard_map/ppermute | solution.py:411
  12.0 35.9 %collective-permute-start.1 = (bf16[1024,128]{1,0:T(8,128)(2,1)}, bf16[1024,128]{1,0:T(8,128)(2,1)S(1)}, u32[]{:S(2)}, u32[]{:S(2)}) collective-permute-start(bf16[1024,128]{1,0:T(8,128)(2,1)} %get-tuple-element.35), channel_id=1, source_target_pairs={{4,16},{8,28},{12,24},{16,4},{20,0},{24,12},{5,17},{9,29},{13,25},... | collective-permute-start | bytes 786440 | tf_op jit(solution)/shard_map/ppermute | solution.py:411
  13.3 42.8 %collective-permute-start.2 = (bf16[1024,128]{1,0:T(8,128)(2,1)}, bf16[1024,128]{1,0:T(8,128)(2,1)S(1)}, u32[]{:S(2)}, u32[]{:S(2)}) collective-permute-start(bf16[1024,128]{1,0:T(8,128)(2,1)} %get-tuple-element.36), channel_id=1, source_target_pairs={{4,28},{8,16},{12,20},{16,8},{20,12},{24,0},{5,29},{9,17},{13,21},... | collective-permute-start | bytes 786440 | tf_op jit(solution)/shard_map/ppermute | solution.py:411
  14.6 41.6 %collective-permute-start.3 = (bf16[1024,128]{1,0:T(8,128)(2,1)}, bf16[1024,128]{1,0:T(8,128)(2,1)}, u32[]{:S(2)}, u32[]{:S(2)}) collective-permute-start(bf16[1024,128]{1,0:T(8,128)(2,1)} %get-tuple-element.37), channel_id=1, source_target_pairs={{4,24},{8,20},{12,16},{16,12},{20,8},{24,4},{5,25},{9,21},{13,17},... | collective-permute-start | bytes 786440 | tf_op jit(solution)/shard_map/ppermute | solution.py:411
  47.0 16.5 %copy-start = (bf16[4,2064,128]{2,1,0:T(8,128)(2,1)}, bf16[4,2064,128]{2,1,0:T(8,128)(2,1)S(1)}, u32[]{:S(2)}) copy-start(bf16[4,2064,128]{2,1,0:T(8,128)(2,1)S(1)} %all-to-all-done.x_ref) | copy-start | bytes 6340612
  47.9 15.6 %copy-start.10 = (bf16[1024,128]{1,0:T(8,128)(2,1)}, bf16[1024,128]{1,0:T(8,128)(2,1)S(1)}, u32[]{:S(2)}) copy-start(bf16[1024,128]{1,0:T(8,128)(2,1)S(1)} %collective-permute-done.refs_0_) | copy-start | bytes 786436
  47.9 15.6 %copy-start.11 = (bf16[1024,128]{1,0:T(8,128)(2,1)}, bf16[1024,128]{1,0:T(8,128)(2,1)S(1)}, u32[]{:S(2)}) copy-start(bf16[1024,128]{1,0:T(8,128)(2,1)S(1)} %collective-permute-done.1.refs_1_) | copy-start | bytes 786436
  56.1 7.4 %copy-start.12 = (bf16[1024,128]{1,0:T(8,128)(2,1)}, bf16[1024,128]{1,0:T(8,128)(2,1)S(1)}, u32[]{:S(2)}) copy-start(bf16[1024,128]{1,0:T(8,128)(2,1)S(1)} %collective-permute-done.2.refs_2_) | copy-start | bytes 786436
  56.1 31.2 %collective-permute-start.4 = (bf16[512,512]{1,0:T(8,128)(2,1)S(1)}, bf16[512,512]{1,0:T(8,128)(2,1)}, u32[]{:S(2)}, u32[]{:S(2)}) collective-permute-start(bf16[512,512]{1,0:T(8,128)(2,1)S(1)} %bitcast.54), channel_id=1, source_target_pairs={{0,4},{4,0},{8,12},{12,8},{16,20},{20,16},{24,28},{28,24},{1,5},{5... | collective-permute-start | bytes 1572872 | tf_op jit(solution)/shard_map/ppermute | solution.py:423
  62.0 25.4 %collective-permute-start.5 = (bf16[512,512]{1,0:T(8,128)(2,1)S(1)}, bf16[512,512]{1,0:T(8,128)(2,1)}, u32[]{:S(2)}, u32[]{:S(2)}) collective-permute-start(bf16[512,512]{1,0:T(8,128)(2,1)S(1)} %bitcast.55), channel_id=1, source_target_pairs={{0,8},{4,12},{8,0},{12,4},{16,24},{20,28},{24,16},{28,20},{1,9},{5... | collective-permute-start | bytes 1572872 | tf_op jit(solution)/shard_map/ppermute | solution.py:423
  63.5 23.9 %collective-permute-start.6 = (bf16[512,512]{1,0:T(8,128)(2,1)S(1)}, bf16[512,512]{1,0:T(8,128)(2,1)}, u32[]{:S(2)}, u32[]{:S(2)}) collective-permute-start(bf16[512,512]{1,0:T(8,128)(2,1)S(1)} %bitcast.56), channel_id=1, source_target_pairs={{0,12},{4,8},{8,4},{12,0},{16,28},{20,24},{24,20},{28,16},{1,13},{... | collective-permute-start | bytes 1572872 | tf_op jit(solution)/shard_map/ppermute | solution.py:423
  81.1 10.9 %copy-start.1 = (bf16[4,2064,128]{2,1,0:T(8,128)(2,1)S(1)}, bf16[4,2064,128]{2,1,0:T(8,128)(2,1)}, u32[]{:S(2)}) copy-start(bf16[4,2064,128]{2,1,0:T(8,128)(2,1)} %copy-done) | copy-start | bytes 6340612
  81.2 40.4 %collective-permute-start.11 = (bf16[3,1024,128]{2,1,0:T(8,128)(2,1)}, bf16[3,1024,128]{2,1,0:T(8,128)(2,1)S(1)}, u32[]{:S(2)}, u32[]{:S(2)}) collective-permute-start(bf16[3,1024,128]{2,1,0:T(8,128)(2,1)} %get-tuple-element.49), channel_id=1, source_target_pairs={{0,16},{4,20},{8,24},{12,28},{16,0},{20,4},{24,8},{28,12},{1,17},{... | collective-permute-start | bytes 2359304 | tf_op jit(solution)/shard_map/ppermute | solution.py:374
  87.4 1.0 copy-start.5
  90.9 13.2 %collective-permute-start.9 = (bf16[32,512]{1,0:T(8,128)(2,1)}, bf16[32,512]{1,0:T(8,128)(2,1)}, u32[]{:S(2)}, u32[]{:S(2)}) collective-permute-start(bf16[32,512]{1,0:T(8,128)(2,1)} %get-tuple-element.62), channel_id=1, source_target_pairs={{0,3},{1,0},{2,1},{3,2},{4,7},{5,4},{6,5},{7,6},{8,11},{9,8},{10,9... | collective-permute-start | bytes 98312 | tf_op jit(solution)/shard_map/ppermute | solution.py:335
  90.9 13.3 %collective-permute-start.8 = (bf16[32,512]{1,0:T(8,128)(2,1)}, bf16[32,512]{1,0:T(8,128)(2,1)}, u32[]{:S(2)}, u32[]{:S(2)}) collective-permute-start(bf16[32,512]{1,0:T(8,128)(2,1)} %get-tuple-element.63), channel_id=1, source_target_pairs={{0,2},{1,3},{2,0},{3,1},{4,6},{5,7},{6,4},{7,5},{8,10},{9,11},{10,... | collective-permute-start | bytes 98312 | tf_op jit(solution)/shard_map/ppermute | solution.py:335
  91.8 12.3 %collective-permute-start.7 = (bf16[32,512]{1,0:T(8,128)(2,1)}, bf16[32,512]{1,0:T(8,128)(2,1)}, u32[]{:S(2)}, u32[]{:S(2)}) collective-permute-start(bf16[32,512]{1,0:T(8,128)(2,1)} %get-tuple-element.61), channel_id=1, source_target_pairs={{0,1},{1,2},{2,3},{3,0},{4,5},{5,6},{6,7},{7,4},{8,9},{9,10},{10,1... | collective-permute-start | bytes 98312 | tf_op jit(solution)/shard_map/ppermute | solution.py:335
  92.1 1.2 copy-start.3
  93.3 0.8 copy-start.8
  94.1 0.7 copy-start.9
  104.1 17.4 %copy-start.6 = (bf16[4,512,128]{2,1,0:T(8,128)(2,1)S(1)}, bf16[4,512,128]{2,1,0:T(8,128)(2,1)}, u32[]{:S(2)}) copy-start(bf16[4,512,128]{2,1,0:T(8,128)(2,1)} %get-tuple-element.44.attn_ref.refs_3_) | copy-start | bytes 1572868
  105.0 16.5 %collective-permute-start.10 = (bf16[32,512]{1,0:T(8,128)(2,1)S(1)}, bf16[32,512]{1,0:T(8,128)(2,1)S(1)}, u32[]{:S(2)}, u32[]{:S(2)}) collective-permute-start(bf16[32,512]{1,0:T(8,128)(2,1)S(1)} %fusion.1), channel_id=1, source_target_pairs={{0,16},{4,20},{8,24},{12,28},{16,0},{20,4},{24,8},{28,12},{1,17},{... | collective-permute-start | bytes 98312 | tf_op jit(solution)/shard_map/ppermute | solution.py:374
  122.0 1.3 copy-start.2
  123.4 6.9 %collective-permute-start.12 = (bf16[32,512]{1,0:T(8,128)(2,1)S(1)}, bf16[32,512]{1,0:T(8,128)(2,1)S(1)}, u32[]{:S(2)}, u32[]{:S(2)}) collective-permute-start(bf16[32,512]{1,0:T(8,128)(2,1)S(1)} %multiply_convert_fusion), channel_id=1, source_target_pairs={{0,12},{4,0},{8,4},{12,8},{16,28},{20,16},{24,20},{28,24},{1,13},{... | collective-permute-start | bytes 98312 | tf_op jit(solution)/shard_map/ppermute | solution.py:345
  123.4 6.8 %collective-permute-start.13 = (bf16[32,512]{1,0:T(8,128)(2,1)S(1)}, bf16[32,512]{1,0:T(8,128)(2,1)S(1)}, u32[]{:S(2)}, u32[]{:S(2)}) collective-permute-start(bf16[32,512]{1,0:T(8,128)(2,1)S(1)} %multiply_convert_fusion), channel_id=1, source_target_pairs={{0,8},{4,12},{8,0},{12,4},{16,24},{20,28},{24,16},{28,20},{1,9},{5... | collective-permute-start | bytes 98312 | tf_op jit(solution)/shard_map/ppermute | solution.py:345
  126.0 4.8 %collective-permute-start.14 = (bf16[32,512]{1,0:T(8,128)(2,1)S(1)}, bf16[32,512]{1,0:T(8,128)(2,1)S(1)}, u32[]{:S(2)}, u32[]{:S(2)}) collective-permute-start(bf16[32,512]{1,0:T(8,128)(2,1)S(1)} %multiply_convert_fusion), channel_id=1, source_target_pairs={{0,4},{4,8},{8,12},{12,0},{16,20},{20,24},{24,28},{28,16},{1,5},{5... | collective-permute-start | bytes 98312 | tf_op jit(solution)/shard_map/ppermute | solution.py:345
  126.0 27.3 %all-to-all-start.1 = ((bf16[4,2048,128]{2,1,0:T(8,128)(2,1)}), bf16[4,2048,128]{2,1,0:T(8,128)(2,1)S(1)}, u32[]{:S(2)}, u32[]{:S(2)}) async-start(bf16[4,2048,128]{2,1,0:T(8,128)(2,1)} %copy-done.2), calls=%async_computation.1 | async-start | bytes 4194304 | tf_op jit(solution)/shard_map/all_to_all | solution.py:367
  130.9 22.5 %copy-start.4 = (bf16[512,512]{1,0:T(8,128)(2,1)S(1)}, bf16[512,512]{1,0:T(8,128)(2,1)}, u32[]{:S(2)}) copy-start(bf16[512,512]{1,0:T(8,128)(2,1)} %w_ref.1) | copy-start | bytes 1572868
  130.9 3.9 %collective-permute-start.15 = (bf16[4,32,512]{2,1,0:T(8,128)(2,1)S(1)}, bf16[4,32,512]{2,1,0:T(8,128)(2,1)S(1)}, u32[]{:S(2)}, u32[]{:S(2)}) collective-permute-start(bf16[4,32,512]{2,1,0:T(8,128)(2,1)S(1)} %constant_dynamic-slice_fusion), channel_id=1, source_target_pairs={{0,3},{1,0},{2,1},{3,2},{4,7},{5,4},{6,5},{7,6},{8,11},{9,8},{10,9... | collective-permute-start | bytes 393224 | tf_op jit(solution)/shard_map/ppermute | solution.py:345
  131.0 6.7 %collective-permute-start.16 = (bf16[4,32,512]{2,1,0:T(8,128)(2,1)S(1)}, bf16[4,32,512]{2,1,0:T(8,128)(2,1)S(1)}, u32[]{:S(2)}, u32[]{:S(2)}) collective-permute-start(bf16[4,32,512]{2,1,0:T(8,128)(2,1)S(1)} %constant_dynamic-slice_fusion), channel_id=1, source_target_pairs={{0,2},{1,3},{2,0},{3,1},{4,6},{5,7},{6,4},{7,5},{8,10},{9,11},{10,... | collective-permute-start | bytes 393224 | tf_op jit(solution)/shard_map/ppermute | solution.py:345
  131.5 7.1 %collective-permute-start.17 = (bf16[4,32,512]{2,1,0:T(8,128)(2,1)S(1)}, bf16[4,32,512]{2,1,0:T(8,128)(2,1)S(1)}, u32[]{:S(2)}, u32[]{:S(2)}) collective-permute-start(bf16[4,32,512]{2,1,0:T(8,128)(2,1)S(1)} %constant_dynamic-slice_fusion), channel_id=1, source_target_pairs={{0,1},{1,2},{2,3},{3,0},{4,5},{5,6},{6,7},{7,4},{8,9},{9,10},{10,1... | collective-permute-start | bytes 393224 | tf_op jit(solution)/shard_map/ppermute | solution.py:345
